TPU v7x, 32 devices: a whole 2x2x4 slice. The times are simulated.
32 devices in a mesh: batch: 1, blk: 4 (over x, core), box: 8 (over z, y).
Axes of the slice: x: 2, y: 2, z: 4, core: 2. Of those that a mesh axis runs over, the one named last changes fastest.
Arguments:
- surface_points: float32 [3, 4096], P(None, ('blk', 'box')), may hold values from -4 to 4
- angle_ids: int32 [128], P('batch'), may hold values from 0 to 16383
- near_mask: int32 [32, 8], P(('blk', 'box')), may hold values 0 or 1
- skeleton: int32 [32, 32], P(('blk', 'box')), may hold values from 0 to 127, as said below
- box_inverse_parts: float32 [32, 2, 128, 128], P(('blk', 'box')), may hold values from -0.375 to 0.375
- near_coupling: float32 [32, 8, 2, 32, 128], P(('blk', 'box')), may hold values from -0.25 to 0.25
- top_inverse: float32 [4, 2, 256, 256], P('blk', None, 'box'), may hold values from -0.25 to 0.25
Outputs:
- scattered: float32 [2, 128, 4096], P(None, ('batch', 'box'), 'blk')
Inputs may be any that keep to these rules, and one draw needn't show every extreme that they name: `skeleton`: each row holds 32 distinct row numbers of a box.
All inputs are finite; a program needn't handle non-finite values. No bound on the sum of `near_mask` on one device may be relied on, other than what follows from the above.
Results may differ from a plain program's by a relative error of at most 0.0003.
Values sent between devices are 32-bit elements; how exact they have to be, the bound alone decides.
No kernel may reach another device: no remote copies, remote signals or barrier semaphores. Data moves between devices by JAX's collectives and lax.ppermute only.
A program may use at most 64 MiB of HBM per device.

v0:
```python
import functools

import jax
import jax.numpy as jnp
import numpy as np
from jax import lax
from jax.experimental import pallas as pl
from jax.experimental.pallas import tpu as pltpu
from jax.sharding import PartitionSpec as P

SWEEP = 16384
WAVENUMBER = 24.0
F32 = jnp.float32
BF16 = jnp.bfloat16
VMEM = pl.BlockSpec(memory_space=pltpu.VMEM)
NN = (((1,), (0,)), ((), ()))
NT = (((1,), (1,)), ((), ()))
TN = (((0,), (0,)), ((), ()))

HALF_PI_1 = float(np.float32(201.0 / 128.0))
HALF_PI_2 = float(np.float32(np.round((np.pi / 2 - HALF_PI_1) * 2.0**22) / 2.0**22))
HALF_PI_3 = float(np.float32(np.pi / 2 - HALF_PI_1 - HALF_PI_2))


def cat(parts, axis):
    return jnp.concatenate(parts, axis=axis)


def dot(a, b, form=NN):
    return lax.dot_general(a, b, form, preferred_element_type=F32)


def split(x):
    high = x.astype(BF16)
    return high, (x - high.astype(F32)).astype(BF16)


def dot3(a, b, form=NN):
    return dot(a[0], b[0], form) + (dot(a[0], b[1], form) + dot(a[1], b[0], form))


def both(pair, function):
    return function(pair[0]), function(pair[1])


def sin_cos_small(r):
    s = r * r
    sin = r + r * s * (-1.6666654611e-1 + s * (8.3321608736e-3 - s * 1.9515295891e-4))
    cos = 1.0 - 0.5 * s + s * s * (4.166664568298827e-2 + s * (-1.388731625493765e-3 + s * 2.443315711809948e-5))
    return sin, cos


def by_quadrant(quadrant, sin, cos):
    odd = (quadrant & 1) == 1
    out_sin = jnp.where(odd, cos, sin)
    out_cos = jnp.where(odd, sin, cos)
    out_sin = jnp.where((quadrant & 2) == 2, -out_sin, out_sin)
    out_cos = jnp.where(((quadrant + 1) & 2) == 2, -out_cos, out_cos)
    return out_sin, out_cos


def one_hot(skeleton, width):
    rows = lax.broadcasted_iota(jnp.int32, (width, skeleton.shape[1]), 0)
    return jnp.where(rows == skeleton, 1.0, 0.0).astype(BF16)


def rows_form(re, im):
    return cat([cat([re, -im], 1), cat([im, re], 1)], 0)


def columns_form(re, im):
    return cat([cat([re, im], 1), cat([-im, re], 1)], 0)


def field_kernel(points_in, angles_in, skeleton_in, inverse_in, top_in, u_out, static_out, high_out, low_out,
                 points, angles, skeleton, inverse, top, sems):
    copies = [
        pltpu.make_async_copy(source, target, sems.at[k])
        for k, (source, target) in enumerate((
            (angles_in, angles), (points_in, points), (skeleton_in, skeleton), (inverse_in, inverse), (top_in, top),
        ))
    ]
    for copy in copies:
        copy.start()
    count = angles.shape[1]
    width = points.shape[1]
    rank = skeleton.shape[1]
    copies[0].wait()
    ids = angles[...]
    quadrant = (ids + SWEEP // 8) >> (SWEEP.bit_length() - 3)
    rest = ids - quadrant * (SWEEP // 4)
    sin, cos = by_quadrant(quadrant, *sin_cos_small(rest.astype(F32) * (2.0 * np.pi / SWEEP)))
    pick = lax.broadcasted_iota(jnp.int32, (8, count), 0) == 0
    columns = jnp.where(pick, cos, sin).T
    cos_column = columns[:, 0:1]
    sin_column = columns[:, 1:2]
    copies[1].wait()
    x = points[0:1, :] * WAVENUMBER
    yz = points[1:2, :] * (0.6 * WAVENUMBER) + points[2:3, :] * (0.8 * WAVENUMBER)
    phase = x * cos_column + yz * sin_column
    turns = jnp.round(phase * (2.0 / np.pi))
    r = ((phase - turns * HALF_PI_1) - turns * HALF_PI_2) - turns * HALF_PI_3
    field_sin, field_cos = by_quadrant(turns.astype(jnp.int32), *sin_cos_small(r))
    field = split(cat([field_cos, field_sin], 1))
    high_out[...] = field[0]
    low_out[...] = field[1]
    copies[2].wait()
    picker = one_hot(skeleton[...], width)
    copies[3].wait()
    parts = split(cat([inverse[0, 0], inverse[0, 1]], 1))
    rows = dot(picker, cat(parts, 1), TN)
    rows_high = rows[:, : 2 * width]
    rows_low = rows[:, 2 * width :]
    whole = rows_high + rows_low
    form = both((rows_high, rows_low), lambda v: rows_form(v[:, :width], v[:, width:]).astype(BF16))
    u_out[...] = dot3(form, field, NT)
    depth = top.shape[3]
    copies[4].wait()
    for part in range(2):
        at = slice(part * rank, (part + 1) * rank)
        static_out[at, :depth] = top[0, part]
        static_out[at, depth:] = whole[:, part * width : (part + 1) * width]


def coupling_kernel(high, low, skeleton_in, mask_in, inverse_in, coupling_in, base_out, high_out, low_out,
                    skeleton, mask, inverse, coupling, sems):
    copies = [
        pltpu.make_async_copy(source, target, sems.at[k])
        for k, (source, target) in enumerate((
            (skeleton_in, skeleton), (mask_in, mask), (inverse_in, inverse), (coupling_in, coupling),
        ))
    ]
    for copy in copies:
        copy.start()
    for copy in copies:
        copy.wait()
    width = inverse.shape[2]
    sides = coupling.shape[1]
    rank = coupling.shape[3]
    depth = sides * rank
    field = (high[...], low[...])
    re = split(inverse[0, 0])
    im = split(inverse[0, 1])
    row_matrix = (rows_form(re[0], im[0]), rows_form(re[1], im[1]))
    column_matrix = (columns_form(re[0], im[0]), columns_form(re[1], im[1]))
    picker = one_hot(skeleton[...], width)
    zero = jnp.zeros_like(picker)
    picker2 = cat([cat([picker, zero], 1), cat([zero, picker], 1)], 0)
    z = split(dot3(field, row_matrix, NT))
    u = dot(z[0], picker2) + dot(z[1], picker2)
    near = []
    for side in range(sides):
        weight = mask[:, side : side + 1].astype(F32)
        near.append(cat([coupling[0, side, 0] * weight, coupling[0, side, 1] * weight], 1))
    near = split(cat(near, 0))
    base_out[:, : 2 * width] = dot3(z, column_matrix)
    base_out[:, 2 * width :] = u
    applied = split(dot3(near, column_matrix))
    for k, out in enumerate((high_out, low_out)):
        chosen = dot(near[k], picker2).astype(BF16)
        for matrix, at, part in ((applied[k], 0, width), (chosen, 2 * width, rank)):
            out[:depth, at : at + 2 * part] = matrix
            out[depth:, at : at + part] = -matrix[:, part:]
            out[depth:, at + part : at + 2 * part] = matrix[:, :part]


def join_kernel(base, even, odd, u, mine, came, row_out, pair_out):
    first = lax.axis_index("box") % 2 == 0
    row_out[0] = jnp.where(first, odd[...], even[...])
    row_out[1] = u[...]
    row_out[2] = jnp.where(first, even[...], odd[...])
    pair_out[0] = mine[...]
    pair_out[1] = came[...]


def message_kernel(even, middle, odd, base, high, low, keep_out, send_out):
    first = lax.axis_index("blk") % 2 == 0
    up = jnp.where(first, odd[...], even[...])
    down = jnp.where(first, even[...], odd[...])
    boxes = 2 * keep_out.shape[0]
    count = base.shape[0]
    width = keep_out.shape[2]
    rank = up.shape[1] // 2
    share = count // boxes
    half = share // 2
    order = (up[0], up[1], up[2], middle[0], middle[2], down[0], down[1], down[2])
    stacked = cat([v[:rank] for v in order] + [v[rank:] for v in order], 0)
    near = split(stacked.T)
    w = base[...] - dot3(near, (high[...], low[...]))
    lower = lax.axis_index("box") % 2 == 0
    for pair in range(boxes // 2):
        at = 2 * pair * share
        mine = w[at : at + share]
        other = w[at + share : at + 2 * share]
        for out, rows in (
            (keep_out, jnp.where(lower, mine, other)),
            (send_out, jnp.where(lower, other, mine)),
        ):
            out[pair, :share] = rows[:, :width]
            out[pair, share : 2 * share] = rows[:, width : 2 * width]
            t = rows[:, 2 * width :]
            out[pair, 2 * share : 2 * share + half] = cat([t[:half], t[half:]], 1)


def forward_kernel(keep, came, *outs):
    place = lax.axis_index("box") // 2
    for k, out in enumerate(outs):
        out[0] = keep[place ^ k]
        out[1] = came[place ^ k]


def blocks_of(refs):
    return [block for v in refs for block in ([v[k] for k in range(v.shape[0])] if len(v.shape) == 3 else [v[...]])]


def stacked_form(block, rank, depth):
    high, low = both(block, lambda part: columns_form(part[:rank, depth:], part[rank:, depth:]))
    return cat([high, high, low], 0)


def prepare_kernel(*refs):
    top_high, top_low, local_out = refs[-3:]
    depth = top_high.shape[1] // 2
    rank = local_out.shape[1] // 6
    for k, block in enumerate(blocks_of(refs[:-3])):
        at = slice(2 * k * rank, 2 * (k + 1) * rank)
        parts = split(block)
        for part, top_out in zip(parts, (top_high, top_low)):
            top_out[at] = rows_form(part[:rank, :depth], part[rank:, :depth])
        local_out[k] = stacked_form(parts, rank, depth)


def top_kernel(offsets, messages, top_high, top_low, prepared, *refs):
    pieces = refs[:messages]
    late = [split(block) for block in blocks_of(refs[messages:-2])]
    out, packed = refs[-2:]
    boxes = 2 * messages
    width = pieces[0].shape[2]
    share = out.shape[1]
    half = share // 2
    ready = prepared.shape[0]
    rank = prepared.shape[1] // 6
    rows = 2 * rank
    depth = boxes * rank
    me = lax.axis_index("box")
    top = [(top_high[...], top_low[...])]
    local = [prepared[k] for k in range(ready)]
    if late:
        top.append([
            cat([rows_form(v[k][:rank, :depth], v[k][rank:, :depth]) for v in late], 0) for k in range(2)
        ])
        local += [stacked_form(v, rank, depth) for v in late]
    for k in range(boxes):
        packed[me ^ k] = pieces[k // 2][k % 2, 2 * share : 2 * share + half]
    t_re = []
    t_im = []
    for box in range(boxes):
        t = cat([packed[box, :, :rows], packed[box, :, rows:]], 0)
        t_re.append(t[:, :rank])
        t_im.append(t[:, rank:])
    t = split(cat(t_re + t_im, 1))
    t_both = cat(t, 0)
    y = []
    for high, low in top:
        first = dot(t_both, high, NT)
        y.append(first[:share] + (first[share:] + dot(t[0], low, NT)))
    y = split(cat(y, 1))
    for k in range(boxes):
        at = slice(k * rows, (k + 1) * rows)
        x = dot(cat([y[0][:, at], y[1][:, at], y[0][:, at]], 1), local[k])
        offset = offsets[k]
        piece = pieces[offset // 2]
        at = pl.ds(pl.multiple_of((me ^ offset) * width, width), width)
        out[0, :, at] = piece[offset % 2, :share] + x[:, :width]
        out[1, :, at] = piece[offset % 2, share : 2 * share] + x[:, width:]


def call(kernel, outs, *arrays, hbm=(), copied=(), extra=()):
    spaces = {i: pl.BlockSpec(memory_space=pl.ANY) for i in hbm}
    spaces.update({i: pl.BlockSpec(memory_space=pltpu.HBM) for i in copied})
    scratch = [pltpu.VMEM(arrays[i].shape, arrays[i].dtype) for i in copied]
    if scratch:
        scratch.append(pltpu.SemaphoreType.DMA((len(scratch),)))
    scratch += extra
    arrays = [pltpu.with_memory_space_constraint(v, pltpu.HBM) if i in copied else v for i, v in enumerate(arrays)]
    return pl.pallas_call(
        kernel,
        out_shape=[jax.ShapeDtypeStruct(shape, dtype) for shape, dtype in outs],
        in_specs=[spaces.get(i, VMEM) for i in range(len(arrays))],
        out_specs=[VMEM] * len(outs),
        scratch_shapes=scratch,
        compiler_params=pltpu.CompilerParams(vmem_limit_bytes=40 * 1024 * 1024),
    )(*arrays)


def swapped(value, axis, bit):
    return lax.ppermute(value, axis, [(i, i ^ bit) for i in range(lax.axis_size(axis))])


def beside(value, axis):
    count = lax.axis_size(axis)
    even = lax.ppermute(value, axis, [(i, i ^ 1) for i in range(count)])
    odd = lax.ppermute(value, axis, [(i, (i + 1) % count if i % 2 else (i - 1) % count) for i in range(count)])
    return even, odd


def on_device(surface_points, angle_ids, near_mask, skeleton, box_inverse_parts, near_coupling, top_inverse):
    boxes = lax.axis_size("box")
    width = box_inverse_parts.shape[2]
    count = angle_ids.shape[0]
    rank = skeleton.shape[1]
    sides = near_mask.shape[1]
    depth = top_inverse.shape[3]
    share = count // boxes
    u, static, high, low = call(
        field_kernel,
        [
            ((2 * rank, count), F32),
            ((2 * rank, depth + width), F32),
            ((count, 2 * width), BF16),
            ((count, 2 * width), BF16),
        ],
        surface_points, angle_ids.reshape(1, count), skeleton, box_inverse_parts, top_inverse,
        copied=range(5),
    )
    base, matrix_high, matrix_low = call(
        coupling_kernel,
        [
            ((count, 2 * width + 2 * rank), F32),
            ((2 * sides * rank, 2 * width + 2 * rank), BF16),
            ((2 * sides * rank, 2 * width + 2 * rank), BF16),
        ],
        high, low, skeleton, near_mask, box_inverse_parts, near_coupling,
        copied=range(2, 6),
    )
    even, odd = beside(u, "box")
    four = swapped(static, "box", boxes // 2)
    row, pair = call(
        join_kernel, [((3,) + u.shape, F32), ((2,) + static.shape, F32)], base, even, odd, u, static, four, hbm=(0,)
    )
    if boxes == 8:
        two = swapped(pair, "box", 2)
        one = swapped(pair, "box", 1)
        early = [pair, two, one]
        late = [swapped(one[:1], "box", 2), swapped(two[1:], "box", 1)]
        offsets = (0, 4, 2, 6, 1, 5, 3, 7)
    else:
        early, late = [pair], []
        offsets = [0, boxes // 2]
        step = boxes // 4
        while step > 0:
            early.append(swapped(jnp.concatenate(early), "box", step))
            offsets += [k ^ step for k in offsets]
            step //= 2
    even, odd = beside(row, "blk")
    length = 2 * share + -(-share // 16) * 8
    message = ((boxes // 2, length, width), F32)
    keep, send = call(
        message_kernel, [message, message],
        even, row, odd, base, matrix_high, matrix_low,
    )
    pieces = call(
        forward_kernel, [((2, length, width), F32)] * (boxes // 2), keep, swapped(send, "box", 1)
    )
    pieces = [pieces[0]] + [swapped(pieces[k], "box", 2 * k) for k in range(1, boxes // 2)]
    ready = boxes - len(late)
    top = ((ready * 2 * rank, 2 * depth), BF16)
    local = ((ready, 6 * rank, 2 * width), BF16)
    prepared = call(prepare_kernel, [top, top, local], *early)
    (out,) = call(
        functools.partial(top_kernel, offsets, len(pieces)), [((2, share, boxes * width), F32)],
        *prepared, *pieces, *late,
        extra=[pltpu.VMEM((boxes, share // 2, width), F32)],
    )
    return out


def solution(mesh):
    return jax.shard_map(
        on_device,
        mesh=mesh,
        in_specs=(
            P(None, ("blk", "box")),
            P("batch"),
            P(("blk", "box"), None),
            P(("blk", "box"), None),
            P(("blk", "box"), None, None, None),
            P(("blk", "box"), None, None, None, None),
            P("blk", None, "box", None),
        ),
        out_specs=P(None, ("batch", "box"), "blk"),
        check_vma=False,
    )
```

profile of v0, /device:TPU:0, one launch (start us, length us, event | category | flops | bytes accessed | tf_op | source)
XLA Modules:
  0.0 33.3 jit_solution(679253369650902572)
XLA Ops:
  0.0 1.4 %shard_map.73 = (f32[64,128]{1,0:T(8,128)S(1)}, f32[64,384]{1,0:T(8,128)S(1)}, bf16[128,256]{1,0:T(8,128)(2,1)S(1)}, bf16[128,256]{1,0:T(8,128)(2,1)S(1)}) custom-call(f32[3,128]{1,0:T(4,128)} %points_in.1, s32[1,128]{1,0:T(1,128)} %bitcast.1, s32[1,32]{1,0:T(1,128)} %skeleton_in.3, f32[1,2,128,128]{3,2,1,0:T(8,128)} %inverse_in.3, f32[1,2,32,256]{3,2,1,0:T(8,128)} %top_in.1), custom_call_target="tpu_custom_call" | custom-call | tf_op jit(solution)/shard_map/pallas_call | solution.py:286
  1.4 4.1 %collective-permute-start.2 = (f32[64,384]{1,0:T(8,128)S(1)}, f32[64,384]{1,0:T(8,128)S(1)}, u32[]{:S(2)}, u32[]{:S(2)}) collective-permute-start(f32[64,384]{1,0:T(8,128)S(1)} %get-tuple-element.27.mine), channel_id=1, source_target_pairs={{0,4},{1,5},{2,6},{3,7},{4,0},{5,1},{6,2},{7,3},{8,12},{9,13},{10,... | collective-permute-start | bytes 294920 | tf_op jit(solution)/shard_map/ppermute | solution.py:297
  5.5 1.5 %collective-permute-start = (f32[64,128]{1,0:T(8,128)S(1)}, f32[64,128]{1,0:T(8,128)S(1)}, u32[]{:S(2)}, u32[]{:S(2)}) collective-permute-start(f32[64,128]{1,0:T(8,128)S(1)} %get-tuple-element.26.u), channel_id=1, source_target_pairs={{0,1},{1,0},{2,3},{3,2},{4,5},{5,4},{6,7},{7,6},{8,9},{9,8},{10,11... | collective-permute-start | bytes 98312 | tf_op jit(solution)/shard_map/ppermute | solution.py:302
  7.0 1.3 %collective-permute-start.1 = (f32[64,128]{1,0:T(8,128)S(1)}, f32[64,128]{1,0:T(8,128)S(1)}, u32[]{:S(2)}, u32[]{:S(2)}) collective-permute-start(f32[64,128]{1,0:T(8,128)S(1)} %get-tuple-element.26.u), channel_id=1, source_target_pairs={{0,7},{1,2},{2,1},{3,4},{4,3},{5,6},{6,5},{7,0},{8,15},{9,10},{10,... | collective-permute-start | bytes 98312 | tf_op jit(solution)/shard_map/ppermute | solution.py:303
  8.3 1.9 %shard_map.74 = (f32[128,320]{1,0:T(8,128)S(1)}, bf16[512,320]{1,0:T(8,128)(2,1)S(1)}, bf16[512,320]{1,0:T(8,128)(2,1)S(1)}) custom-call(bf16[128,256]{1,0:T(8,128)(2,1)S(1)} %get-tuple-element.23.high, bf16[128,256]{1,0:T(8,128)(2,1)S(1)} %get-tuple-element.24.low, s32[1,32]{1,0:T(1,128)} %skeleton_in.3, s32[1,8]{1,0:T(1,128)} %mask_in.1, ...), custom_call_target="tpu_custom_call" | custom-call | tf_op jit(solution)/shard_map/pallas_call | solution.py:286
  10.2 0.0 collective-permute-done.even
  10.2 3.4 %collective-permute-done.1.odd = f32[64,128]{1,0:T(8,128)S(1)} collective-permute-done((f32[64,128]{1,0:T(8,128)S(1)}, f32[64,128]{1,0:T(8,128)S(1)}, u32[]{:S(2)}, u32[]{:S(2)}) %collective-permute-start.1) | collective-permute-done | bytes 32800 | tf_op jit(solution)/shard_map/ppermute | solution.py:303
  13.6 0.1 collective-permute-start.4
  13.7 0.3 collective-permute-start.3
  14.0 1.6 %collective-permute-start.6 = (f32[3,64,128]{2,1,0:T(8,128)S(1)}, f32[3,64,128]{2,1,0:T(8,128)S(1)}, u32[]{:S(2)}, u32[]{:S(2)}) collective-permute-start(f32[3,64,128]{2,1,0:T(8,128)S(1)} %get-tuple-element.32.middle), channel_id=1, source_target_pairs={{0,24},{8,16},{16,8},{24,0},{1,25},{9,17},{17,9},{25,1},{2,26},{10... | collective-permute-start | bytes 294920 | tf_op jit(solution)/shard_map/ppermute | solution.py:303
  15.6 2.8 %collective-permute-done.6.odd = f32[3,64,128]{2,1,0:T(8,128)S(1)} collective-permute-done((f32[3,64,128]{2,1,0:T(8,128)S(1)}, f32[3,64,128]{2,1,0:T(8,128)S(1)}, u32[]{:S(2)}, u32[]{:S(2)}) %collective-permute-start.6) | collective-permute-done | bytes 98336 | tf_op jit(solution)/shard_map/ppermute | solution.py:303
  18.4 0.5 %shard_map.77 = (f32[4,40,128]{2,1,0:T(8,128)S(1)}, f32[4,40,128]{2,1,0:T(8,128)S(1)}) custom-call(f32[3,64,128]{2,1,0:T(8,128)S(1)} %collective-permute-done.5.even, f32[3,64,128]{2,1,0:T(8,128)S(1)} %get-tuple-element.32.middle, f32[3,64,128]{2,1,0:T(8,128)S(1)} %collective-permute-done.6.odd, f32[128,320]{1,0:T(8,128)S(1)} %get-tuple-element.25.base, ...), custom_call_target="tpu_custom_call" | custom-call | tf_op jit(solution)/shard_map/pallas_call | solution.py:286
  19.0 1.8 %collective-permute-start.7 = (f32[4,40,128]{2,1,0:T(8,128)S(1)}, f32[4,40,128]{2,1,0:T(8,128)S(1)}, u32[]{:S(2)}, u32[]{:S(2)}) collective-permute-start(f32[4,40,128]{2,1,0:T(8,128)S(1)} %get-tuple-element.36), channel_id=1, source_target_pairs={{0,1},{1,0},{2,3},{3,2},{4,5},{5,4},{6,7},{7,6},{8,9},{9,8},{10,11... | collective-permute-start | bytes 245768 | tf_op jit(solution)/shard_map/ppermute | solution.py:297
  20.7 2.1 %collective-permute-start.11 = (f32[1,64,384]{2,1,0:T(8,128)S(1)}, f32[1,64,384]{2,1,0:T(8,128)S(1)}, u32[]{:S(2)}, u32[]{:S(2)}) collective-permute-start(f32[1,64,384]{2,1,0:T(8,128)S(1)} %slice.8), channel_id=1, source_target_pairs={{0,2},{1,3},{2,0},{3,1},{4,6},{5,7},{6,4},{7,5},{8,10},{9,11},{10,... | collective-permute-start | bytes 294920 | tf_op jit(solution)/shard_map/ppermute | solution.py:297
  22.8 0.1 collective-permute-start.12
  23.0 1.1 %collective-permute-done.7.came = f32[4,40,128]{2,1,0:T(8,128)S(1)} collective-permute-done((f32[4,40,128]{2,1,0:T(8,128)S(1)}, f32[4,40,128]{2,1,0:T(8,128)S(1)}, u32[]{:S(2)}, u32[]{:S(2)}) %collective-permute-start.7) | collective-permute-done | bytes 81952 | tf_op jit(solution)/shard_map/ppermute | solution.py:297
  24.1 2.5 %collective-permute-start.10 = (f32[2,40,128]{2,1,0:T(8,128)S(1)}, f32[2,40,128]{2,1,0:T(8,128)S(1)}, u32[]{:S(2)}, u32[]{:S(2)}) collective-permute-start(f32[2,40,128]{2,1,0:T(8,128)S(1)} %get-tuple-element.40), channel_id=1, source_target_pairs={{0,6},{1,7},{2,4},{3,5},{4,2},{5,3},{6,0},{7,1},{8,14},{9,15},{10,... | collective-permute-start | bytes 122888 | tf_op jit(solution)/shard_map/ppermute | solution.py:297
  26.6 0.4 %collective-permute-start.8 = (f32[2,40,128]{2,1,0:T(8,128)S(1)}, f32[2,40,128]{2,1,0:T(8,128)S(1)}, u32[]{:S(2)}, u32[]{:S(2)}) collective-permute-start(f32[2,40,128]{2,1,0:T(8,128)S(1)} %get-tuple-element.38), channel_id=1, source_target_pairs={{0,2},{1,3},{2,0},{3,1},{4,6},{5,7},{6,4},{7,5},{8,10},{9,11},{10,... | collective-permute-start | bytes 122888 | tf_op jit(solution)/shard_map/ppermute | solution.py:297
  27.0 1.6 %collective-permute-start.9 = (f32[2,40,128]{2,1,0:T(8,128)S(1)}, f32[2,40,128]{2,1,0:T(8,128)S(1)}, u32[]{:S(2)}, u32[]{:S(2)}) collective-permute-start(f32[2,40,128]{2,1,0:T(8,128)S(1)} %get-tuple-element.39), channel_id=1, source_target_pairs={{0,4},{1,5},{2,6},{3,7},{4,0},{5,1},{6,2},{7,3},{8,12},{9,13},{10,... | collective-permute-start | bytes 122888 | tf_op jit(solution)/shard_map/ppermute | solution.py:297
  28.6 0.1 shard_map.76
  28.7 1.3 %collective-permute-done.10.refs_3_ = f32[2,40,128]{2,1,0:T(8,128)S(1)} collective-permute-done((f32[2,40,128]{2,1,0:T(8,128)S(1)}, f32[2,40,128]{2,1,0:T(8,128)S(1)}, u32[]{:S(2)}, u32[]{:S(2)}) %collective-permute-start.10) | collective-permute-done | bytes 40992 | tf_op jit(solution)/shard_map/ppermute | solution.py:297
  30.0 0.9 %collective-permute-done.8.refs_1_ = f32[2,40,128]{2,1,0:T(8,128)S(1)} collective-permute-done((f32[2,40,128]{2,1,0:T(8,128)S(1)}, f32[2,40,128]{2,1,0:T(8,128)S(1)}, u32[]{:S(2)}, u32[]{:S(2)}) %collective-permute-start.8) | collective-permute-done | bytes 40992 | tf_op jit(solution)/shard_map/ppermute | solution.py:297
  30.8 1.0 %collective-permute-done.9.refs_2_ = f32[2,40,128]{2,1,0:T(8,128)S(1)} collective-permute-done((f32[2,40,128]{2,1,0:T(8,128)S(1)}, f32[2,40,128]{2,1,0:T(8,128)S(1)}, u32[]{:S(2)}, u32[]{:S(2)}) %collective-permute-start.9) | collective-permute-done | bytes 40992 | tf_op jit(solution)/shard_map/ppermute | solution.py:297
  31.9 1.4 %shard_map.79 = f32[2,16,1024]{2,1,0:T(8,128)} custom-call(bf16[384,512]{1,0:T(8,128)(2,1)S(1)} %get-tuple-element.29.top_high, bf16[384,512]{1,0:T(8,128)(2,1)S(1)} %get-tuple-element.30.top_low, bf16[6,192,256]{2,1,0:T(8,128)(2,1)S(1)} %get-tuple-element.31.prepared, f32[2,40,128]{2,1,0:T(8,128)S(1)} %get-tuple-element.37.refs_0_, ...), custom_call_target="tpu_custom_call" | custom-call | tf_op jit(solution)/shard_map/pallas_call | solution.py:286
  (11 shorter events, 0.1 us)
Async XLA Ops:
  1.4 12.2 %collective-permute-start.2 = (f32[64,384]{1,0:T(8,128)S(1)}, f32[64,384]{1,0:T(8,128)S(1)}, u32[]{:S(2)}, u32[]{:S(2)}) collective-permute-start(f32[64,384]{1,0:T(8,128)S(1)} %get-tuple-element.27.mine), channel_id=1, source_target_pairs={{0,4},{1,5},{2,6},{3,7},{4,0},{5,1},{6,2},{7,3},{8,12},{9,13},{10,... | collective-permute-start | bytes 294920 | tf_op jit(solution)/shard_map/ppermute | solution.py:297
  5.5 4.8 %collective-permute-start = (f32[64,128]{1,0:T(8,128)S(1)}, f32[64,128]{1,0:T(8,128)S(1)}, u32[]{:S(2)}, u32[]{:S(2)}) collective-permute-start(f32[64,128]{1,0:T(8,128)S(1)} %get-tuple-element.26.u), channel_id=1, source_target_pairs={{0,1},{1,0},{2,3},{3,2},{4,5},{5,4},{6,7},{7,6},{8,9},{9,8},{10,11... | collective-permute-start | bytes 98312 | tf_op jit(solution)/shard_map/ppermute | solution.py:302
  7.0 6.6 %collective-permute-start.1 = (f32[64,128]{1,0:T(8,128)S(1)}, f32[64,128]{1,0:T(8,128)S(1)}, u32[]{:S(2)}, u32[]{:S(2)}) collective-permute-start(f32[64,128]{1,0:T(8,128)S(1)} %get-tuple-element.26.u), channel_id=1, source_target_pairs={{0,7},{1,2},{2,1},{3,4},{4,3},{5,6},{6,5},{7,0},{8,15},{9,10},{10,... | collective-permute-start | bytes 98312 | tf_op jit(solution)/shard_map/ppermute | solution.py:303
  13.6 7.1 %collective-permute-start.4 = (f32[2,64,384]{2,1,0:T(8,128)S(1)}, f32[2,64,384]{2,1,0:T(8,128)S(1)}, u32[]{:S(2)}, u32[]{:S(2)}) collective-permute-start(f32[2,64,384]{2,1,0:T(8,128)S(1)} %get-tuple-element.28.refs_0_), channel_id=1, source_target_pairs={{0,1},{1,0},{2,3},{3,2},{4,5},{5,4},{6,7},{7,6},{8,9},{9,8},{10,11... | collective-permute-start | bytes 589832 | tf_op jit(solution)/shard_map/ppermute | solution.py:297
  13.7 9.1 %collective-permute-start.3 = (f32[2,64,384]{2,1,0:T(8,128)S(1)}, f32[2,64,384]{2,1,0:T(8,128)S(1)}, u32[]{:S(2)}, u32[]{:S(2)}) collective-permute-start(f32[2,64,384]{2,1,0:T(8,128)S(1)} %get-tuple-element.28.refs_0_), channel_id=1, source_target_pairs={{0,2},{1,3},{2,0},{3,1},{4,6},{5,7},{6,4},{7,5},{8,10},{9,11},{10,... | collective-permute-start | bytes 589832 | tf_op jit(solution)/shard_map/ppermute | solution.py:297
  14.0 1.6 %collective-permute-start.5 = (f32[3,64,128]{2,1,0:T(8,128)S(1)}, f32[3,64,128]{2,1,0:T(8,128)S(1)}, u32[]{:S(2)}, u32[]{:S(2)}) collective-permute-start(f32[3,64,128]{2,1,0:T(8,128)S(1)} %get-tuple-element.32.middle), channel_id=1, source_target_pairs={{0,8},{8,0},{16,24},{24,16},{1,9},{9,1},{17,25},{25,17},{2,10},{10... | collective-permute-start | bytes 294920 | tf_op jit(solution)/shard_map/ppermute | solution.py:302
  14.0 4.4 %collective-permute-start.6 = (f32[3,64,128]{2,1,0:T(8,128)S(1)}, f32[3,64,128]{2,1,0:T(8,128)S(1)}, u32[]{:S(2)}, u32[]{:S(2)}) collective-permute-start(f32[3,64,128]{2,1,0:T(8,128)S(1)} %get-tuple-element.32.middle), channel_id=1, source_target_pairs={{0,24},{8,16},{16,8},{24,0},{1,25},{9,17},{17,9},{25,1},{2,26},{10... | collective-permute-start | bytes 294920 | tf_op jit(solution)/shard_map/ppermute | solution.py:303
  19.0 5.1 %collective-permute-start.7 = (f32[4,40,128]{2,1,0:T(8,128)S(1)}, f32[4,40,128]{2,1,0:T(8,128)S(1)}, u32[]{:S(2)}, u32[]{:S(2)}) collective-permute-start(f32[4,40,128]{2,1,0:T(8,128)S(1)} %get-tuple-element.36), channel_id=1, source_target_pairs={{0,1},{1,0},{2,3},{3,2},{4,5},{5,4},{6,7},{7,6},{8,9},{9,8},{10,11... | collective-permute-start | bytes 245768 | tf_op jit(solution)/shard_map/ppermute | solution.py:297
  20.7 11.2 %collective-permute-start.11 = (f32[1,64,384]{2,1,0:T(8,128)S(1)}, f32[1,64,384]{2,1,0:T(8,128)S(1)}, u32[]{:S(2)}, u32[]{:S(2)}) collective-permute-start(f32[1,64,384]{2,1,0:T(8,128)S(1)} %slice.8), channel_id=1, source_target_pairs={{0,2},{1,3},{2,0},{3,1},{4,6},{5,7},{6,4},{7,5},{8,10},{9,11},{10,... | collective-permute-start | bytes 294920 | tf_op jit(solution)/shard_map/ppermute | solution.py:297
  22.8 9.1 %collective-permute-start.12 = (f32[1,64,384]{2,1,0:T(8,128)S(1)}, f32[1,64,384]{2,1,0:T(8,128)S(1)}, u32[]{:S(2)}, u32[]{:S(2)}) collective-permute-start(f32[1,64,384]{2,1,0:T(8,128)S(1)} %slice.9), channel_id=1, source_target_pairs={{0,1},{1,0},{2,3},{3,2},{4,5},{5,4},{6,7},{7,6},{8,9},{9,8},{10,11... | collective-permute-start | bytes 294920 | tf_op jit(solution)/shard_map/ppermute | solution.py:297
  24.1 5.9 %collective-permute-start.10 = (f32[2,40,128]{2,1,0:T(8,128)S(1)}, f32[2,40,128]{2,1,0:T(8,128)S(1)}, u32[]{:S(2)}, u32[]{:S(2)}) collective-permute-start(f32[2,40,128]{2,1,0:T(8,128)S(1)} %get-tuple-element.40), channel_id=1, source_target_pairs={{0,6},{1,7},{2,4},{3,5},{4,2},{5,3},{6,0},{7,1},{8,14},{9,15},{10,... | collective-permute-start | bytes 122888 | tf_op jit(solution)/shard_map/ppermute | solution.py:297
  26.6 4.2 %collective-permute-start.8 = (f32[2,40,128]{2,1,0:T(8,128)S(1)}, f32[2,40,128]{2,1,0:T(8,128)S(1)}, u32[]{:S(2)}, u32[]{:S(2)}) collective-permute-start(f32[2,40,128]{2,1,0:T(8,128)S(1)} %get-tuple-element.38), channel_id=1, source_target_pairs={{0,2},{1,3},{2,0},{3,1},{4,6},{5,7},{6,4},{7,5},{8,10},{9,11},{10,... | collective-permute-start | bytes 122888 | tf_op jit(solution)/shard_map/ppermute | solution.py:297
  27.0 4.9 %collective-permute-start.9 = (f32[2,40,128]{2,1,0:T(8,128)S(1)}, f32[2,40,128]{2,1,0:T(8,128)S(1)}, u32[]{:S(2)}, u32[]{:S(2)}) collective-permute-start(f32[2,40,128]{2,1,0:T(8,128)S(1)} %get-tuple-element.39), channel_id=1, source_target_pairs={{0,4},{1,5},{2,6},{3,7},{4,0},{5,1},{6,2},{7,3},{8,12},{9,13},{10,... | collective-permute-start | bytes 122888 | tf_op jit(solution)/shard_map/ppermute | solution.py:297
where the time goes:
time: 33.4 us; the launch traced here: 33.3 us
  starting transfers between devices  17.3 us (52%)
  waiting for transfers between devices  10.6 us (32%)
  Pallas kernels  5.36 us (16%)
    ppermute x9, starting transfers between devices, swapped(): lax.ppermute(value, axis, [(i, i ^ bit) for i in range(lax.axis_size(axis...  12.9 us
    ppermute x2, waiting for transfers between devices, beside(): lax.ppermute(value, axis, [(i, (i + 1) % count if i % 2 else (i - 1) % co...  6.21 us
    pallas_call x7, Pallas kernels, call(): pl.pallas_call(kernel, out_shape=[jax.ShapeDtypeStruct(shape, dtype) for...  5.36 us
    ppermute x9, waiting for transfers between devices, swapped(): lax.ppermute(value, axis, [(i, i ^ bit) for i in range(lax.axis_size(axis...  4.33 us
    ppermute x2, starting transfers between devices, beside(): lax.ppermute(value, axis, [(i, (i + 1) % count if i % 2 else (i - 1) % co...  2.89 us
    ppermute x2, starting transfers between devices, beside(): even = lax.ppermute(value, axis, [(i, i ^ 1) for i in range(count)])  1.52 us
  transfers between devices with their start and end apart: 13, of which 6 were waited for; matrix products, arithmetic and copies ran while one was open for 0% of the time, Pallas kernels for 8%

commit v1 on v0

--- a/solution.py
+++ b/solution.py
@@ -12,6 +12,7 @@
 WAVENUMBER = 24.0
 F32 = jnp.float32
 BF16 = jnp.bfloat16
+COST = pl.CostEstimate(flops=10**10, bytes_accessed=10**7, transcendentals=0)
 VMEM = pl.BlockSpec(memory_space=pltpu.VMEM)
 NN = (((1,), (0,)), ((), ()))
 NT = (((1,), (1,)), ((), ()))
@@ -164,26 +165,27 @@
             out[depth:, at + part : at + 2 * part] = matrix[:, :part]
 
 
-def join_kernel(base, even, odd, u, mine, came, row_out, pair_out):
+def join_kernel(base, middle_even, middle_odd, even, odd, mine, came, sides_out, pair_out):
     first = lax.axis_index("box") % 2 == 0
-    row_out[0] = jnp.where(first, odd[...], even[...])
-    row_out[1] = u[...]
-    row_out[2] = jnp.where(first, even[...], odd[...])
+    sides_out[0] = jnp.where(first, odd[...], even[...])
+    sides_out[1] = jnp.where(first, even[...], odd[...])
     pair_out[0] = mine[...]
     pair_out[1] = came[...]
 
 
-def message_kernel(even, middle, odd, base, high, low, keep_out, send_out):
+def message_kernel(even, odd, middle_even, middle_odd, sides, base, high, low, keep_out, send_out):
     first = lax.axis_index("blk") % 2 == 0
     up = jnp.where(first, odd[...], even[...])
     down = jnp.where(first, even[...], odd[...])
+    middle_up = jnp.where(first, middle_odd[...], middle_even[...])
+    middle_down = jnp.where(first, middle_even[...], middle_odd[...])
     boxes = 2 * keep_out.shape[0]
     count = base.shape[0]
     width = keep_out.shape[2]
     rank = up.shape[1] // 2
     share = count // boxes
     half = share // 2
-    order = (up[0], up[1], up[2], middle[0], middle[2], down[0], down[1], down[2])
+    order = (up[0], middle_up, up[1], sides[0], sides[1], down[0], middle_down, down[1])
     stacked = cat([v[:rank] for v in order] + [v[rank:] for v in order], 0)
     near = split(stacked.T)
     w = base[...] - dot3(near, (high[...], low[...]))
@@ -275,7 +277,7 @@
         out[1, :, at] = piece[offset % 2, share : 2 * share] + x[:, width:]
 
 
-def call(kernel, outs, *arrays, hbm=(), copied=(), extra=()):
+def call(kernel, outs, *arrays, hbm=(), copied=(), extra=(), cost=None):
     spaces = {i: pl.BlockSpec(memory_space=pl.ANY) for i in hbm}
     spaces.update({i: pl.BlockSpec(memory_space=pltpu.HBM) for i in copied})
     scratch = [pltpu.VMEM(arrays[i].shape, arrays[i].dtype) for i in copied]
@@ -289,6 +291,7 @@
         in_specs=[spaces.get(i, VMEM) for i in range(len(arrays))],
         out_specs=[VMEM] * len(outs),
         scratch_shapes=scratch,
+        cost_estimate=cost,
         compiler_params=pltpu.CompilerParams(vmem_limit_bytes=40 * 1024 * 1024),
     )(*arrays)
 
@@ -335,8 +338,10 @@
     )
     even, odd = beside(u, "box")
     four = swapped(static, "box", boxes // 2)
-    row, pair = call(
-        join_kernel, [((3,) + u.shape, F32), ((2,) + static.shape, F32)], base, even, odd, u, static, four, hbm=(0,)
+    middle = beside(u, "blk")
+    across, pair = call(
+        join_kernel, [((2,) + u.shape, F32), ((2,) + static.shape, F32)],
+        base, *middle, even, odd, static, four, hbm=(0, 1, 2),
     )
     if boxes == 8:
         two = swapped(pair, "box", 2)
@@ -352,12 +357,13 @@
             early.append(swapped(jnp.concatenate(early), "box", step))
             offsets += [k ^ step for k in offsets]
             step //= 2
-    even, odd = beside(row, "blk")
+    even, odd = beside(across, "blk")
     length = 2 * share + -(-share // 16) * 8
     message = ((boxes // 2, length, width), F32)
     keep, send = call(
         message_kernel, [message, message],
-        even, row, odd, base, matrix_high, matrix_low,
+        even, odd, *middle, across, base, matrix_high, matrix_low,
+        cost=COST,
     )
     pieces = call(
         forward_kernel, [((2, length, width), F32)] * (boxes // 2), keep, swapped(send, "box", 1)

time: 33.4 us -> 35.5 us (1.063)
  waiting for transfers between devices: 10.6 us -> 12.9 us
    ppermute x9, waiting for transfers between devices: 4.33 us -> 6.54 us  [swapped(): lax.ppermute(value, axis, [(i, i ^ bit) for i in range(lax.axis_size(axis...]
    ppermute x9, starting transfers between devices: 12.9 us -> 11.9 us  [swapped(): lax.ppermute(value, axis, [(i, i ^ bit) for i in range(lax.axis_size(axis...]
    ppermute x2 -> x3, starting transfers between devices: 2.89 us -> 3.55 us  [beside(): lax.ppermute(value, axis, [(i, (i + 1) % count if i % 2 else (i - 1) % co...]
    ppermute x2 -> x3, waiting for transfers between devices: 6.21 us -> 6 us  [beside(): lax.ppermute(value, axis, [(i, (i + 1) % count if i % 2 else (i - 1) % co...]
    ppermute x2 -> x3, starting transfers between devices: 1.52 us -> 1.59 us  [beside(): even = lax.ppermute(value, axis, [(i, i ^ 1) for i in range(count)])]
  transfers between devices with their start and end apart: 13 -> 15, of which waited for: 6 -> 6; matrix products, arithmetic and copies ran while one was open for 0% -> 0% of each run, Pallas kernels for 8% -> 7%
where the time goes in v1:
time: 35.5 us; the launch traced here: 35.3 us
  starting transfers between devices  17 us (48%)
  waiting for transfers between devices  12.9 us (36%)
  Pallas kernels  5.35 us (15%)
    ppermute x9, starting transfers between devices, swapped(): lax.ppermute(value, axis, [(i, i ^ bit) for i in range(lax.axis_size(axis...  11.9 us
    ppermute x9, waiting for transfers between devices, swapped(): lax.ppermute(value, axis, [(i, i ^ bit) for i in range(lax.axis_size(axis...  6.54 us
    ppermute x3, waiting for transfers between devices, beside(): lax.ppermute(value, axis, [(i, (i + 1) % count if i % 2 else (i - 1) % co...  6 us
    pallas_call x7, Pallas kernels, call(): pl.pallas_call(kernel, out_shape=[jax.ShapeDtypeStruct(shape, dtype) for...  5.35 us
    ppermute x3, starting transfers between devices, beside(): lax.ppermute(value, axis, [(i, (i + 1) % count if i % 2 else (i - 1) % co...  3.55 us
    ppermute x3, starting transfers between devices, beside(): even = lax.ppermute(value, axis, [(i, i ^ 1) for i in range(count)])  1.59 us
  transfers between devices with their start and end apart: 15, of which 6 were waited for; matrix products, arithmetic and copies ran while one was open for 0% of the time, Pallas kernels for 7%

profile of v1, /device:TPU:0, one launch (start us, length us, event | category | flops | bytes accessed | tf_op | source)
XLA Modules:
  0.0 35.3 jit_solution(17340524722075695322)
XLA Ops:
  0.0 1.4 %shard_map.73 = (f32[64,128]{1,0:T(8,128)S(1)}, f32[64,384]{1,0:T(8,128)S(1)}, bf16[128,256]{1,0:T(8,128)(2,1)S(1)}, bf16[128,256]{1,0:T(8,128)(2,1)S(1)}) custom-call(f32[3,128]{1,0:T(4,128)} %points_in.1, s32[1,128]{1,0:T(1,128)} %bitcast.1, s32[1,32]{1,0:T(1,128)} %skeleton_in.3, f32[1,2,128,128]{3,2,1,0:T(8,128)} %inverse_in.3, f32[1,2,32,256]{3,2,1,0:T(8,128)} %top_in.1), custom_call_target="tpu_custom_call" | custom-call | tf_op jit(solution)/shard_map/pallas_call | solution.py:288
  1.4 4.1 %collective-permute-start.4 = (f32[64,384]{1,0:T(8,128)S(1)}, f32[64,384]{1,0:T(8,128)S(1)}, u32[]{:S(2)}, u32[]{:S(2)}) collective-permute-start(f32[64,384]{1,0:T(8,128)S(1)} %get-tuple-element.27.mine), channel_id=1, source_target_pairs={{0,4},{1,5},{2,6},{3,7},{4,0},{5,1},{6,2},{7,3},{8,12},{9,13},{10,... | collective-permute-start | bytes 294920 | tf_op jit(solution)/shard_map/ppermute | solution.py:300
  5.5 1.6 %collective-permute-start.1 = (f32[64,128]{1,0:T(8,128)S(1)}, f32[64,128]{1,0:T(8,128)S(1)}, u32[]{:S(2)}, u32[]{:S(2)}) collective-permute-start(f32[64,128]{1,0:T(8,128)S(1)} %get-tuple-element.26), channel_id=1, source_target_pairs={{0,24},{8,16},{16,8},{24,0},{1,25},{9,17},{17,9},{25,1},{2,26},{10... | collective-permute-start | bytes 98312 | tf_op jit(solution)/shard_map/ppermute | solution.py:306
  7.1 1.5 %collective-permute-start.2 = (f32[64,128]{1,0:T(8,128)S(1)}, f32[64,128]{1,0:T(8,128)S(1)}, u32[]{:S(2)}, u32[]{:S(2)}) collective-permute-start(f32[64,128]{1,0:T(8,128)S(1)} %get-tuple-element.26), channel_id=1, source_target_pairs={{0,1},{1,0},{2,3},{3,2},{4,5},{5,4},{6,7},{7,6},{8,9},{9,8},{10,11... | collective-permute-start | bytes 98312 | tf_op jit(solution)/shard_map/ppermute | solution.py:305
  8.6 1.3 %collective-permute-start.3 = (f32[64,128]{1,0:T(8,128)S(1)}, f32[64,128]{1,0:T(8,128)S(1)}, u32[]{:S(2)}, u32[]{:S(2)}) collective-permute-start(f32[64,128]{1,0:T(8,128)S(1)} %get-tuple-element.26), channel_id=1, source_target_pairs={{0,7},{1,2},{2,1},{3,4},{4,3},{5,6},{6,5},{7,0},{8,15},{9,10},{10,... | collective-permute-start | bytes 98312 | tf_op jit(solution)/shard_map/ppermute | solution.py:306
  9.9 1.9 %shard_map.74 = (f32[128,320]{1,0:T(8,128)S(1)}, bf16[512,320]{1,0:T(8,128)(2,1)S(1)}, bf16[512,320]{1,0:T(8,128)(2,1)S(1)}) custom-call(bf16[128,256]{1,0:T(8,128)(2,1)S(1)} %get-tuple-element.23.high, bf16[128,256]{1,0:T(8,128)(2,1)S(1)} %get-tuple-element.24.low, s32[1,32]{1,0:T(1,128)} %skeleton_in.3, s32[1,8]{1,0:T(1,128)} %mask_in.1, ...), custom_call_target="tpu_custom_call" | custom-call | tf_op jit(solution)/shard_map/pallas_call | solution.py:288
  11.9 3.4 %collective-permute-done.3.odd = f32[64,128]{1,0:T(8,128)S(1)} collective-permute-done((f32[64,128]{1,0:T(8,128)S(1)}, f32[64,128]{1,0:T(8,128)S(1)}, u32[]{:S(2)}, u32[]{:S(2)}) %collective-permute-start.3) | collective-permute-done | bytes 32800 | tf_op jit(solution)/shard_map/ppermute | solution.py:306
  15.2 0.1 collective-permute-start.7
  15.3 0.7 %collective-permute-start.8 = (f32[2,64,128]{2,1,0:T(8,128)S(1)}, f32[2,64,128]{2,1,0:T(8,128)S(1)}, u32[]{:S(2)}, u32[]{:S(2)}) collective-permute-start(f32[2,64,128]{2,1,0:T(8,128)S(1)} %get-tuple-element.32.sides), channel_id=1, source_target_pairs={{0,24},{8,16},{16,8},{24,0},{1,25},{9,17},{17,9},{25,1},{2,26},{10... | collective-permute-start | bytes 196616 | tf_op jit(solution)/shard_map/ppermute | solution.py:306
  16.0 0.3 collective-permute-start.6
  16.3 0.3 collective-permute-done.7.even
  16.6 2.6 %collective-permute-done.8.odd = f32[2,64,128]{2,1,0:T(8,128)S(1)} collective-permute-done((f32[2,64,128]{2,1,0:T(8,128)S(1)}, f32[2,64,128]{2,1,0:T(8,128)S(1)}, u32[]{:S(2)}, u32[]{:S(2)}) %collective-permute-start.8) | collective-permute-done | bytes 65568 | tf_op jit(solution)/shard_map/ppermute | solution.py:306
  19.2 0.5 %shard_map.77 = (f32[4,40,128]{2,1,0:T(8,128)S(1)}, f32[4,40,128]{2,1,0:T(8,128)S(1)}) custom-call(f32[2,64,128]{2,1,0:T(8,128)S(1)} %collective-permute-done.7.even, f32[2,64,128]{2,1,0:T(8,128)S(1)} %collective-permute-done.8.odd, f32[64,128]{1,0:T(8,128)S(1)} %collective-permute-done.middle_even, f32[64,128]{1,0:T(8,128)S(1)} %collective-permute-done.1.middle_odd, ...), custom_call_target="tpu_custom_call" | custom-call | flops 10000000000 | bytes 10000000 | tf_op jit(solution)/shard_map/pallas_call | solution.py:288
  19.7 0.0 collective-permute-start.9
  19.8 3.1 %collective-permute-done.6.refs_2_ = f32[2,64,384]{2,1,0:T(8,128)S(1)} collective-permute-done((f32[2,64,384]{2,1,0:T(8,128)S(1)}, f32[2,64,384]{2,1,0:T(8,128)S(1)}, u32[]{:S(2)}, u32[]{:S(2)}) %collective-permute-start.6) | collective-permute-done | bytes 196640 | tf_op jit(solution)/shard_map/ppermute | solution.py:300
  22.9 2.7 %collective-permute-start.13 = (f32[1,64,384]{2,1,0:T(8,128)S(1)}, f32[1,64,384]{2,1,0:T(8,128)S(1)}, u32[]{:S(2)}, u32[]{:S(2)}) collective-permute-start(f32[1,64,384]{2,1,0:T(8,128)S(1)} %slice.8), channel_id=1, source_target_pairs={{0,2},{1,3},{2,0},{3,1},{4,6},{5,7},{6,4},{7,5},{8,10},{9,11},{10,... | collective-permute-start | bytes 294920 | tf_op jit(solution)/shard_map/ppermute | solution.py:300
  25.6 0.3 collective-permute-start.14
  25.9 0.5 %collective-permute-start.10 = (f32[2,40,128]{2,1,0:T(8,128)S(1)}, f32[2,40,128]{2,1,0:T(8,128)S(1)}, u32[]{:S(2)}, u32[]{:S(2)}) collective-permute-start(f32[2,40,128]{2,1,0:T(8,128)S(1)} %get-tuple-element.38), channel_id=1, source_target_pairs={{0,2},{1,3},{2,0},{3,1},{4,6},{5,7},{6,4},{7,5},{8,10},{9,11},{10,... | collective-permute-start | bytes 122888 | tf_op jit(solution)/shard_map/ppermute | solution.py:300
  26.4 1.7 %collective-permute-start.11 = (f32[2,40,128]{2,1,0:T(8,128)S(1)}, f32[2,40,128]{2,1,0:T(8,128)S(1)}, u32[]{:S(2)}, u32[]{:S(2)}) collective-permute-start(f32[2,40,128]{2,1,0:T(8,128)S(1)} %get-tuple-element.39), channel_id=1, source_target_pairs={{0,4},{1,5},{2,6},{3,7},{4,0},{5,1},{6,2},{7,3},{8,12},{9,13},{10,... | collective-permute-start | bytes 122888 | tf_op jit(solution)/shard_map/ppermute | solution.py:300
  28.1 2.3 %collective-permute-start.12 = (f32[2,40,128]{2,1,0:T(8,128)S(1)}, f32[2,40,128]{2,1,0:T(8,128)S(1)}, u32[]{:S(2)}, u32[]{:S(2)}) collective-permute-start(f32[2,40,128]{2,1,0:T(8,128)S(1)} %get-tuple-element.40), channel_id=1, source_target_pairs={{0,6},{1,7},{2,4},{3,5},{4,2},{5,3},{6,0},{7,1},{8,14},{9,15},{10,... | collective-permute-start | bytes 122888 | tf_op jit(solution)/shard_map/ppermute | solution.py:300
  30.4 0.1 shard_map.76
  30.5 0.8 %collective-permute-done.11.refs_2_ = f32[2,40,128]{2,1,0:T(8,128)S(1)} collective-permute-done((f32[2,40,128]{2,1,0:T(8,128)S(1)}, f32[2,40,128]{2,1,0:T(8,128)S(1)}, u32[]{:S(2)}, u32[]{:S(2)}) %collective-permute-start.11) | collective-permute-done | bytes 40992 | tf_op jit(solution)/shard_map/ppermute | solution.py:300
  31.3 2.6 %collective-permute-done.12.refs_3_ = f32[2,40,128]{2,1,0:T(8,128)S(1)} collective-permute-done((f32[2,40,128]{2,1,0:T(8,128)S(1)}, f32[2,40,128]{2,1,0:T(8,128)S(1)}, u32[]{:S(2)}, u32[]{:S(2)}) %collective-permute-start.12) | collective-permute-done | bytes 40992 | tf_op jit(solution)/shard_map/ppermute | solution.py:300
  33.9 1.4 %shard_map.79 = f32[2,16,1024]{2,1,0:T(8,128)} custom-call(bf16[384,512]{1,0:T(8,128)(2,1)S(1)} %get-tuple-element.29.top_high, bf16[384,512]{1,0:T(8,128)(2,1)S(1)} %get-tuple-element.30.top_low, bf16[6,192,256]{2,1,0:T(8,128)(2,1)S(1)} %get-tuple-element.31.prepared, f32[2,40,128]{2,1,0:T(8,128)S(1)} %get-tuple-element.37.refs_0_, ...), custom_call_target="tpu_custom_call" | custom-call | tf_op jit(solution)/shard_map/pallas_call | solution.py:288
  (15 shorter events, 0.1 us)
Async XLA Ops:
  1.4 13.8 %collective-permute-start.4 = (f32[64,384]{1,0:T(8,128)S(1)}, f32[64,384]{1,0:T(8,128)S(1)}, u32[]{:S(2)}, u32[]{:S(2)}) collective-permute-start(f32[64,384]{1,0:T(8,128)S(1)} %get-tuple-element.27.mine), channel_id=1, source_target_pairs={{0,4},{1,5},{2,6},{3,7},{4,0},{5,1},{6,2},{7,3},{8,12},{9,13},{10,... | collective-permute-start | bytes 294920 | tf_op jit(solution)/shard_map/ppermute | solution.py:300
  5.5 6.4 %collective-permute-start = (f32[64,128]{1,0:T(8,128)S(1)}, f32[64,128]{1,0:T(8,128)S(1)}, u32[]{:S(2)}, u32[]{:S(2)}) collective-permute-start(f32[64,128]{1,0:T(8,128)S(1)} %get-tuple-element.26), channel_id=1, source_target_pairs={{0,8},{8,0},{16,24},{24,16},{1,9},{9,1},{17,25},{25,17},{2,10},{10... | collective-permute-start | bytes 98312 | tf_op jit(solution)/shard_map/ppermute | solution.py:305
  5.5 6.4 %collective-permute-start.1 = (f32[64,128]{1,0:T(8,128)S(1)}, f32[64,128]{1,0:T(8,128)S(1)}, u32[]{:S(2)}, u32[]{:S(2)}) collective-permute-start(f32[64,128]{1,0:T(8,128)S(1)} %get-tuple-element.26), channel_id=1, source_target_pairs={{0,24},{8,16},{16,8},{24,0},{1,25},{9,17},{17,9},{25,1},{2,26},{10... | collective-permute-start | bytes 98312 | tf_op jit(solution)/shard_map/ppermute | solution.py:306
  7.1 4.8 %collective-permute-start.2 = (f32[64,128]{1,0:T(8,128)S(1)}, f32[64,128]{1,0:T(8,128)S(1)}, u32[]{:S(2)}, u32[]{:S(2)}) collective-permute-start(f32[64,128]{1,0:T(8,128)S(1)} %get-tuple-element.26), channel_id=1, source_target_pairs={{0,1},{1,0},{2,3},{3,2},{4,5},{5,4},{6,7},{7,6},{8,9},{9,8},{10,11... | collective-permute-start | bytes 98312 | tf_op jit(solution)/shard_map/ppermute | solution.py:305
  8.6 6.6 %collective-permute-start.3 = (f32[64,128]{1,0:T(8,128)S(1)}, f32[64,128]{1,0:T(8,128)S(1)}, u32[]{:S(2)}, u32[]{:S(2)}) collective-permute-start(f32[64,128]{1,0:T(8,128)S(1)} %get-tuple-element.26), channel_id=1, source_target_pairs={{0,7},{1,2},{2,1},{3,4},{4,3},{5,6},{6,5},{7,0},{8,15},{9,10},{10,... | collective-permute-start | bytes 98312 | tf_op jit(solution)/shard_map/ppermute | solution.py:306
  15.2 1.3 %collective-permute-start.7 = (f32[2,64,128]{2,1,0:T(8,128)S(1)}, f32[2,64,128]{2,1,0:T(8,128)S(1)}, u32[]{:S(2)}, u32[]{:S(2)}) collective-permute-start(f32[2,64,128]{2,1,0:T(8,128)S(1)} %get-tuple-element.32.sides), channel_id=1, source_target_pairs={{0,8},{8,0},{16,24},{24,16},{1,9},{9,1},{17,25},{25,17},{2,10},{10... | collective-permute-start | bytes 196616 | tf_op jit(solution)/shard_map/ppermute | solution.py:305
  15.3 3.9 %collective-permute-start.8 = (f32[2,64,128]{2,1,0:T(8,128)S(1)}, f32[2,64,128]{2,1,0:T(8,128)S(1)}, u32[]{:S(2)}, u32[]{:S(2)}) collective-permute-start(f32[2,64,128]{2,1,0:T(8,128)S(1)} %get-tuple-element.32.sides), channel_id=1, source_target_pairs={{0,24},{8,16},{16,8},{24,0},{1,25},{9,17},{17,9},{25,1},{2,26},{10... | collective-permute-start | bytes 196616 | tf_op jit(solution)/shard_map/ppermute | solution.py:306
  16.0 9.6 %collective-permute-start.5 = (f32[2,64,384]{2,1,0:T(8,128)S(1)}, f32[2,64,384]{2,1,0:T(8,128)S(1)}, u32[]{:S(2)}, u32[]{:S(2)}) collective-permute-start(f32[2,64,384]{2,1,0:T(8,128)S(1)} %get-tuple-element.28.refs_0_), channel_id=1, source_target_pairs={{0,2},{1,3},{2,0},{3,1},{4,6},{5,7},{6,4},{7,5},{8,10},{9,11},{10,... | collective-permute-start | bytes 589832 | tf_op jit(solution)/shard_map/ppermute | solution.py:300
  16.0 6.9 %collective-permute-start.6 = (f32[2,64,384]{2,1,0:T(8,128)S(1)}, f32[2,64,384]{2,1,0:T(8,128)S(1)}, u32[]{:S(2)}, u32[]{:S(2)}) collective-permute-start(f32[2,64,384]{2,1,0:T(8,128)S(1)} %get-tuple-element.28.refs_0_), channel_id=1, source_target_pairs={{0,1},{1,0},{2,3},{3,2},{4,5},{5,4},{6,7},{7,6},{8,9},{9,8},{10,11... | collective-permute-start | bytes 589832 | tf_op jit(solution)/shard_map/ppermute | solution.py:300
  19.7 6.2 %collective-permute-start.9 = (f32[4,40,128]{2,1,0:T(8,128)S(1)}, f32[4,40,128]{2,1,0:T(8,128)S(1)}, u32[]{:S(2)}, u32[]{:S(2)}) collective-permute-start(f32[4,40,128]{2,1,0:T(8,128)S(1)} %get-tuple-element.36), channel_id=1, source_target_pairs={{0,1},{1,0},{2,3},{3,2},{4,5},{5,4},{6,7},{7,6},{8,9},{9,8},{10,11... | collective-permute-start | bytes 245768 | tf_op jit(solution)/shard_map/ppermute | solution.py:300
  22.9 11.1 %collective-permute-start.13 = (f32[1,64,384]{2,1,0:T(8,128)S(1)}, f32[1,64,384]{2,1,0:T(8,128)S(1)}, u32[]{:S(2)}, u32[]{:S(2)}) collective-permute-start(f32[1,64,384]{2,1,0:T(8,128)S(1)} %slice.8), channel_id=1, source_target_pairs={{0,2},{1,3},{2,0},{3,1},{4,6},{5,7},{6,4},{7,5},{8,10},{9,11},{10,... | collective-permute-start | bytes 294920 | tf_op jit(solution)/shard_map/ppermute | solution.py:300
  25.6 8.4 %collective-permute-start.14 = (f32[1,64,384]{2,1,0:T(8,128)S(1)}, f32[1,64,384]{2,1,0:T(8,128)S(1)}, u32[]{:S(2)}, u32[]{:S(2)}) collective-permute-start(f32[1,64,384]{2,1,0:T(8,128)S(1)} %slice.9), channel_id=1, source_target_pairs={{0,1},{1,0},{2,3},{3,2},{4,5},{5,4},{6,7},{7,6},{8,9},{9,8},{10,11... | collective-permute-start | bytes 294920 | tf_op jit(solution)/shard_map/ppermute | solution.py:300
  25.9 4.6 %collective-permute-start.10 = (f32[2,40,128]{2,1,0:T(8,128)S(1)}, f32[2,40,128]{2,1,0:T(8,128)S(1)}, u32[]{:S(2)}, u32[]{:S(2)}) collective-permute-start(f32[2,40,128]{2,1,0:T(8,128)S(1)} %get-tuple-element.38), channel_id=1, source_target_pairs={{0,2},{1,3},{2,0},{3,1},{4,6},{5,7},{6,4},{7,5},{8,10},{9,11},{10,... | collective-permute-start | bytes 122888 | tf_op jit(solution)/shard_map/ppermute | solution.py:300
  26.4 4.9 %collective-permute-start.11 = (f32[2,40,128]{2,1,0:T(8,128)S(1)}, f32[2,40,128]{2,1,0:T(8,128)S(1)}, u32[]{:S(2)}, u32[]{:S(2)}) collective-permute-start(f32[2,40,128]{2,1,0:T(8,128)S(1)} %get-tuple-element.39), channel_id=1, source_target_pairs={{0,4},{1,5},{2,6},{3,7},{4,0},{5,1},{6,2},{7,3},{8,12},{9,13},{10,... | collective-permute-start | bytes 122888 | tf_op jit(solution)/shard_map/ppermute | solution.py:300
  28.1 5.8 %collective-permute-start.12 = (f32[2,40,128]{2,1,0:T(8,128)S(1)}, f32[2,40,128]{2,1,0:T(8,128)S(1)}, u32[]{:S(2)}, u32[]{:S(2)}) collective-permute-start(f32[2,40,128]{2,1,0:T(8,128)S(1)} %get-tuple-element.40), channel_id=1, source_target_pairs={{0,6},{1,7},{2,4},{3,5},{4,2},{5,3},{6,0},{7,1},{8,14},{9,15},{10,... | collective-permute-start | bytes 122888 | tf_op jit(solution)/shard_map/ppermute | solution.py:300

commit v2 on v0

--- a/solution.py
+++ b/solution.py
@@ -12,6 +12,7 @@
 WAVENUMBER = 24.0
 F32 = jnp.float32
 BF16 = jnp.bfloat16
+COST = pl.CostEstimate(flops=10**10, bytes_accessed=10**7, transcendentals=0)
 VMEM = pl.BlockSpec(memory_space=pltpu.VMEM)
 NN = (((1,), (0,)), ((), ()))
 NT = (((1,), (1,)), ((), ()))
@@ -164,13 +165,20 @@
             out[depth:, at + part : at + 2 * part] = matrix[:, :part]
 
 
-def join_kernel(base, even, odd, u, mine, came, row_out, pair_out):
+def hold_kernel(static, out):
+    out[...] = static[...]
+
+
+def pack_kernel(one, two, four, out):
+    out[0] = two[...]
+    out[1] = four[...]
+
+
+def join_kernel(base, even, odd, u, row_out):
     first = lax.axis_index("box") % 2 == 0
     row_out[0] = jnp.where(first, odd[...], even[...])
     row_out[1] = u[...]
     row_out[2] = jnp.where(first, even[...], odd[...])
-    pair_out[0] = mine[...]
-    pair_out[1] = came[...]
 
 
 def message_kernel(even, middle, odd, base, high, low, keep_out, send_out):
@@ -202,7 +210,8 @@
             out[pair, 2 * share : 2 * share + half] = cat([t[:half], t[half:]], 1)
 
 
-def forward_kernel(keep, came, *outs):
+def forward_kernel(count, keep, came, *refs):
+    outs = refs[-count:]
     place = lax.axis_index("box") // 2
     for k, out in enumerate(outs):
         out[0] = keep[place ^ k]
@@ -275,7 +284,7 @@
         out[1, :, at] = piece[offset % 2, share : 2 * share] + x[:, width:]
 
 
-def call(kernel, outs, *arrays, hbm=(), copied=(), extra=()):
+def call(kernel, outs, *arrays, hbm=(), copied=(), extra=(), cost=None):
     spaces = {i: pl.BlockSpec(memory_space=pl.ANY) for i in hbm}
     spaces.update({i: pl.BlockSpec(memory_space=pltpu.HBM) for i in copied})
     scratch = [pltpu.VMEM(arrays[i].shape, arrays[i].dtype) for i in copied]
@@ -289,6 +298,7 @@
         in_specs=[spaces.get(i, VMEM) for i in range(len(arrays))],
         out_specs=[VMEM] * len(outs),
         scratch_shapes=scratch,
+        cost_estimate=cost,
         compiler_params=pltpu.CompilerParams(vmem_limit_bytes=40 * 1024 * 1024),
     )(*arrays)
 
@@ -334,20 +344,19 @@
         copied=range(2, 6),
     )
     even, odd = beside(u, "box")
-    four = swapped(static, "box", boxes // 2)
-    row, pair = call(
-        join_kernel, [((3,) + u.shape, F32), ((2,) + static.shape, F32)], base, even, odd, u, static, four, hbm=(0,)
-    )
+    (row,) = call(join_kernel, [((3,) + u.shape, F32)], base, even, odd, u, hbm=(0,))
+    (static,) = call(hold_kernel, [(static.shape, F32)], static, cost=COST)
+    waited = []
     if boxes == 8:
-        two = swapped(pair, "box", 2)
-        one = swapped(pair, "box", 1)
-        early = [pair, two, one]
-        late = [swapped(one[:1], "box", 2), swapped(two[1:], "box", 1)]
-        offsets = (0, 4, 2, 6, 1, 5, 3, 7)
+        four, two, one = [swapped(static, "box", k) for k in (4, 2, 1)]
+        (pair,) = call(pack_kernel, [((2,) + static.shape, F32)], one, two, four, hbm=(0,))
+        waited = [swapped(four, "box", 2), swapped(four, "box", 3)]
+        early, late = [static, four, two, one, *waited], [swapped(pair, "box", 1)]
+        offsets = (0, 4, 2, 1, 6, 7, 3, 5)
     else:
-        early, late = [pair], []
-        offsets = [0, boxes // 2]
-        step = boxes // 4
+        early, late = [static[None]], []
+        offsets = [0]
+        step = boxes // 2
         while step > 0:
             early.append(swapped(jnp.concatenate(early), "box", step))
             offsets += [k ^ step for k in offsets]
@@ -358,12 +367,14 @@
     keep, send = call(
         message_kernel, [message, message],
         even, row, odd, base, matrix_high, matrix_low,
+        cost=COST,
     )
     pieces = call(
-        forward_kernel, [((2, length, width), F32)] * (boxes // 2), keep, swapped(send, "box", 1)
+        functools.partial(forward_kernel, boxes // 2), [((2, length, width), F32)] * (boxes // 2),
+        keep, swapped(send, "box", 1), *waited, hbm=range(2, 2 + len(waited)),
     )
     pieces = [pieces[0]] + [swapped(pieces[k], "box", 2 * k) for k in range(1, boxes // 2)]
-    ready = boxes - len(late)
+    ready = 6 if late else boxes
     top = ((ready * 2 * rank, 2 * depth), BF16)
     local = ((ready, 6 * rank, 2 * width), BF16)
     prepared = call(prepare_kernel, [top, top, local], *early)

time: 33.4 us -> 35.2 us (1.054)
  starting transfers between devices: 17.3 us -> 19.3 us
    ppermute x2, waiting for transfers between devices: 6.21 us -> 0.01 us  [beside(): lax.ppermute(value, axis, [(i, (i + 1) % count if i % 2 else (i - 1) % co...]
    ppermute x9 -> x10, waiting for transfers between devices: 4.33 us -> 10.3 us  [swapped(): lax.ppermute(value, axis, [(i, i ^ bit) for i in range(lax.axis_size(axis...]
    ppermute x2, starting transfers between devices: 2.89 us -> 5.14 us  [beside(): lax.ppermute(value, axis, [(i, (i + 1) % count if i % 2 else (i - 1) % co...]
    ppermute x9 -> x10, starting transfers between devices: 12.9 us -> 11 us  [swapped(): lax.ppermute(value, axis, [(i, i ^ bit) for i in range(lax.axis_size(axis...]
    ppermute x2, starting transfers between devices: 1.52 us -> 3.1 us  [beside(): even = lax.ppermute(value, axis, [(i, i ^ 1) for i in range(count)])]
    pallas_call x7 -> x9, Pallas kernels: 5.36 us -> 5.38 us  [call(): pl.pallas_call(kernel, out_shape=[jax.ShapeDtypeStruct(shape, dtype) for...]
  transfers between devices with their start and end apart: 13 -> 14, of which waited for: 6 -> 6; matrix products, arithmetic and copies ran while one was open for 0% -> 0% of each run, Pallas kernels for 8% -> 7%
where the time goes in v2:
time: 35.2 us; the launch traced here: 35.1 us
  starting transfers between devices  19.3 us (55%)
  waiting for transfers between devices  10.3 us (29%)
  Pallas kernels  5.38 us (15%)
    ppermute x10, starting transfers between devices, swapped(): lax.ppermute(value, axis, [(i, i ^ bit) for i in range(lax.axis_size(axis...  11 us
    ppermute x10, waiting for transfers between devices, swapped(): lax.ppermute(value, axis, [(i, i ^ bit) for i in range(lax.axis_size(axis...  10.3 us
    pallas_call x9, Pallas kernels, call(): pl.pallas_call(kernel, out_shape=[jax.ShapeDtypeStruct(shape, dtype) for...  5.38 us
    ppermute x2, starting transfers between devices, beside(): lax.ppermute(value, axis, [(i, (i + 1) % count if i % 2 else (i - 1) % co...  5.14 us
    ppermute x2, starting transfers between devices, beside(): even = lax.ppermute(value, axis, [(i, i ^ 1) for i in range(count)])  3.1 us
  transfers between devices with their start and end apart: 14, of which 6 were waited for; matrix products, arithmetic and copies ran while one was open for 0% of the time, Pallas kernels for 7%

profile of v2, /device:TPU:0, one launch (start us, length us, event | category | flops | bytes accessed | tf_op | source)
XLA Modules:
  0.0 35.1 jit_solution(4940502800251872966)
XLA Ops:
  0.0 1.4 %shard_map.73 = (f32[64,128]{1,0:T(8,128)S(1)}, f32[64,384]{1,0:T(8,128)S(1)}, bf16[128,256]{1,0:T(8,128)(2,1)S(1)}, bf16[128,256]{1,0:T(8,128)(2,1)S(1)}) custom-call(f32[3,128]{1,0:T(4,128)} %points_in.1, s32[1,128]{1,0:T(1,128)} %bitcast.1, s32[1,32]{1,0:T(1,128)} %skeleton_in.3, f32[1,2,128,128]{3,2,1,0:T(8,128)} %inverse_in.3, f32[1,2,32,256]{3,2,1,0:T(8,128)} %top_in.1), custom_call_target="tpu_custom_call" | custom-call | tf_op jit(solution)/shard_map/pallas_call | solution.py:295
  1.4 3.0 %collective-permute-start.5 = (f32[64,128]{1,0:T(8,128)S(1)}, f32[64,128]{1,0:T(8,128)S(1)}, u32[]{:S(2)}, u32[]{:S(2)}) collective-permute-start(f32[64,128]{1,0:T(8,128)S(1)} %get-tuple-element.28.u), channel_id=1, source_target_pairs={{0,1},{1,0},{2,3},{3,2},{4,5},{5,4},{6,7},{7,6},{8,9},{9,8},{10,11... | collective-permute-start | bytes 98312 | tf_op jit(solution)/shard_map/ppermute | solution.py:312
  4.4 3.5 %collective-permute-start.6 = (f32[64,128]{1,0:T(8,128)S(1)}, f32[64,128]{1,0:T(8,128)S(1)}, u32[]{:S(2)}, u32[]{:S(2)}) collective-permute-start(f32[64,128]{1,0:T(8,128)S(1)} %get-tuple-element.28.u), channel_id=1, source_target_pairs={{0,7},{1,2},{2,1},{3,4},{4,3},{5,6},{6,5},{7,0},{8,15},{9,10},{10,... | collective-permute-start | bytes 98312 | tf_op jit(solution)/shard_map/ppermute | solution.py:313
  8.0 1.0 %collective-permute-start.1 = (f32[64,384]{1,0:T(8,128)S(1)}, f32[64,384]{1,0:T(8,128)S(1)}, u32[]{:S(2)}, u32[]{:S(2)}) collective-permute-start(f32[64,384]{1,0:T(8,128)S(1)} %shard_map.74.refs_0_), channel_id=1, source_target_pairs={{0,2},{1,3},{2,0},{3,1},{4,6},{5,7},{6,4},{7,5},{8,10},{9,11},{10,... | collective-permute-start | bytes 294920 | tf_op jit(solution)/shard_map/ppermute | solution.py:307
  9.0 1.3 %collective-permute-start.2 = (f32[64,384]{1,0:T(8,128)S(1)}, f32[64,384]{1,0:T(8,128)S(1)}, u32[]{:S(2)}, u32[]{:S(2)}) collective-permute-start(f32[64,384]{1,0:T(8,128)S(1)} %shard_map.74.refs_0_), channel_id=1, source_target_pairs={{0,1},{1,0},{2,3},{3,2},{4,5},{5,4},{6,7},{7,6},{8,9},{9,8},{10,11... | collective-permute-start | bytes 294920 | tf_op jit(solution)/shard_map/ppermute | solution.py:307
  10.3 1.9 %shard_map.76 = (f32[128,320]{1,0:T(8,128)S(1)}, bf16[512,320]{1,0:T(8,128)(2,1)S(1)}, bf16[512,320]{1,0:T(8,128)(2,1)S(1)}) custom-call(bf16[128,256]{1,0:T(8,128)(2,1)S(1)} %get-tuple-element.25.high, bf16[128,256]{1,0:T(8,128)(2,1)S(1)} %get-tuple-element.26.low, s32[1,32]{1,0:T(1,128)} %skeleton_in.3, s32[1,8]{1,0:T(1,128)} %mask_in.1, ...), custom_call_target="tpu_custom_call" | custom-call | tf_op jit(solution)/shard_map/pallas_call | solution.py:295
  12.3 0.1 collective-permute-start.7
  12.4 1.6 %collective-permute-start.8 = (f32[3,64,128]{2,1,0:T(8,128)S(1)}, f32[3,64,128]{2,1,0:T(8,128)S(1)}, u32[]{:S(2)}, u32[]{:S(2)}) collective-permute-start(f32[3,64,128]{2,1,0:T(8,128)S(1)} %shard_map.77.middle), channel_id=1, source_target_pairs={{0,24},{8,16},{16,8},{24,0},{1,25},{9,17},{17,9},{25,1},{2,26},{10... | collective-permute-start | bytes 294920 | tf_op jit(solution)/shard_map/ppermute | solution.py:313
  14.0 0.5 %collective-permute-done.1.refs_2_.two = f32[64,384]{1,0:T(8,128)S(1)} collective-permute-done((f32[64,384]{1,0:T(8,128)S(1)}, f32[64,384]{1,0:T(8,128)S(1)}, u32[]{:S(2)}, u32[]{:S(2)}) %collective-permute-start.1) | collective-permute-done | bytes 98336 | tf_op jit(solution)/shard_map/ppermute | solution.py:307
  14.5 0.7 %collective-permute-start.13 = (f32[2,64,384]{2,1,0:T(8,128)S(1)}, f32[2,64,384]{2,1,0:T(8,128)S(1)}, u32[]{:S(2)}, u32[]{:S(2)}) collective-permute-start(f32[2,64,384]{2,1,0:T(8,128)S(1)} %shard_map.80), channel_id=1, source_target_pairs={{0,1},{1,0},{2,3},{3,2},{4,5},{5,4},{6,7},{7,6},{8,9},{9,8},{10,11... | collective-permute-start | bytes 589832 | tf_op jit(solution)/shard_map/ppermute | solution.py:307
  15.2 1.6 %collective-permute-start.3 = (f32[64,384]{1,0:T(8,128)S(1)}, f32[64,384]{1,0:T(8,128)S(1)}, u32[]{:S(2)}, u32[]{:S(2)}) collective-permute-start(f32[64,384]{1,0:T(8,128)S(1)} %collective-permute-done.refs_1_.four), channel_id=1, source_target_pairs={{0,2},{1,3},{2,0},{3,1},{4,6},{5,7},{6,4},{7,5},{8,10},{9,11},{10,... | collective-permute-start | bytes 294920 | tf_op jit(solution)/shard_map/ppermute | solution.py:307
  16.8 1.2 %collective-permute-start.4 = (f32[64,384]{1,0:T(8,128)S(1)}, f32[64,384]{1,0:T(8,128)S(1)}, u32[]{:S(2)}, u32[]{:S(2)}) collective-permute-start(f32[64,384]{1,0:T(8,128)S(1)} %collective-permute-done.refs_1_.four), channel_id=1, source_target_pairs={{0,3},{1,2},{2,1},{3,0},{4,7},{5,6},{6,5},{7,4},{8,11},{9,10},{10,... | collective-permute-start | bytes 294920 | tf_op jit(solution)/shard_map/ppermute | solution.py:307
  18.1 0.5 %shard_map.78 = (f32[4,40,128]{2,1,0:T(8,128)S(1)}, f32[4,40,128]{2,1,0:T(8,128)S(1)}) custom-call(f32[3,64,128]{2,1,0:T(8,128)S(1)} %collective-permute-done.7.even, f32[3,64,128]{2,1,0:T(8,128)S(1)} %shard_map.77.middle, f32[3,64,128]{2,1,0:T(8,128)S(1)} %collective-permute-done.8.odd, f32[128,320]{1,0:T(8,128)S(1)} %get-tuple-element.27.base, ...), custom_call_target="tpu_custom_call" | custom-call | flops 10000000000 | bytes 10000000 | tf_op jit(solution)/shard_map/pallas_call | solution.py:295
  18.6 0.7 %collective-permute-start.9 = (f32[4,40,128]{2,1,0:T(8,128)S(1)}, f32[4,40,128]{2,1,0:T(8,128)S(1)}, u32[]{:S(2)}, u32[]{:S(2)}) collective-permute-start(f32[4,40,128]{2,1,0:T(8,128)S(1)} %get-tuple-element.32), channel_id=1, source_target_pairs={{0,1},{1,0},{2,3},{3,2},{4,5},{5,4},{6,7},{7,6},{8,9},{9,8},{10,11... | collective-permute-start | bytes 245768 | tf_op jit(solution)/shard_map/ppermute | solution.py:307
  19.3 1.0 %collective-permute-done.3.refs_4_.refs_0_ = f32[64,384]{1,0:T(8,128)S(1)} collective-permute-done((f32[64,384]{1,0:T(8,128)S(1)}, f32[64,384]{1,0:T(8,128)S(1)}, u32[]{:S(2)}, u32[]{:S(2)}) %collective-permute-start.3) | collective-permute-done | bytes 98336 | tf_op jit(solution)/shard_map/ppermute | solution.py:307
  20.3 2.2 %collective-permute-done.4.refs_5_.refs_1_ = f32[64,384]{1,0:T(8,128)S(1)} collective-permute-done((f32[64,384]{1,0:T(8,128)S(1)}, f32[64,384]{1,0:T(8,128)S(1)}, u32[]{:S(2)}, u32[]{:S(2)}) %collective-permute-start.4) | collective-permute-done | bytes 98336 | tf_op jit(solution)/shard_map/ppermute | solution.py:307
  22.5 2.4 %collective-permute-done.9.came = f32[4,40,128]{2,1,0:T(8,128)S(1)} collective-permute-done((f32[4,40,128]{2,1,0:T(8,128)S(1)}, f32[4,40,128]{2,1,0:T(8,128)S(1)}, u32[]{:S(2)}, u32[]{:S(2)}) %collective-permute-start.9) | collective-permute-done | bytes 81952 | tf_op jit(solution)/shard_map/ppermute | solution.py:307
  24.8 1.9 %collective-permute-start.10 = (f32[2,40,128]{2,1,0:T(8,128)S(1)}, f32[2,40,128]{2,1,0:T(8,128)S(1)}, u32[]{:S(2)}, u32[]{:S(2)}) collective-permute-start(f32[2,40,128]{2,1,0:T(8,128)S(1)} %get-tuple-element.34), channel_id=1, source_target_pairs={{0,2},{1,3},{2,0},{3,1},{4,6},{5,7},{6,4},{7,5},{8,10},{9,11},{10,... | collective-permute-start | bytes 122888 | tf_op jit(solution)/shard_map/ppermute | solution.py:307
  26.7 1.1 %collective-permute-start.11 = (f32[2,40,128]{2,1,0:T(8,128)S(1)}, f32[2,40,128]{2,1,0:T(8,128)S(1)}, u32[]{:S(2)}, u32[]{:S(2)}) collective-permute-start(f32[2,40,128]{2,1,0:T(8,128)S(1)} %get-tuple-element.35), channel_id=1, source_target_pairs={{0,4},{1,5},{2,6},{3,7},{4,0},{5,1},{6,2},{7,3},{8,12},{9,13},{10,... | collective-permute-start | bytes 122888 | tf_op jit(solution)/shard_map/ppermute | solution.py:307
  27.9 1.4 %collective-permute-start.12 = (f32[2,40,128]{2,1,0:T(8,128)S(1)}, f32[2,40,128]{2,1,0:T(8,128)S(1)}, u32[]{:S(2)}, u32[]{:S(2)}) collective-permute-start(f32[2,40,128]{2,1,0:T(8,128)S(1)} %get-tuple-element.36), channel_id=1, source_target_pairs={{0,6},{1,7},{2,4},{3,5},{4,2},{5,3},{6,0},{7,1},{8,14},{9,15},{10,... | collective-permute-start | bytes 122888 | tf_op jit(solution)/shard_map/ppermute | solution.py:307
  29.3 0.1 shard_map.75
  29.4 2.3 %collective-permute-done.11.refs_2_ = f32[2,40,128]{2,1,0:T(8,128)S(1)} collective-permute-done((f32[2,40,128]{2,1,0:T(8,128)S(1)}, f32[2,40,128]{2,1,0:T(8,128)S(1)}, u32[]{:S(2)}, u32[]{:S(2)}) %collective-permute-start.11) | collective-permute-done | bytes 40992 | tf_op jit(solution)/shard_map/ppermute | solution.py:307
  31.7 1.9 %collective-permute-done.12.refs_3_ = f32[2,40,128]{2,1,0:T(8,128)S(1)} collective-permute-done((f32[2,40,128]{2,1,0:T(8,128)S(1)}, f32[2,40,128]{2,1,0:T(8,128)S(1)}, u32[]{:S(2)}, u32[]{:S(2)}) %collective-permute-start.12) | collective-permute-done | bytes 40992 | tf_op jit(solution)/shard_map/ppermute | solution.py:307
  33.7 1.4 %shard_map.81 = f32[2,16,1024]{2,1,0:T(8,128)} custom-call(bf16[384,512]{1,0:T(8,128)(2,1)S(1)} %get-tuple-element.22.top_high, bf16[384,512]{1,0:T(8,128)(2,1)S(1)} %get-tuple-element.23.top_low, bf16[6,192,256]{2,1,0:T(8,128)(2,1)S(1)} %get-tuple-element.24.prepared, f32[2,40,128]{2,1,0:T(8,128)S(1)} %get-tuple-element.33.refs_0_, ...), custom_call_target="tpu_custom_call" | custom-call | tf_op jit(solution)/shard_map/pallas_call | solution.py:295
  (13 shorter events, 0.1 us)
Async XLA Ops:
  1.4 10.9 %collective-permute-start.5 = (f32[64,128]{1,0:T(8,128)S(1)}, f32[64,128]{1,0:T(8,128)S(1)}, u32[]{:S(2)}, u32[]{:S(2)}) collective-permute-start(f32[64,128]{1,0:T(8,128)S(1)} %get-tuple-element.28.u), channel_id=1, source_target_pairs={{0,1},{1,0},{2,3},{3,2},{4,5},{5,4},{6,7},{7,6},{8,9},{9,8},{10,11... | collective-permute-start | bytes 98312 | tf_op jit(solution)/shard_map/ppermute | solution.py:312
  4.4 7.9 %collective-permute-start.6 = (f32[64,128]{1,0:T(8,128)S(1)}, f32[64,128]{1,0:T(8,128)S(1)}, u32[]{:S(2)}, u32[]{:S(2)}) collective-permute-start(f32[64,128]{1,0:T(8,128)S(1)} %get-tuple-element.28.u), channel_id=1, source_target_pairs={{0,7},{1,2},{2,1},{3,4},{4,3},{5,6},{6,5},{7,0},{8,15},{9,10},{10,... | collective-permute-start | bytes 98312 | tf_op jit(solution)/shard_map/ppermute | solution.py:313
  8.0 6.0 %collective-permute-start = (f32[64,384]{1,0:T(8,128)S(1)}, f32[64,384]{1,0:T(8,128)S(1)}, u32[]{:S(2)}, u32[]{:S(2)}) collective-permute-start(f32[64,384]{1,0:T(8,128)S(1)} %shard_map.74.refs_0_), channel_id=1, source_target_pairs={{0,4},{1,5},{2,6},{3,7},{4,0},{5,1},{6,2},{7,3},{8,12},{9,13},{10,... | collective-permute-start | bytes 294920 | tf_op jit(solution)/shard_map/ppermute | solution.py:307
  8.0 6.5 %collective-permute-start.1 = (f32[64,384]{1,0:T(8,128)S(1)}, f32[64,384]{1,0:T(8,128)S(1)}, u32[]{:S(2)}, u32[]{:S(2)}) collective-permute-start(f32[64,384]{1,0:T(8,128)S(1)} %shard_map.74.refs_0_), channel_id=1, source_target_pairs={{0,2},{1,3},{2,0},{3,1},{4,6},{5,7},{6,4},{7,5},{8,10},{9,11},{10,... | collective-permute-start | bytes 294920 | tf_op jit(solution)/shard_map/ppermute | solution.py:307
  9.0 5.5 %collective-permute-start.2 = (f32[64,384]{1,0:T(8,128)S(1)}, f32[64,384]{1,0:T(8,128)S(1)}, u32[]{:S(2)}, u32[]{:S(2)}) collective-permute-start(f32[64,384]{1,0:T(8,128)S(1)} %shard_map.74.refs_0_), channel_id=1, source_target_pairs={{0,1},{1,0},{2,3},{3,2},{4,5},{5,4},{6,7},{7,6},{8,9},{9,8},{10,11... | collective-permute-start | bytes 294920 | tf_op jit(solution)/shard_map/ppermute | solution.py:307
  12.3 5.8 %collective-permute-start.7 = (f32[3,64,128]{2,1,0:T(8,128)S(1)}, f32[3,64,128]{2,1,0:T(8,128)S(1)}, u32[]{:S(2)}, u32[]{:S(2)}) collective-permute-start(f32[3,64,128]{2,1,0:T(8,128)S(1)} %shard_map.77.middle), channel_id=1, source_target_pairs={{0,8},{8,0},{16,24},{24,16},{1,9},{9,1},{17,25},{25,17},{2,10},{10... | collective-permute-start | bytes 294920 | tf_op jit(solution)/shard_map/ppermute | solution.py:312
  12.4 5.7 %collective-permute-start.8 = (f32[3,64,128]{2,1,0:T(8,128)S(1)}, f32[3,64,128]{2,1,0:T(8,128)S(1)}, u32[]{:S(2)}, u32[]{:S(2)}) collective-permute-start(f32[3,64,128]{2,1,0:T(8,128)S(1)} %shard_map.77.middle), channel_id=1, source_target_pairs={{0,24},{8,16},{16,8},{24,0},{1,25},{9,17},{17,9},{25,1},{2,26},{10... | collective-permute-start | bytes 294920 | tf_op jit(solution)/shard_map/ppermute | solution.py:313
  14.5 19.1 %collective-permute-start.13 = (f32[2,64,384]{2,1,0:T(8,128)S(1)}, f32[2,64,384]{2,1,0:T(8,128)S(1)}, u32[]{:S(2)}, u32[]{:S(2)}) collective-permute-start(f32[2,64,384]{2,1,0:T(8,128)S(1)} %shard_map.80), channel_id=1, source_target_pairs={{0,1},{1,0},{2,3},{3,2},{4,5},{5,4},{6,7},{7,6},{8,9},{9,8},{10,11... | collective-permute-start | bytes 589832 | tf_op jit(solution)/shard_map/ppermute | solution.py:307
  15.2 5.1 %collective-permute-start.3 = (f32[64,384]{1,0:T(8,128)S(1)}, f32[64,384]{1,0:T(8,128)S(1)}, u32[]{:S(2)}, u32[]{:S(2)}) collective-permute-start(f32[64,384]{1,0:T(8,128)S(1)} %collective-permute-done.refs_1_.four), channel_id=1, source_target_pairs={{0,2},{1,3},{2,0},{3,1},{4,6},{5,7},{6,4},{7,5},{8,10},{9,11},{10,... | collective-permute-start | bytes 294920 | tf_op jit(solution)/shard_map/ppermute | solution.py:307
  16.8 5.6 %collective-permute-start.4 = (f32[64,384]{1,0:T(8,128)S(1)}, f32[64,384]{1,0:T(8,128)S(1)}, u32[]{:S(2)}, u32[]{:S(2)}) collective-permute-start(f32[64,384]{1,0:T(8,128)S(1)} %collective-permute-done.refs_1_.four), channel_id=1, source_target_pairs={{0,3},{1,2},{2,1},{3,0},{4,7},{5,6},{6,5},{7,4},{8,11},{9,10},{10,... | collective-permute-start | bytes 294920 | tf_op jit(solution)/shard_map/ppermute | solution.py:307
  18.6 6.2 %collective-permute-start.9 = (f32[4,40,128]{2,1,0:T(8,128)S(1)}, f32[4,40,128]{2,1,0:T(8,128)S(1)}, u32[]{:S(2)}, u32[]{:S(2)}) collective-permute-start(f32[4,40,128]{2,1,0:T(8,128)S(1)} %get-tuple-element.32), channel_id=1, source_target_pairs={{0,1},{1,0},{2,3},{3,2},{4,5},{5,4},{6,7},{7,6},{8,9},{9,8},{10,11... | collective-permute-start | bytes 245768 | tf_op jit(solution)/shard_map/ppermute | solution.py:307
  24.8 4.6 %collective-permute-start.10 = (f32[2,40,128]{2,1,0:T(8,128)S(1)}, f32[2,40,128]{2,1,0:T(8,128)S(1)}, u32[]{:S(2)}, u32[]{:S(2)}) collective-permute-start(f32[2,40,128]{2,1,0:T(8,128)S(1)} %get-tuple-element.34), channel_id=1, source_target_pairs={{0,2},{1,3},{2,0},{3,1},{4,6},{5,7},{6,4},{7,5},{8,10},{9,11},{10,... | collective-permute-start | bytes 122888 | tf_op jit(solution)/shard_map/ppermute | solution.py:307
  26.7 5.0 %collective-permute-start.11 = (f32[2,40,128]{2,1,0:T(8,128)S(1)}, f32[2,40,128]{2,1,0:T(8,128)S(1)}, u32[]{:S(2)}, u32[]{:S(2)}) collective-permute-start(f32[2,40,128]{2,1,0:T(8,128)S(1)} %get-tuple-element.35), channel_id=1, source_target_pairs={{0,4},{1,5},{2,6},{3,7},{4,0},{5,1},{6,2},{7,3},{8,12},{9,13},{10,... | collective-permute-start | bytes 122888 | tf_op jit(solution)/shard_map/ppermute | solution.py:307
  27.9 5.8 %collective-permute-start.12 = (f32[2,40,128]{2,1,0:T(8,128)S(1)}, f32[2,40,128]{2,1,0:T(8,128)S(1)}, u32[]{:S(2)}, u32[]{:S(2)}) collective-permute-start(f32[2,40,128]{2,1,0:T(8,128)S(1)} %get-tuple-element.36), channel_id=1, source_target_pairs={{0,6},{1,7},{2,4},{3,5},{4,2},{5,3},{6,0},{7,1},{8,14},{9,15},{10,... | collective-permute-start | bytes 122888 | tf_op jit(solution)/shard_map/ppermute | solution.py:307

commit v3 on v2

--- a/solution.py
+++ b/solution.py
@@ -169,9 +169,8 @@
     out[...] = static[...]
 
 
-def pack_kernel(one, two, four, out):
-    out[0] = two[...]
-    out[1] = four[...]
+def copy_kernel(value, first, second, out):
+    out[...] = value[...]
 
 
 def join_kernel(base, even, odd, u, row_out):
@@ -349,10 +348,11 @@
     waited = []
     if boxes == 8:
         four, two, one = [swapped(static, "box", k) for k in (4, 2, 1)]
-        (pair,) = call(pack_kernel, [((2,) + static.shape, F32)], one, two, four, hbm=(0,))
-        waited = [swapped(four, "box", 2), swapped(four, "box", 3)]
-        early, late = [static, four, two, one, *waited], [swapped(pair, "box", 1)]
-        offsets = (0, 4, 2, 1, 6, 7, 3, 5)
+        (four,) = call(copy_kernel, [(static.shape, F32)], four, two, one, hbm=(1, 2))
+        five, six, three = swapped(four, "box", 1), swapped(four, "box", 2), swapped(one, "box", 2)
+        waited = [five]
+        early, late = [static, four, two, one, five, six], [three, swapped(six, "box", 1)]
+        offsets = (0, 4, 2, 1, 5, 6, 3, 7)
     else:
         early, late = [static[None]], []
         offsets = [0]

time: 35.2 us -> 33 us (0.937)
  waiting for transfers between devices: 10.3 us -> 8.17 us
    ppermute x10 -> x11, waiting for transfers between devices: 10.3 us -> 8.16 us  [swapped(): lax.ppermute(value, axis, [(i, i ^ bit) for i in range(lax.axis_size(axis...]
    ppermute x10 -> x11, starting transfers between devices: 11 us -> 10.9 us  [swapped(): lax.ppermute(value, axis, [(i, i ^ bit) for i in range(lax.axis_size(axis...]
  transfers between devices with their start and end apart: 14 -> 15, of which waited for: 6 -> 5; matrix products, arithmetic and copies ran while one was open for 0% -> 0% of each run, Pallas kernels for 7% -> 8%
where the time goes in v3:
time: 33 us; the launch traced here: 32.8 us
  starting transfers between devices  19.2 us (58%)
  waiting for transfers between devices  8.17 us (25%)
  Pallas kernels  5.37 us (16%)
    ppermute x11, starting transfers between devices, swapped(): lax.ppermute(value, axis, [(i, i ^ bit) for i in range(lax.axis_size(axis...  10.9 us
    ppermute x11, waiting for transfers between devices, swapped(): lax.ppermute(value, axis, [(i, i ^ bit) for i in range(lax.axis_size(axis...  8.16 us
    pallas_call x9, Pallas kernels, call(): pl.pallas_call(kernel, out_shape=[jax.ShapeDtypeStruct(shape, dtype) for...  5.37 us
    ppermute x2, starting transfers between devices, beside(): lax.ppermute(value, axis, [(i, (i + 1) % count if i % 2 else (i - 1) % co...  5.14 us
    ppermute x2, starting transfers between devices, beside(): even = lax.ppermute(value, axis, [(i, i ^ 1) for i in range(count)])  3.1 us
  transfers between devices with their start and end apart: 15, of which 5 were waited for; matrix products, arithmetic and copies ran while one was open for 0% of the time, Pallas kernels for 8%

profile of v3, /device:TPU:0, one launch (start us, length us, event | category | flops | bytes accessed | tf_op | source)
XLA Modules:
  0.0 32.8 jit_solution(3706202024222653361)
XLA Ops:
  0.0 1.4 %shard_map.73 = (f32[64,128]{1,0:T(8,128)S(1)}, f32[64,384]{1,0:T(8,128)S(1)}, bf16[128,256]{1,0:T(8,128)(2,1)S(1)}, bf16[128,256]{1,0:T(8,128)(2,1)S(1)}) custom-call(f32[3,128]{1,0:T(4,128)} %points_in.1, s32[1,128]{1,0:T(1,128)} %bitcast.1, s32[1,32]{1,0:T(1,128)} %skeleton_in.3, f32[1,2,128,128]{3,2,1,0:T(8,128)} %inverse_in.3, f32[1,2,32,256]{3,2,1,0:T(8,128)} %top_in.1), custom_call_target="tpu_custom_call" | custom-call | tf_op jit(solution)/shard_map/pallas_call | solution.py:294
  1.4 3.0 %collective-permute-start.5 = (f32[64,128]{1,0:T(8,128)S(1)}, f32[64,128]{1,0:T(8,128)S(1)}, u32[]{:S(2)}, u32[]{:S(2)}) collective-permute-start(f32[64,128]{1,0:T(8,128)S(1)} %get-tuple-element.28.u), channel_id=1, source_target_pairs={{0,1},{1,0},{2,3},{3,2},{4,5},{5,4},{6,7},{7,6},{8,9},{9,8},{10,11... | collective-permute-start | bytes 98312 | tf_op jit(solution)/shard_map/ppermute | solution.py:311
  4.4 3.5 %collective-permute-start.6 = (f32[64,128]{1,0:T(8,128)S(1)}, f32[64,128]{1,0:T(8,128)S(1)}, u32[]{:S(2)}, u32[]{:S(2)}) collective-permute-start(f32[64,128]{1,0:T(8,128)S(1)} %get-tuple-element.28.u), channel_id=1, source_target_pairs={{0,7},{1,2},{2,1},{3,4},{4,3},{5,6},{6,5},{7,0},{8,15},{9,10},{10,... | collective-permute-start | bytes 98312 | tf_op jit(solution)/shard_map/ppermute | solution.py:312
  8.0 0.1 collective-permute-start.2
  8.0 1.1 %collective-permute-start.1 = (f32[64,384]{1,0:T(8,128)S(1)}, f32[64,384]{1,0:T(8,128)S(1)}, u32[]{:S(2)}, u32[]{:S(2)}) collective-permute-start(f32[64,384]{1,0:T(8,128)S(1)} %shard_map.74.refs_0_), channel_id=1, source_target_pairs={{0,2},{1,3},{2,0},{3,1},{4,6},{5,7},{6,4},{7,5},{8,10},{9,11},{10,... | collective-permute-start | bytes 294920 | tf_op jit(solution)/shard_map/ppermute | solution.py:306
  9.1 1.2 %collective-permute-start = (f32[64,384]{1,0:T(8,128)S(1)}, f32[64,384]{1,0:T(8,128)S(1)}, u32[]{:S(2)}, u32[]{:S(2)}) collective-permute-start(f32[64,384]{1,0:T(8,128)S(1)} %shard_map.74.refs_0_), channel_id=1, source_target_pairs={{0,4},{1,5},{2,6},{3,7},{4,0},{5,1},{6,2},{7,3},{8,12},{9,13},{10,... | collective-permute-start | bytes 294920 | tf_op jit(solution)/shard_map/ppermute | solution.py:306
  10.3 1.9 %shard_map.77 = (f32[128,320]{1,0:T(8,128)S(1)}, bf16[512,320]{1,0:T(8,128)(2,1)S(1)}, bf16[512,320]{1,0:T(8,128)(2,1)S(1)}) custom-call(bf16[128,256]{1,0:T(8,128)(2,1)S(1)} %get-tuple-element.25.high, bf16[128,256]{1,0:T(8,128)(2,1)S(1)} %get-tuple-element.26.low, s32[1,32]{1,0:T(1,128)} %skeleton_in.3, s32[1,8]{1,0:T(1,128)} %mask_in.1, ...), custom_call_target="tpu_custom_call" | custom-call | tf_op jit(solution)/shard_map/pallas_call | solution.py:294
  12.3 0.1 collective-permute-start.7
  12.4 1.6 %collective-permute-start.8 = (f32[3,64,128]{2,1,0:T(8,128)S(1)}, f32[3,64,128]{2,1,0:T(8,128)S(1)}, u32[]{:S(2)}, u32[]{:S(2)}) collective-permute-start(f32[3,64,128]{2,1,0:T(8,128)S(1)} %shard_map.78.middle), channel_id=1, source_target_pairs={{0,24},{8,16},{16,8},{24,0},{1,25},{9,17},{17,9},{25,1},{2,26},{10... | collective-permute-start | bytes 294920 | tf_op jit(solution)/shard_map/ppermute | solution.py:312
  14.0 1.7 %collective-permute-done.value = f32[64,384]{1,0:T(8,128)S(1)} collective-permute-done((f32[64,384]{1,0:T(8,128)S(1)}, f32[64,384]{1,0:T(8,128)S(1)}, u32[]{:S(2)}, u32[]{:S(2)}) %collective-permute-start) | collective-permute-done | bytes 98336 | tf_op jit(solution)/shard_map/ppermute | solution.py:306
  15.7 1.6 %collective-permute-start.3 = (f32[64,384]{1,0:T(8,128)S(1)}, f32[64,384]{1,0:T(8,128)S(1)}, u32[]{:S(2)}, u32[]{:S(2)}) collective-permute-start(f32[64,384]{1,0:T(8,128)S(1)} %shard_map.75.refs_1_), channel_id=1, source_target_pairs={{0,1},{1,0},{2,3},{3,2},{4,5},{5,4},{6,7},{7,6},{8,9},{9,8},{10,11... | collective-permute-start | bytes 294920 | tf_op jit(solution)/shard_map/ppermute | solution.py:306
  17.3 0.4 %collective-permute-start.4 = (f32[64,384]{1,0:T(8,128)S(1)}, f32[64,384]{1,0:T(8,128)S(1)}, u32[]{:S(2)}, u32[]{:S(2)}) collective-permute-start(f32[64,384]{1,0:T(8,128)S(1)} %shard_map.75.refs_1_), channel_id=1, source_target_pairs={{0,2},{1,3},{2,0},{3,1},{4,6},{5,7},{6,4},{7,5},{8,10},{9,11},{10,... | collective-permute-start | bytes 294920 | tf_op jit(solution)/shard_map/ppermute | solution.py:306
  17.8 0.5 %shard_map.79 = (f32[4,40,128]{2,1,0:T(8,128)S(1)}, f32[4,40,128]{2,1,0:T(8,128)S(1)}) custom-call(f32[3,64,128]{2,1,0:T(8,128)S(1)} %collective-permute-done.7.even, f32[3,64,128]{2,1,0:T(8,128)S(1)} %shard_map.78.middle, f32[3,64,128]{2,1,0:T(8,128)S(1)} %collective-permute-done.8.odd, f32[128,320]{1,0:T(8,128)S(1)} %get-tuple-element.27.base, ...), custom_call_target="tpu_custom_call" | custom-call | flops 10000000000 | bytes 10000000 | tf_op jit(solution)/shard_map/pallas_call | solution.py:294
  18.3 0.4 %collective-permute-start.9 = (f32[4,40,128]{2,1,0:T(8,128)S(1)}, f32[4,40,128]{2,1,0:T(8,128)S(1)}, u32[]{:S(2)}, u32[]{:S(2)}) collective-permute-start(f32[4,40,128]{2,1,0:T(8,128)S(1)} %get-tuple-element.32), channel_id=1, source_target_pairs={{0,1},{1,0},{2,3},{3,2},{4,5},{5,4},{6,7},{7,6},{8,9},{9,8},{10,11... | collective-permute-start | bytes 245768 | tf_op jit(solution)/shard_map/ppermute | solution.py:306
  18.7 1.6 %collective-permute-start.13 = (f32[64,384]{1,0:T(8,128)S(1)}, f32[64,384]{1,0:T(8,128)S(1)}, u32[]{:S(2)}, u32[]{:S(2)}) collective-permute-start(f32[64,384]{1,0:T(8,128)S(1)} %collective-permute-done.2.second.refs_3_), channel_id=1, source_target_pairs={{0,2},{1,3},{2,0},{3,1},{4,6},{5,7},{6,4},{7,5},{8,10},{9,11},{10,... | collective-permute-start | bytes 294920 | tf_op jit(solution)/shard_map/ppermute | solution.py:306
  20.3 2.6 %collective-permute-done.4.refs_5_ = f32[64,384]{1,0:T(8,128)S(1)} collective-permute-done((f32[64,384]{1,0:T(8,128)S(1)}, f32[64,384]{1,0:T(8,128)S(1)}, u32[]{:S(2)}, u32[]{:S(2)}) %collective-permute-start.4) | collective-permute-done | bytes 98336 | tf_op jit(solution)/shard_map/ppermute | solution.py:306
  22.9 0.5 %collective-permute-done.9.came = f32[4,40,128]{2,1,0:T(8,128)S(1)} collective-permute-done((f32[4,40,128]{2,1,0:T(8,128)S(1)}, f32[4,40,128]{2,1,0:T(8,128)S(1)}, u32[]{:S(2)}, u32[]{:S(2)}) %collective-permute-start.9) | collective-permute-done | bytes 81952 | tf_op jit(solution)/shard_map/ppermute | solution.py:306
  23.4 1.8 %collective-permute-start.10 = (f32[2,40,128]{2,1,0:T(8,128)S(1)}, f32[2,40,128]{2,1,0:T(8,128)S(1)}, u32[]{:S(2)}, u32[]{:S(2)}) collective-permute-start(f32[2,40,128]{2,1,0:T(8,128)S(1)} %get-tuple-element.34), channel_id=1, source_target_pairs={{0,2},{1,3},{2,0},{3,1},{4,6},{5,7},{6,4},{7,5},{8,10},{9,11},{10,... | collective-permute-start | bytes 122888 | tf_op jit(solution)/shard_map/ppermute | solution.py:306
  25.2 0.4 %collective-permute-start.11 = (f32[2,40,128]{2,1,0:T(8,128)S(1)}, f32[2,40,128]{2,1,0:T(8,128)S(1)}, u32[]{:S(2)}, u32[]{:S(2)}) collective-permute-start(f32[2,40,128]{2,1,0:T(8,128)S(1)} %get-tuple-element.35), channel_id=1, source_target_pairs={{0,4},{1,5},{2,6},{3,7},{4,0},{5,1},{6,2},{7,3},{8,12},{9,13},{10,... | collective-permute-start | bytes 122888 | tf_op jit(solution)/shard_map/ppermute | solution.py:306
  25.6 2.2 %collective-permute-start.12 = (f32[2,40,128]{2,1,0:T(8,128)S(1)}, f32[2,40,128]{2,1,0:T(8,128)S(1)}, u32[]{:S(2)}, u32[]{:S(2)}) collective-permute-start(f32[2,40,128]{2,1,0:T(8,128)S(1)} %get-tuple-element.36), channel_id=1, source_target_pairs={{0,6},{1,7},{2,4},{3,5},{4,2},{5,3},{6,0},{7,1},{8,14},{9,15},{10,... | collective-permute-start | bytes 122888 | tf_op jit(solution)/shard_map/ppermute | solution.py:306
  27.9 0.1 shard_map.76
  28.0 2.3 %collective-permute-done.11.refs_2_ = f32[2,40,128]{2,1,0:T(8,128)S(1)} collective-permute-done((f32[2,40,128]{2,1,0:T(8,128)S(1)}, f32[2,40,128]{2,1,0:T(8,128)S(1)}, u32[]{:S(2)}, u32[]{:S(2)}) %collective-permute-start.11) | collective-permute-done | bytes 40992 | tf_op jit(solution)/shard_map/ppermute | solution.py:306
  30.3 1.1 %collective-permute-done.12.refs_3_ = f32[2,40,128]{2,1,0:T(8,128)S(1)} collective-permute-done((f32[2,40,128]{2,1,0:T(8,128)S(1)}, f32[2,40,128]{2,1,0:T(8,128)S(1)}, u32[]{:S(2)}, u32[]{:S(2)}) %collective-permute-start.12) | collective-permute-done | bytes 40992 | tf_op jit(solution)/shard_map/ppermute | solution.py:306
  31.4 1.4 %shard_map.81 = f32[2,16,1024]{2,1,0:T(8,128)} custom-call(bf16[384,512]{1,0:T(8,128)(2,1)S(1)} %get-tuple-element.22.top_high, bf16[384,512]{1,0:T(8,128)(2,1)S(1)} %get-tuple-element.23.top_low, bf16[6,192,256]{2,1,0:T(8,128)(2,1)S(1)} %get-tuple-element.24.prepared, f32[2,40,128]{2,1,0:T(8,128)S(1)} %get-tuple-element.33.refs_0_, ...), custom_call_target="tpu_custom_call" | custom-call | tf_op jit(solution)/shard_map/pallas_call | solution.py:294
  (15 shorter events, 0.1 us)
Async XLA Ops:
  1.4 10.9 %collective-permute-start.5 = (f32[64,128]{1,0:T(8,128)S(1)}, f32[64,128]{1,0:T(8,128)S(1)}, u32[]{:S(2)}, u32[]{:S(2)}) collective-permute-start(f32[64,128]{1,0:T(8,128)S(1)} %get-tuple-element.28.u), channel_id=1, source_target_pairs={{0,1},{1,0},{2,3},{3,2},{4,5},{5,4},{6,7},{7,6},{8,9},{9,8},{10,11... | collective-permute-start | bytes 98312 | tf_op jit(solution)/shard_map/ppermute | solution.py:311
  4.4 7.9 %collective-permute-start.6 = (f32[64,128]{1,0:T(8,128)S(1)}, f32[64,128]{1,0:T(8,128)S(1)}, u32[]{:S(2)}, u32[]{:S(2)}) collective-permute-start(f32[64,128]{1,0:T(8,128)S(1)} %get-tuple-element.28.u), channel_id=1, source_target_pairs={{0,7},{1,2},{2,1},{3,4},{4,3},{5,6},{6,5},{7,0},{8,15},{9,10},{10,... | collective-permute-start | bytes 98312 | tf_op jit(solution)/shard_map/ppermute | solution.py:312
  8.0 6.0 %collective-permute-start.2 = (f32[64,384]{1,0:T(8,128)S(1)}, f32[64,384]{1,0:T(8,128)S(1)}, u32[]{:S(2)}, u32[]{:S(2)}) collective-permute-start(f32[64,384]{1,0:T(8,128)S(1)} %shard_map.74.refs_0_), channel_id=1, source_target_pairs={{0,1},{1,0},{2,3},{3,2},{4,5},{5,4},{6,7},{7,6},{8,9},{9,8},{10,11... | collective-permute-start | bytes 294920 | tf_op jit(solution)/shard_map/ppermute | solution.py:306
  8.0 6.0 %collective-permute-start.1 = (f32[64,384]{1,0:T(8,128)S(1)}, f32[64,384]{1,0:T(8,128)S(1)}, u32[]{:S(2)}, u32[]{:S(2)}) collective-permute-start(f32[64,384]{1,0:T(8,128)S(1)} %shard_map.74.refs_0_), channel_id=1, source_target_pairs={{0,2},{1,3},{2,0},{3,1},{4,6},{5,7},{6,4},{7,5},{8,10},{9,11},{10,... | collective-permute-start | bytes 294920 | tf_op jit(solution)/shard_map/ppermute | solution.py:306
  9.1 6.6 %collective-permute-start = (f32[64,384]{1,0:T(8,128)S(1)}, f32[64,384]{1,0:T(8,128)S(1)}, u32[]{:S(2)}, u32[]{:S(2)}) collective-permute-start(f32[64,384]{1,0:T(8,128)S(1)} %shard_map.74.refs_0_), channel_id=1, source_target_pairs={{0,4},{1,5},{2,6},{3,7},{4,0},{5,1},{6,2},{7,3},{8,12},{9,13},{10,... | collective-permute-start | bytes 294920 | tf_op jit(solution)/shard_map/ppermute | solution.py:306
  12.3 5.5 %collective-permute-start.7 = (f32[3,64,128]{2,1,0:T(8,128)S(1)}, f32[3,64,128]{2,1,0:T(8,128)S(1)}, u32[]{:S(2)}, u32[]{:S(2)}) collective-permute-start(f32[3,64,128]{2,1,0:T(8,128)S(1)} %shard_map.78.middle), channel_id=1, source_target_pairs={{0,8},{8,0},{16,24},{24,16},{1,9},{9,1},{17,25},{25,17},{2,10},{10... | collective-permute-start | bytes 294920 | tf_op jit(solution)/shard_map/ppermute | solution.py:311
  12.4 5.4 %collective-permute-start.8 = (f32[3,64,128]{2,1,0:T(8,128)S(1)}, f32[3,64,128]{2,1,0:T(8,128)S(1)}, u32[]{:S(2)}, u32[]{:S(2)}) collective-permute-start(f32[3,64,128]{2,1,0:T(8,128)S(1)} %shard_map.78.middle), channel_id=1, source_target_pairs={{0,24},{8,16},{16,8},{24,0},{1,25},{9,17},{17,9},{25,1},{2,26},{10... | collective-permute-start | bytes 294920 | tf_op jit(solution)/shard_map/ppermute | solution.py:312
  15.7 7.3 %collective-permute-start.3 = (f32[64,384]{1,0:T(8,128)S(1)}, f32[64,384]{1,0:T(8,128)S(1)}, u32[]{:S(2)}, u32[]{:S(2)}) collective-permute-start(f32[64,384]{1,0:T(8,128)S(1)} %shard_map.75.refs_1_), channel_id=1, source_target_pairs={{0,1},{1,0},{2,3},{3,2},{4,5},{5,4},{6,7},{7,6},{8,9},{9,8},{10,11... | collective-permute-start | bytes 294920 | tf_op jit(solution)/shard_map/ppermute | solution.py:306
  17.3 5.6 %collective-permute-start.4 = (f32[64,384]{1,0:T(8,128)S(1)}, f32[64,384]{1,0:T(8,128)S(1)}, u32[]{:S(2)}, u32[]{:S(2)}) collective-permute-start(f32[64,384]{1,0:T(8,128)S(1)} %shard_map.75.refs_1_), channel_id=1, source_target_pairs={{0,2},{1,3},{2,0},{3,1},{4,6},{5,7},{6,4},{7,5},{8,10},{9,11},{10,... | collective-permute-start | bytes 294920 | tf_op jit(solution)/shard_map/ppermute | solution.py:306
  18.3 5.1 %collective-permute-start.9 = (f32[4,40,128]{2,1,0:T(8,128)S(1)}, f32[4,40,128]{2,1,0:T(8,128)S(1)}, u32[]{:S(2)}, u32[]{:S(2)}) collective-permute-start(f32[4,40,128]{2,1,0:T(8,128)S(1)} %get-tuple-element.32), channel_id=1, source_target_pairs={{0,1},{1,0},{2,3},{3,2},{4,5},{5,4},{6,7},{7,6},{8,9},{9,8},{10,11... | collective-permute-start | bytes 245768 | tf_op jit(solution)/shard_map/ppermute | solution.py:306
  18.7 9.3 %collective-permute-start.13 = (f32[64,384]{1,0:T(8,128)S(1)}, f32[64,384]{1,0:T(8,128)S(1)}, u32[]{:S(2)}, u32[]{:S(2)}) collective-permute-start(f32[64,384]{1,0:T(8,128)S(1)} %collective-permute-done.2.second.refs_3_), channel_id=1, source_target_pairs={{0,2},{1,3},{2,0},{3,1},{4,6},{5,7},{6,4},{7,5},{8,10},{9,11},{10,... | collective-permute-start | bytes 294920 | tf_op jit(solution)/shard_map/ppermute | solution.py:306
  22.9 8.5 %collective-permute-start.14 = (f32[64,384]{1,0:T(8,128)S(1)}, f32[64,384]{1,0:T(8,128)S(1)}, u32[]{:S(2)}, u32[]{:S(2)}) collective-permute-start(f32[64,384]{1,0:T(8,128)S(1)} %collective-permute-done.4.refs_5_), channel_id=1, source_target_pairs={{0,1},{1,0},{2,3},{3,2},{4,5},{5,4},{6,7},{7,6},{8,9},{9,8},{10,11... | collective-permute-start | bytes 294920 | tf_op jit(solution)/shard_map/ppermute | solution.py:306
  23.4 4.6 %collective-permute-start.10 = (f32[2,40,128]{2,1,0:T(8,128)S(1)}, f32[2,40,128]{2,1,0:T(8,128)S(1)}, u32[]{:S(2)}, u32[]{:S(2)}) collective-permute-start(f32[2,40,128]{2,1,0:T(8,128)S(1)} %get-tuple-element.34), channel_id=1, source_target_pairs={{0,2},{1,3},{2,0},{3,1},{4,6},{5,7},{6,4},{7,5},{8,10},{9,11},{10,... | collective-permute-start | bytes 122888 | tf_op jit(solution)/shard_map/ppermute | solution.py:306
  25.2 5.1 %collective-permute-start.11 = (f32[2,40,128]{2,1,0:T(8,128)S(1)}, f32[2,40,128]{2,1,0:T(8,128)S(1)}, u32[]{:S(2)}, u32[]{:S(2)}) collective-permute-start(f32[2,40,128]{2,1,0:T(8,128)S(1)} %get-tuple-element.35), channel_id=1, source_target_pairs={{0,4},{1,5},{2,6},{3,7},{4,0},{5,1},{6,2},{7,3},{8,12},{9,13},{10,... | collective-permute-start | bytes 122888 | tf_op jit(solution)/shard_map/ppermute | solution.py:306
  25.6 5.8 %collective-permute-start.12 = (f32[2,40,128]{2,1,0:T(8,128)S(1)}, f32[2,40,128]{2,1,0:T(8,128)S(1)}, u32[]{:S(2)}, u32[]{:S(2)}) collective-permute-start(f32[2,40,128]{2,1,0:T(8,128)S(1)} %get-tuple-element.36), channel_id=1, source_target_pairs={{0,6},{1,7},{2,4},{3,5},{4,2},{5,3},{6,0},{7,1},{8,14},{9,15},{10,... | collective-permute-start | bytes 122888 | tf_op jit(solution)/shard_map/ppermute | solution.py:306

commit v4 on v3

--- a/solution.py
+++ b/solution.py
@@ -169,11 +169,12 @@
     out[...] = static[...]
 
 
-def copy_kernel(value, first, second, out):
+def copy_kernel(value, *refs):
+    out = refs[-1]
     out[...] = value[...]
 
 
-def join_kernel(base, even, odd, u, row_out):
+def join_kernel(even, odd, u, row_out):
     first = lax.axis_index("box") % 2 == 0
     row_out[0] = jnp.where(first, odd[...], even[...])
     row_out[1] = u[...]
@@ -340,21 +341,19 @@
             ((2 * sides * rank, 2 * width + 2 * rank), BF16),
         ],
         high, low, skeleton, near_mask, box_inverse_parts, near_coupling,
-        copied=range(2, 6),
+        copied=range(2, 6), cost=COST,
     )
     even, odd = beside(u, "box")
-    (row,) = call(join_kernel, [((3,) + u.shape, F32)], base, even, odd, u, hbm=(0,))
+    (row,) = call(join_kernel, [((3,) + u.shape, F32)], even, odd, u)
     (static,) = call(hold_kernel, [(static.shape, F32)], static, cost=COST)
-    waited = []
     if boxes == 8:
         four, two, one = [swapped(static, "box", k) for k in (4, 2, 1)]
-        (four,) = call(copy_kernel, [(static.shape, F32)], four, two, one, hbm=(1, 2))
+        (four,) = call(copy_kernel, [(static.shape, F32)], four, two, one, base, hbm=(1, 2, 3))
         five, six, three = swapped(four, "box", 1), swapped(four, "box", 2), swapped(one, "box", 2)
-        waited = [five]
-        early, late = [static, four, two, one, five, six], [three, swapped(six, "box", 1)]
+        early, late, waited = [static, four, two, one, five, six], [three], [five]
         offsets = (0, 4, 2, 1, 5, 6, 3, 7)
     else:
-        early, late = [static[None]], []
+        early, late, waited = [static[None]], [], []
         offsets = [0]
         step = boxes // 2
         while step > 0:
@@ -373,6 +372,9 @@
         functools.partial(forward_kernel, boxes // 2), [((2, length, width), F32)] * (boxes // 2),
         keep, swapped(send, "box", 1), *waited, hbm=range(2, 2 + len(waited)),
     )
+    if late:
+        (six,) = call(copy_kernel, [(six.shape, F32)], six, pieces[0], hbm=(1,))
+        late.append(swapped(six, "box", 1))
     pieces = [pieces[0]] + [swapped(pieces[k], "box", 2 * k) for k in range(1, boxes // 2)]
     ready = 6 if late else boxes
     top = ((ready * 2 * rank, 2 * depth), BF16)

time: 33 us -> 33.8 us (1.024)
  starting transfers between devices: 19.2 us -> 19.8 us
    ppermute x2, waiting for transfers between devices: 0.01 us -> 0.79 us  [beside(): lax.ppermute(value, axis, [(i, (i + 1) % count if i % 2 else (i - 1) % co...]
    ppermute x11, waiting for transfers between devices: 8.16 us -> 7.54 us  [swapped(): lax.ppermute(value, axis, [(i, i ^ bit) for i in range(lax.axis_size(axis...]
    ppermute x11, starting transfers between devices: 10.9 us -> 11.6 us  [swapped(): lax.ppermute(value, axis, [(i, i ^ bit) for i in range(lax.axis_size(axis...]
    pallas_call x9 -> x10, Pallas kernels: 5.37 us -> 5.37 us  [call(): pl.pallas_call(kernel, out_shape=[jax.ShapeDtypeStruct(shape, dtype) for...]
  transfers between devices with their start and end apart: 15 -> 15, of which waited for: 5 -> 6; matrix products, arithmetic and copies ran while one was open for 0% -> 0% of each run, Pallas kernels for 8% -> 8%
where the time goes in v4:
time: 33.8 us; the launch traced here: 33.6 us
  starting transfers between devices  19.8 us (59%)
  waiting for transfers between devices  8.34 us (25%)
  Pallas kernels  5.37 us (16%)
    ppermute x11, starting transfers between devices, swapped(): lax.ppermute(value, axis, [(i, i ^ bit) for i in range(lax.axis_size(axis...  11.6 us
    ppermute x11, waiting for transfers between devices, swapped(): lax.ppermute(value, axis, [(i, i ^ bit) for i in range(lax.axis_size(axis...  7.54 us
    pallas_call x10, Pallas kernels, call(): pl.pallas_call(kernel, out_shape=[jax.ShapeDtypeStruct(shape, dtype) for...  5.37 us
    ppermute x2, starting transfers between devices, beside(): lax.ppermute(value, axis, [(i, (i + 1) % count if i % 2 else (i - 1) % co...  5.15 us
    ppermute x2, starting transfers between devices, beside(): even = lax.ppermute(value, axis, [(i, i ^ 1) for i in range(count)])  3.1 us
    ppermute x2, waiting for transfers between devices, beside(): lax.ppermute(value, axis, [(i, (i + 1) % count if i % 2 else (i - 1) % co...  0.79 us
  transfers between devices with their start and end apart: 15, of which 6 were waited for; matrix products, arithmetic and copies ran while one was open for 0% of the time, Pallas kernels for 8%

profile of v4, /device:TPU:0, one launch (start us, length us, event | category | flops | bytes accessed | tf_op | source)
XLA Modules:
  0.0 33.6 jit_solution(2240687412727988686)
XLA Ops:
  0.0 1.4 %shard_map.73 = (f32[64,128]{1,0:T(8,128)S(1)}, f32[64,384]{1,0:T(8,128)S(1)}, bf16[128,256]{1,0:T(8,128)(2,1)S(1)}, bf16[128,256]{1,0:T(8,128)(2,1)S(1)}) custom-call(f32[3,128]{1,0:T(4,128)} %points_in.1, s32[1,128]{1,0:T(1,128)} %bitcast.1, s32[1,32]{1,0:T(1,128)} %skeleton_in.3, f32[1,2,128,128]{3,2,1,0:T(8,128)} %inverse_in.3, f32[1,2,32,256]{3,2,1,0:T(8,128)} %top_in.1), custom_call_target="tpu_custom_call" | custom-call | tf_op jit(solution)/shard_map/pallas_call | solution.py:295
  1.4 3.0 %collective-permute-start.5 = (f32[64,128]{1,0:T(8,128)S(1)}, f32[64,128]{1,0:T(8,128)S(1)}, u32[]{:S(2)}, u32[]{:S(2)}) collective-permute-start(f32[64,128]{1,0:T(8,128)S(1)} %get-tuple-element.28.u), channel_id=1, source_target_pairs={{0,1},{1,0},{2,3},{3,2},{4,5},{5,4},{6,7},{7,6},{8,9},{9,8},{10,11... | collective-permute-start | bytes 98312 | tf_op jit(solution)/shard_map/ppermute | solution.py:312
  4.4 3.5 %collective-permute-start.6 = (f32[64,128]{1,0:T(8,128)S(1)}, f32[64,128]{1,0:T(8,128)S(1)}, u32[]{:S(2)}, u32[]{:S(2)}) collective-permute-start(f32[64,128]{1,0:T(8,128)S(1)} %get-tuple-element.28.u), channel_id=1, source_target_pairs={{0,7},{1,2},{2,1},{3,4},{4,3},{5,6},{6,5},{7,0},{8,15},{9,10},{10,... | collective-permute-start | bytes 98312 | tf_op jit(solution)/shard_map/ppermute | solution.py:313
  8.0 1.1 %collective-permute-start.1 = (f32[64,384]{1,0:T(8,128)S(1)}, f32[64,384]{1,0:T(8,128)S(1)}, u32[]{:S(2)}, u32[]{:S(2)}) collective-permute-start(f32[64,384]{1,0:T(8,128)S(1)} %shard_map.74.refs_0_), channel_id=1, source_target_pairs={{0,2},{1,3},{2,0},{3,1},{4,6},{5,7},{6,4},{7,5},{8,10},{9,11},{10,... | collective-permute-start | bytes 294920 | tf_op jit(solution)/shard_map/ppermute | solution.py:307
  9.1 1.2 %collective-permute-start = (f32[64,384]{1,0:T(8,128)S(1)}, f32[64,384]{1,0:T(8,128)S(1)}, u32[]{:S(2)}, u32[]{:S(2)}) collective-permute-start(f32[64,384]{1,0:T(8,128)S(1)} %shard_map.74.refs_0_), channel_id=1, source_target_pairs={{0,4},{1,5},{2,6},{3,7},{4,0},{5,1},{6,2},{7,3},{8,12},{9,13},{10,... | collective-permute-start | bytes 294920 | tf_op jit(solution)/shard_map/ppermute | solution.py:307
  10.3 0.8 %collective-permute-done.6.odd = f32[64,128]{1,0:T(8,128)S(1)} collective-permute-done((f32[64,128]{1,0:T(8,128)S(1)}, f32[64,128]{1,0:T(8,128)S(1)}, u32[]{:S(2)}, u32[]{:S(2)}) %collective-permute-start.6) | collective-permute-done | bytes 32800 | tf_op jit(solution)/shard_map/ppermute | solution.py:313
  11.2 1.6 %collective-permute-start.8 = (f32[3,64,128]{2,1,0:T(8,128)S(1)}, f32[3,64,128]{2,1,0:T(8,128)S(1)}, u32[]{:S(2)}, u32[]{:S(2)}) collective-permute-start(f32[3,64,128]{2,1,0:T(8,128)S(1)} %shard_map.78.middle), channel_id=1, source_target_pairs={{0,24},{8,16},{16,8},{24,0},{1,25},{9,17},{17,9},{25,1},{2,26},{10... | collective-permute-start | bytes 294920 | tf_op jit(solution)/shard_map/ppermute | solution.py:313
  12.8 1.9 %shard_map.75 = (f32[128,320]{1,0:T(8,128)S(1)}, bf16[512,320]{1,0:T(8,128)(2,1)S(1)}, bf16[512,320]{1,0:T(8,128)(2,1)S(1)}) custom-call(bf16[128,256]{1,0:T(8,128)(2,1)S(1)} %get-tuple-element.22.high, bf16[128,256]{1,0:T(8,128)(2,1)S(1)} %get-tuple-element.23.low, s32[1,32]{1,0:T(1,128)} %skeleton_in.3, s32[1,8]{1,0:T(1,128)} %mask_in.1, ...), custom_call_target="tpu_custom_call" | custom-call | flops 10000000000 | bytes 10000000 | tf_op jit(solution)/shard_map/pallas_call | solution.py:295
  14.8 0.9 %collective-permute-done.value = f32[64,384]{1,0:T(8,128)S(1)} collective-permute-done((f32[64,384]{1,0:T(8,128)S(1)}, f32[64,384]{1,0:T(8,128)S(1)}, u32[]{:S(2)}, u32[]{:S(2)}) %collective-permute-start) | collective-permute-done | bytes 98336 | tf_op jit(solution)/shard_map/ppermute | solution.py:307
  15.7 1.6 %collective-permute-start.3 = (f32[64,384]{1,0:T(8,128)S(1)}, f32[64,384]{1,0:T(8,128)S(1)}, u32[]{:S(2)}, u32[]{:S(2)}) collective-permute-start(f32[64,384]{1,0:T(8,128)S(1)} %shard_map.76.refs_1_), channel_id=1, source_target_pairs={{0,1},{1,0},{2,3},{3,2},{4,5},{5,4},{6,7},{7,6},{8,9},{9,8},{10,11... | collective-permute-start | bytes 294920 | tf_op jit(solution)/shard_map/ppermute | solution.py:307
  17.3 0.4 %collective-permute-start.4 = (f32[64,384]{1,0:T(8,128)S(1)}, f32[64,384]{1,0:T(8,128)S(1)}, u32[]{:S(2)}, u32[]{:S(2)}) collective-permute-start(f32[64,384]{1,0:T(8,128)S(1)} %shard_map.76.refs_1_), channel_id=1, source_target_pairs={{0,2},{1,3},{2,0},{3,1},{4,6},{5,7},{6,4},{7,5},{8,10},{9,11},{10,... | collective-permute-start | bytes 294920 | tf_op jit(solution)/shard_map/ppermute | solution.py:307
  17.8 0.5 %shard_map.79 = (f32[4,40,128]{2,1,0:T(8,128)S(1)}, f32[4,40,128]{2,1,0:T(8,128)S(1)}) custom-call(f32[3,64,128]{2,1,0:T(8,128)S(1)} %collective-permute-done.7.even, f32[3,64,128]{2,1,0:T(8,128)S(1)} %shard_map.78.middle, f32[3,64,128]{2,1,0:T(8,128)S(1)} %collective-permute-done.8.odd, f32[128,320]{1,0:T(8,128)S(1)} %get-tuple-element.24.refs_2_.base, ...), custom_call_target="tpu_custom_call" | custom-call | flops 10000000000 | bytes 10000000 | tf_op jit(solution)/shard_map/pallas_call | solution.py:295
  18.3 0.4 %collective-permute-start.9 = (f32[4,40,128]{2,1,0:T(8,128)S(1)}, f32[4,40,128]{2,1,0:T(8,128)S(1)}, u32[]{:S(2)}, u32[]{:S(2)}) collective-permute-start(f32[4,40,128]{2,1,0:T(8,128)S(1)} %get-tuple-element.32), channel_id=1, source_target_pairs={{0,1},{1,0},{2,3},{3,2},{4,5},{5,4},{6,7},{7,6},{8,9},{9,8},{10,11... | collective-permute-start | bytes 245768 | tf_op jit(solution)/shard_map/ppermute | solution.py:307
  18.7 1.6 %collective-permute-start.13 = (f32[64,384]{1,0:T(8,128)S(1)}, f32[64,384]{1,0:T(8,128)S(1)}, u32[]{:S(2)}, u32[]{:S(2)}) collective-permute-start(f32[64,384]{1,0:T(8,128)S(1)} %collective-permute-done.2.refs_1_.refs_3_), channel_id=1, source_target_pairs={{0,2},{1,3},{2,0},{3,1},{4,6},{5,7},{6,4},{7,5},{8,10},{9,11},{10,... | collective-permute-start | bytes 294920 | tf_op jit(solution)/shard_map/ppermute | solution.py:307
  20.3 0.9 %collective-permute-done.3.refs_4_.refs_0_ = f32[64,384]{1,0:T(8,128)S(1)} collective-permute-done((f32[64,384]{1,0:T(8,128)S(1)}, f32[64,384]{1,0:T(8,128)S(1)}, u32[]{:S(2)}, u32[]{:S(2)}) %collective-permute-start.3) | collective-permute-done | bytes 98336 | tf_op jit(solution)/shard_map/ppermute | solution.py:307
  21.2 1.5 %collective-permute-done.9.came = f32[4,40,128]{2,1,0:T(8,128)S(1)} collective-permute-done((f32[4,40,128]{2,1,0:T(8,128)S(1)}, f32[4,40,128]{2,1,0:T(8,128)S(1)}, u32[]{:S(2)}, u32[]{:S(2)}) %collective-permute-start.9) | collective-permute-done | bytes 81952 | tf_op jit(solution)/shard_map/ppermute | solution.py:307
  22.8 0.7 %collective-permute-start.14 = (f32[64,384]{1,0:T(8,128)S(1)}, f32[64,384]{1,0:T(8,128)S(1)}, u32[]{:S(2)}, u32[]{:S(2)}) collective-permute-start(f32[64,384]{1,0:T(8,128)S(1)} %shard_map.81), channel_id=1, source_target_pairs={{0,1},{1,0},{2,3},{3,2},{4,5},{5,4},{6,7},{7,6},{8,9},{9,8},{10,11... | collective-permute-start | bytes 294920 | tf_op jit(solution)/shard_map/ppermute | solution.py:307
  23.5 1.4 %collective-permute-start.10 = (f32[2,40,128]{2,1,0:T(8,128)S(1)}, f32[2,40,128]{2,1,0:T(8,128)S(1)}, u32[]{:S(2)}, u32[]{:S(2)}) collective-permute-start(f32[2,40,128]{2,1,0:T(8,128)S(1)} %get-tuple-element.34), channel_id=1, source_target_pairs={{0,2},{1,3},{2,0},{3,1},{4,6},{5,7},{6,4},{7,5},{8,10},{9,11},{10,... | collective-permute-start | bytes 122888 | tf_op jit(solution)/shard_map/ppermute | solution.py:307
  24.9 1.5 %collective-permute-start.11 = (f32[2,40,128]{2,1,0:T(8,128)S(1)}, f32[2,40,128]{2,1,0:T(8,128)S(1)}, u32[]{:S(2)}, u32[]{:S(2)}) collective-permute-start(f32[2,40,128]{2,1,0:T(8,128)S(1)} %get-tuple-element.35), channel_id=1, source_target_pairs={{0,4},{1,5},{2,6},{3,7},{4,0},{5,1},{6,2},{7,3},{8,12},{9,13},{10,... | collective-permute-start | bytes 122888 | tf_op jit(solution)/shard_map/ppermute | solution.py:307
  26.4 1.4 %collective-permute-start.12 = (f32[2,40,128]{2,1,0:T(8,128)S(1)}, f32[2,40,128]{2,1,0:T(8,128)S(1)}, u32[]{:S(2)}, u32[]{:S(2)}) collective-permute-start(f32[2,40,128]{2,1,0:T(8,128)S(1)} %get-tuple-element.36), channel_id=1, source_target_pairs={{0,6},{1,7},{2,4},{3,5},{4,2},{5,3},{6,0},{7,1},{8,14},{9,15},{10,... | collective-permute-start | bytes 122888 | tf_op jit(solution)/shard_map/ppermute | solution.py:307
  27.9 0.1 shard_map.77
  28.0 2.7 %collective-permute-done.11.refs_2_ = f32[2,40,128]{2,1,0:T(8,128)S(1)} collective-permute-done((f32[2,40,128]{2,1,0:T(8,128)S(1)}, f32[2,40,128]{2,1,0:T(8,128)S(1)}, u32[]{:S(2)}, u32[]{:S(2)}) %collective-permute-start.11) | collective-permute-done | bytes 40992 | tf_op jit(solution)/shard_map/ppermute | solution.py:307
  30.7 1.6 %collective-permute-done.12.refs_3_ = f32[2,40,128]{2,1,0:T(8,128)S(1)} collective-permute-done((f32[2,40,128]{2,1,0:T(8,128)S(1)}, f32[2,40,128]{2,1,0:T(8,128)S(1)}, u32[]{:S(2)}, u32[]{:S(2)}) %collective-permute-start.12) | collective-permute-done | bytes 40992 | tf_op jit(solution)/shard_map/ppermute | solution.py:307
  32.2 1.4 %shard_map.82 = f32[2,16,1024]{2,1,0:T(8,128)} custom-call(bf16[384,512]{1,0:T(8,128)(2,1)S(1)} %get-tuple-element.25.top_high, bf16[384,512]{1,0:T(8,128)(2,1)S(1)} %get-tuple-element.26.top_low, bf16[6,192,256]{2,1,0:T(8,128)(2,1)S(1)} %get-tuple-element.27.prepared, f32[2,40,128]{2,1,0:T(8,128)S(1)} %get-tuple-element.33.refs_0_, ...), custom_call_target="tpu_custom_call" | custom-call | tf_op jit(solution)/shard_map/pallas_call | solution.py:295
  (16 shorter events, 0.2 us)
Async XLA Ops:
  1.4 9.0 %collective-permute-start.5 = (f32[64,128]{1,0:T(8,128)S(1)}, f32[64,128]{1,0:T(8,128)S(1)}, u32[]{:S(2)}, u32[]{:S(2)}) collective-permute-start(f32[64,128]{1,0:T(8,128)S(1)} %get-tuple-element.28.u), channel_id=1, source_target_pairs={{0,1},{1,0},{2,3},{3,2},{4,5},{5,4},{6,7},{7,6},{8,9},{9,8},{10,11... | collective-permute-start | bytes 98312 | tf_op jit(solution)/shard_map/ppermute | solution.py:312
  4.4 6.7 %collective-permute-start.6 = (f32[64,128]{1,0:T(8,128)S(1)}, f32[64,128]{1,0:T(8,128)S(1)}, u32[]{:S(2)}, u32[]{:S(2)}) collective-permute-start(f32[64,128]{1,0:T(8,128)S(1)} %get-tuple-element.28.u), channel_id=1, source_target_pairs={{0,7},{1,2},{2,1},{3,4},{4,3},{5,6},{6,5},{7,0},{8,15},{9,10},{10,... | collective-permute-start | bytes 98312 | tf_op jit(solution)/shard_map/ppermute | solution.py:313
  8.0 6.8 %collective-permute-start.2 = (f32[64,384]{1,0:T(8,128)S(1)}, f32[64,384]{1,0:T(8,128)S(1)}, u32[]{:S(2)}, u32[]{:S(2)}) collective-permute-start(f32[64,384]{1,0:T(8,128)S(1)} %shard_map.74.refs_0_), channel_id=1, source_target_pairs={{0,1},{1,0},{2,3},{3,2},{4,5},{5,4},{6,7},{7,6},{8,9},{9,8},{10,11... | collective-permute-start | bytes 294920 | tf_op jit(solution)/shard_map/ppermute | solution.py:307
  8.0 6.7 %collective-permute-start.1 = (f32[64,384]{1,0:T(8,128)S(1)}, f32[64,384]{1,0:T(8,128)S(1)}, u32[]{:S(2)}, u32[]{:S(2)}) collective-permute-start(f32[64,384]{1,0:T(8,128)S(1)} %shard_map.74.refs_0_), channel_id=1, source_target_pairs={{0,2},{1,3},{2,0},{3,1},{4,6},{5,7},{6,4},{7,5},{8,10},{9,11},{10,... | collective-permute-start | bytes 294920 | tf_op jit(solution)/shard_map/ppermute | solution.py:307
  9.1 6.6 %collective-permute-start = (f32[64,384]{1,0:T(8,128)S(1)}, f32[64,384]{1,0:T(8,128)S(1)}, u32[]{:S(2)}, u32[]{:S(2)}) collective-permute-start(f32[64,384]{1,0:T(8,128)S(1)} %shard_map.74.refs_0_), channel_id=1, source_target_pairs={{0,4},{1,5},{2,6},{3,7},{4,0},{5,1},{6,2},{7,3},{8,12},{9,13},{10,... | collective-permute-start | bytes 294920 | tf_op jit(solution)/shard_map/ppermute | solution.py:307
  11.1 6.6 %collective-permute-start.7 = (f32[3,64,128]{2,1,0:T(8,128)S(1)}, f32[3,64,128]{2,1,0:T(8,128)S(1)}, u32[]{:S(2)}, u32[]{:S(2)}) collective-permute-start(f32[3,64,128]{2,1,0:T(8,128)S(1)} %shard_map.78.middle), channel_id=1, source_target_pairs={{0,8},{8,0},{16,24},{24,16},{1,9},{9,1},{17,25},{25,17},{2,10},{10... | collective-permute-start | bytes 294920 | tf_op jit(solution)/shard_map/ppermute | solution.py:312
  11.2 6.6 %collective-permute-start.8 = (f32[3,64,128]{2,1,0:T(8,128)S(1)}, f32[3,64,128]{2,1,0:T(8,128)S(1)}, u32[]{:S(2)}, u32[]{:S(2)}) collective-permute-start(f32[3,64,128]{2,1,0:T(8,128)S(1)} %shard_map.78.middle), channel_id=1, source_target_pairs={{0,24},{8,16},{16,8},{24,0},{1,25},{9,17},{17,9},{25,1},{2,26},{10... | collective-permute-start | bytes 294920 | tf_op jit(solution)/shard_map/ppermute | solution.py:313
  15.7 5.6 %collective-permute-start.3 = (f32[64,384]{1,0:T(8,128)S(1)}, f32[64,384]{1,0:T(8,128)S(1)}, u32[]{:S(2)}, u32[]{:S(2)}) collective-permute-start(f32[64,384]{1,0:T(8,128)S(1)} %shard_map.76.refs_1_), channel_id=1, source_target_pairs={{0,1},{1,0},{2,3},{3,2},{4,5},{5,4},{6,7},{7,6},{8,9},{9,8},{10,11... | collective-permute-start | bytes 294920 | tf_op jit(solution)/shard_map/ppermute | solution.py:307
  17.3 5.4 %collective-permute-start.4 = (f32[64,384]{1,0:T(8,128)S(1)}, f32[64,384]{1,0:T(8,128)S(1)}, u32[]{:S(2)}, u32[]{:S(2)}) collective-permute-start(f32[64,384]{1,0:T(8,128)S(1)} %shard_map.76.refs_1_), channel_id=1, source_target_pairs={{0,2},{1,3},{2,0},{3,1},{4,6},{5,7},{6,4},{7,5},{8,10},{9,11},{10,... | collective-permute-start | bytes 294920 | tf_op jit(solution)/shard_map/ppermute | solution.py:307
  18.3 4.5 %collective-permute-start.9 = (f32[4,40,128]{2,1,0:T(8,128)S(1)}, f32[4,40,128]{2,1,0:T(8,128)S(1)}, u32[]{:S(2)}, u32[]{:S(2)}) collective-permute-start(f32[4,40,128]{2,1,0:T(8,128)S(1)} %get-tuple-element.32), channel_id=1, source_target_pairs={{0,1},{1,0},{2,3},{3,2},{4,5},{5,4},{6,7},{7,6},{8,9},{9,8},{10,11... | collective-permute-start | bytes 245768 | tf_op jit(solution)/shard_map/ppermute | solution.py:307
  18.7 9.3 %collective-permute-start.13 = (f32[64,384]{1,0:T(8,128)S(1)}, f32[64,384]{1,0:T(8,128)S(1)}, u32[]{:S(2)}, u32[]{:S(2)}) collective-permute-start(f32[64,384]{1,0:T(8,128)S(1)} %collective-permute-done.2.refs_1_.refs_3_), channel_id=1, source_target_pairs={{0,2},{1,3},{2,0},{3,1},{4,6},{5,7},{6,4},{7,5},{8,10},{9,11},{10,... | collective-permute-start | bytes 294920 | tf_op jit(solution)/shard_map/ppermute | solution.py:307
  22.8 9.4 %collective-permute-start.14 = (f32[64,384]{1,0:T(8,128)S(1)}, f32[64,384]{1,0:T(8,128)S(1)}, u32[]{:S(2)}, u32[]{:S(2)}) collective-permute-start(f32[64,384]{1,0:T(8,128)S(1)} %shard_map.81), channel_id=1, source_target_pairs={{0,1},{1,0},{2,3},{3,2},{4,5},{5,4},{6,7},{7,6},{8,9},{9,8},{10,11... | collective-permute-start | bytes 294920 | tf_op jit(solution)/shard_map/ppermute | solution.py:307
  23.5 4.5 %collective-permute-start.10 = (f32[2,40,128]{2,1,0:T(8,128)S(1)}, f32[2,40,128]{2,1,0:T(8,128)S(1)}, u32[]{:S(2)}, u32[]{:S(2)}) collective-permute-start(f32[2,40,128]{2,1,0:T(8,128)S(1)} %get-tuple-element.34), channel_id=1, source_target_pairs={{0,2},{1,3},{2,0},{3,1},{4,6},{5,7},{6,4},{7,5},{8,10},{9,11},{10,... | collective-permute-start | bytes 122888 | tf_op jit(solution)/shard_map/ppermute | solution.py:307
  24.9 5.8 %collective-permute-start.11 = (f32[2,40,128]{2,1,0:T(8,128)S(1)}, f32[2,40,128]{2,1,0:T(8,128)S(1)}, u32[]{:S(2)}, u32[]{:S(2)}) collective-permute-start(f32[2,40,128]{2,1,0:T(8,128)S(1)} %get-tuple-element.35), channel_id=1, source_target_pairs={{0,4},{1,5},{2,6},{3,7},{4,0},{5,1},{6,2},{7,3},{8,12},{9,13},{10,... | collective-permute-start | bytes 122888 | tf_op jit(solution)/shard_map/ppermute | solution.py:307
  26.4 5.8 %collective-permute-start.12 = (f32[2,40,128]{2,1,0:T(8,128)S(1)}, f32[2,40,128]{2,1,0:T(8,128)S(1)}, u32[]{:S(2)}, u32[]{:S(2)}) collective-permute-start(f32[2,40,128]{2,1,0:T(8,128)S(1)} %get-tuple-element.36), channel_id=1, source_target_pairs={{0,6},{1,7},{2,4},{3,5},{4,2},{5,3},{6,0},{7,1},{8,14},{9,15},{10,... | collective-permute-start | bytes 122888 | tf_op jit(solution)/shard_map/ppermute | solution.py:307

commit v5 on v4

--- a/solution.py
+++ b/solution.py
@@ -73,12 +73,13 @@
     return cat([cat([re, im], 1), cat([-im, re], 1)], 0)
 
 
-def field_kernel(points_in, angles_in, skeleton_in, inverse_in, top_in, u_out, static_out, high_out, low_out,
-                 points, angles, skeleton, inverse, top, sems):
+def field_kernel(points_in, angles_in, skeleton_in, inverse_in, top_in, mask_in, u_out, static_out, high_out, low_out,
+                 picker_out, mask_out, points, angles, skeleton, inverse, top, mask, sems):
     copies = [
         pltpu.make_async_copy(source, target, sems.at[k])
         for k, (source, target) in enumerate((
             (angles_in, angles), (points_in, points), (skeleton_in, skeleton), (inverse_in, inverse), (top_in, top),
+            (mask_in, mask),
         ))
     ]
     for copy in copies:
@@ -107,6 +108,9 @@
     low_out[...] = field[1]
     copies[2].wait()
     picker = one_hot(skeleton[...], width)
+    picker_out[...] = picker
+    copies[5].wait()
+    mask_out[...] = mask[...].astype(F32)
     copies[3].wait()
     parts = split(cat([inverse[0, 0], inverse[0, 1]], 1))
     rows = dot(picker, cat(parts, 1), TN)
@@ -123,18 +127,7 @@
         static_out[at, depth:] = whole[:, part * width : (part + 1) * width]
 
 
-def coupling_kernel(high, low, skeleton_in, mask_in, inverse_in, coupling_in, base_out, high_out, low_out,
-                    skeleton, mask, inverse, coupling, sems):
-    copies = [
-        pltpu.make_async_copy(source, target, sems.at[k])
-        for k, (source, target) in enumerate((
-            (skeleton_in, skeleton), (mask_in, mask), (inverse_in, inverse), (coupling_in, coupling),
-        ))
-    ]
-    for copy in copies:
-        copy.start()
-    for copy in copies:
-        copy.wait()
+def coupling_kernel(high, low, picker_in, mask, inverse, coupling, base_out, high_out, low_out):
     width = inverse.shape[2]
     sides = coupling.shape[1]
     rank = coupling.shape[3]
@@ -144,14 +137,14 @@
     im = split(inverse[0, 1])
     row_matrix = (rows_form(re[0], im[0]), rows_form(re[1], im[1]))
     column_matrix = (columns_form(re[0], im[0]), columns_form(re[1], im[1]))
-    picker = one_hot(skeleton[...], width)
+    picker = picker_in[...]
     zero = jnp.zeros_like(picker)
     picker2 = cat([cat([picker, zero], 1), cat([zero, picker], 1)], 0)
     z = split(dot3(field, row_matrix, NT))
     u = dot(z[0], picker2) + dot(z[1], picker2)
     near = []
     for side in range(sides):
-        weight = mask[:, side : side + 1].astype(F32)
+        weight = mask[:, side : side + 1]
         near.append(cat([coupling[0, side, 0] * weight, coupling[0, side, 1] * weight], 1))
     near = split(cat(near, 0))
     base_out[:, : 2 * width] = dot3(z, column_matrix)
@@ -229,36 +222,28 @@
 
 def prepare_kernel(*refs):
     top_high, top_low, local_out = refs[-3:]
-    depth = top_high.shape[1] // 2
+    depth = top_high.shape[0] // 2
     rank = local_out.shape[1] // 6
     for k, block in enumerate(blocks_of(refs[:-3])):
         at = slice(2 * k * rank, 2 * (k + 1) * rank)
-        parts = split(block)
-        for part, top_out in zip(parts, (top_high, top_low)):
-            top_out[at] = rows_form(part[:rank, :depth], part[rank:, :depth])
-        local_out[k] = stacked_form(parts, rank, depth)
-
-
-def top_kernel(offsets, messages, top_high, top_low, prepared, *refs):
-    pieces = refs[:messages]
-    late = [split(block) for block in blocks_of(refs[messages:-2])]
+        re = block[:rank, :depth]
+        im = block[rank:, :depth]
+        high, low = split(cat([cat([re, im], 0).T, cat([-im, re], 0).T], 0))
+        top_high[:, at] = high
+        top_low[:, at] = low
+        local_out[k] = stacked_form(split(block), rank, depth)
+
+
+def top_kernel(offsets, top_high, top_low, local, *refs):
+    pieces = refs[:-2][::-1]
     out, packed = refs[-2:]
-    boxes = 2 * messages
+    boxes = 2 * len(pieces)
     width = pieces[0].shape[2]
     share = out.shape[1]
     half = share // 2
-    ready = prepared.shape[0]
-    rank = prepared.shape[1] // 6
+    rank = local.shape[1] // 6
     rows = 2 * rank
-    depth = boxes * rank
     me = lax.axis_index("box")
-    top = [(top_high[...], top_low[...])]
-    local = [prepared[k] for k in range(ready)]
-    if late:
-        top.append([
-            cat([rows_form(v[k][:rank, :depth], v[k][rank:, :depth]) for v in late], 0) for k in range(2)
-        ])
-        local += [stacked_form(v, rank, depth) for v in late]
     for k in range(boxes):
         packed[me ^ k] = pieces[k // 2][k % 2, 2 * share : 2 * share + half]
     t_re = []
@@ -268,12 +253,8 @@
         t_re.append(t[:, :rank])
         t_im.append(t[:, rank:])
     t = split(cat(t_re + t_im, 1))
-    t_both = cat(t, 0)
-    y = []
-    for high, low in top:
-        first = dot(t_both, high, NT)
-        y.append(first[:share] + (first[share:] + dot(t[0], low, NT)))
-    y = split(cat(y, 1))
+    first = dot(cat(t, 0), top_high[...])
+    y = split(first[:share] + (first[share:] + dot(t[0], top_low[...])))
     for k in range(boxes):
         at = slice(k * rows, (k + 1) * rows)
         x = dot(cat([y[0][:, at], y[1][:, at], y[0][:, at]], 1), local[k])
@@ -322,16 +303,18 @@
     sides = near_mask.shape[1]
     depth = top_inverse.shape[3]
     share = count // boxes
-    u, static, high, low = call(
+    u, static, high, low, picker, mask = call(
         field_kernel,
         [
             ((2 * rank, count), F32),
             ((2 * rank, depth + width), F32),
             ((count, 2 * width), BF16),
             ((count, 2 * width), BF16),
+            ((width, rank), BF16),
+            (near_mask.shape, F32),
         ],
         surface_points, angle_ids.reshape(1, count), skeleton, box_inverse_parts, top_inverse,
-        copied=range(5),
+        near_mask, copied=range(6),
     )
     base, matrix_high, matrix_low = call(
         coupling_kernel,
@@ -340,8 +323,7 @@
             ((2 * sides * rank, 2 * width + 2 * rank), BF16),
             ((2 * sides * rank, 2 * width + 2 * rank), BF16),
         ],
-        high, low, skeleton, near_mask, box_inverse_parts, near_coupling,
-        copied=range(2, 6), cost=COST,
+        high, low, picker, mask, box_inverse_parts, near_coupling, cost=COST,
     )
     even, odd = beside(u, "box")
     (row,) = call(join_kernel, [((3,) + u.shape, F32)], even, odd, u)
@@ -375,14 +357,12 @@
     if late:
         (six,) = call(copy_kernel, [(six.shape, F32)], six, pieces[0], hbm=(1,))
         late.append(swapped(six, "box", 1))
-    pieces = [pieces[0]] + [swapped(pieces[k], "box", 2 * k) for k in range(1, boxes // 2)]
-    ready = 6 if late else boxes
-    top = ((ready * 2 * rank, 2 * depth), BF16)
-    local = ((ready, 6 * rank, 2 * width), BF16)
-    prepared = call(prepare_kernel, [top, top, local], *early)
+    pieces = [swapped(pieces[k], "box", 2 * k) for k in reversed(range(1, boxes // 2))] + [pieces[0]]
+    top = ((2 * depth, 2 * depth), BF16)
+    local = ((boxes, 6 * rank, 2 * width), BF16)
+    prepared = call(prepare_kernel, [top, top, local], *early, *late)
     (out,) = call(
-        functools.partial(top_kernel, offsets, len(pieces)), [((2, share, boxes * width), F32)],
-        *prepared, *pieces, *late,
+        functools.partial(top_kernel, offsets), [((2, share, boxes * width), F32)], *prepared, *pieces,
         extra=[pltpu.VMEM((boxes, share // 2, width), F32)],
     )
     return out

time: 33.8 us -> 32.7 us (0.967)
  waiting for transfers between devices: 8.34 us -> 5.69 us
  starting transfers between devices: 19.8 us -> 21.5 us
    ppermute x11, waiting for transfers between devices: 7.54 us -> 4.9 us  [swapped(): lax.ppermute(value, axis, [(i, i ^ bit) for i in range(lax.axis_size(axis...]
    ppermute x11, starting transfers between devices: 11.6 us -> 13.8 us  [swapped(): lax.ppermute(value, axis, [(i, i ^ bit) for i in range(lax.axis_size(axis...]
    ppermute x2, starting transfers between devices: 3.1 us -> 1.6 us  [beside(): even = lax.ppermute(value, axis, [(i, i ^ 1) for i in range(count)])]
    ppermute x2, starting transfers between devices: 5.15 us -> 6.14 us  [beside(): lax.ppermute(value, axis, [(i, (i + 1) % count if i % 2 else (i - 1) % co...]
    ppermute x2, waiting for transfers between devices: 0.79 us -> 0.01 us  [beside(): lax.ppermute(value, axis, [(i, (i + 1) % count if i % 2 else (i - 1) % co...]
    ppermute x2, waiting for transfers between devices: 0.01 us -> 0.78 us  [beside(): even = lax.ppermute(value, axis, [(i, i ^ 1) for i in range(count)])]
  transfers between devices with their start and end apart: 15 -> 15, of which waited for: 6 -> 7; matrix products, arithmetic and copies ran while one was open for 0% -> 0% of each run, Pallas kernels for 8% -> 8%
where the time goes in v5:
time: 32.7 us; the launch traced here: 32.6 us
  starting transfers between devices  21.5 us (66%)
  waiting for transfers between devices  5.69 us (17%)
  Pallas kernels  5.27 us (16%)
    ppermute x11, starting transfers between devices, swapped(): lax.ppermute(value, axis, [(i, i ^ bit) for i in range(lax.axis_size(axis...  13.8 us
    ppermute x2, starting transfers between devices, beside(): lax.ppermute(value, axis, [(i, (i + 1) % count if i % 2 else (i - 1) % co...  6.14 us
    pallas_call x10, Pallas kernels, call(): pl.pallas_call(kernel, out_shape=[jax.ShapeDtypeStruct(shape, dtype) for...  5.27 us
    ppermute x11, waiting for transfers between devices, swapped(): lax.ppermute(value, axis, [(i, i ^ bit) for i in range(lax.axis_size(axis...  4.9 us
    ppermute x2, starting transfers between devices, beside(): even = lax.ppermute(value, axis, [(i, i ^ 1) for i in range(count)])  1.6 us
    ppermute x2, waiting for transfers between devices, beside(): even = lax.ppermute(value, axis, [(i, i ^ 1) for i in range(count)])  0.78 us
  transfers between devices with their start and end apart: 15, of which 7 were waited for; matrix products, arithmetic and copies ran while one was open for 0% of the time, Pallas kernels for 8%

profile of v5, /device:TPU:0, one launch (start us, length us, event | category | flops | bytes accessed | tf_op | source)
XLA Modules:
  0.0 32.6 jit_solution(5693525054073525939)
XLA Ops:
  0.0 1.4 %shard_map.73 = (f32[64,128]{1,0:T(8,128)S(1)}, f32[64,384]{1,0:T(8,128)S(1)}, bf16[128,256]{1,0:T(8,128)(2,1)S(1)}, bf16[128,256]{1,0:T(8,128)(2,1)S(1)}, bf16[...) custom-call(f32[3,128]{1,0:T(4,128)} %points_in.1, s32[1,128]{1,0:T(1,128)} %bitcast.1, s32[1,32]{1,0:T(1,128)} %skeleton_in.1, ...), custom_call_target="tpu_custom_call" | custom-call | tf_op jit(solution)/shard_map/pallas_call | solution.py:276
  1.4 6.1 %collective-permute-start.7 = (f32[64,128]{1,0:T(8,128)S(1)}, f32[64,128]{1,0:T(8,128)S(1)}, u32[]{:S(2)}, u32[]{:S(2)}) collective-permute-start(f32[64,128]{1,0:T(8,128)S(1)} %get-tuple-element.29.u), channel_id=1, source_target_pairs={{0,7},{1,2},{2,1},{3,4},{4,3},{5,6},{6,5},{7,0},{8,15},{9,10},{10,... | collective-permute-start | bytes 98312 | tf_op jit(solution)/shard_map/ppermute | solution.py:294
  7.5 2.1 %collective-permute-start.2 = (f32[64,384]{1,0:T(8,128)S(1)}, f32[64,384]{1,0:T(8,128)S(1)}, u32[]{:S(2)}, u32[]{:S(2)}) collective-permute-start(f32[64,384]{1,0:T(8,128)S(1)} %shard_map.74.refs_0_), channel_id=1, source_target_pairs={{0,1},{1,0},{2,3},{3,2},{4,5},{5,4},{6,7},{7,6},{8,9},{9,8},{10,11... | collective-permute-start | bytes 294920 | tf_op jit(solution)/shard_map/ppermute | solution.py:288
  9.6 1.0 %collective-permute-start = (f32[64,384]{1,0:T(8,128)S(1)}, f32[64,384]{1,0:T(8,128)S(1)}, u32[]{:S(2)}, u32[]{:S(2)}) collective-permute-start(f32[64,384]{1,0:T(8,128)S(1)} %shard_map.74.refs_0_), channel_id=1, source_target_pairs={{0,4},{1,5},{2,6},{3,7},{4,0},{5,1},{6,2},{7,3},{8,12},{9,13},{10,... | collective-permute-start | bytes 294920 | tf_op jit(solution)/shard_map/ppermute | solution.py:288
  10.6 0.8 %collective-permute-done.6.even = f32[64,128]{1,0:T(8,128)S(1)} collective-permute-done((f32[64,128]{1,0:T(8,128)S(1)}, f32[64,128]{1,0:T(8,128)S(1)}, u32[]{:S(2)}, u32[]{:S(2)}) %collective-permute-start.6) | collective-permute-done | bytes 32800 | tf_op jit(solution)/shard_map/ppermute | solution.py:293
  11.5 1.6 %collective-permute-start.8 = (f32[3,64,128]{2,1,0:T(8,128)S(1)}, f32[3,64,128]{2,1,0:T(8,128)S(1)}, u32[]{:S(2)}, u32[]{:S(2)}) collective-permute-start(f32[3,64,128]{2,1,0:T(8,128)S(1)} %shard_map.77.middle), channel_id=1, source_target_pairs={{0,8},{8,0},{16,24},{24,16},{1,9},{9,1},{17,25},{25,17},{2,10},{10... | collective-permute-start | bytes 294920 | tf_op jit(solution)/shard_map/ppermute | solution.py:293
  13.1 0.9 %shard_map.75 = (f32[128,320]{1,0:T(8,128)S(1)}, bf16[512,320]{1,0:T(8,128)(2,1)S(1)}, bf16[512,320]{1,0:T(8,128)(2,1)S(1)}) custom-call(bf16[128,256]{1,0:T(8,128)(2,1)S(1)} %get-tuple-element.24.high, bf16[128,256]{1,0:T(8,128)(2,1)S(1)} %get-tuple-element.25.low, bf16[128,32]{1,0:T(8,128)(2,1)S(1)} %get-tuple-element.26.picker_in, ...), custom_call_target="tpu_custom_call" | custom-call | flops 10000000000 | bytes 10000000 | tf_op jit(solution)/shard_map/pallas_call | solution.py:276
  13.9 0.4 %collective-permute-done.1.refs_0_.refs_2_ = f32[64,384]{1,0:T(8,128)S(1)} collective-permute-done((f32[64,384]{1,0:T(8,128)S(1)}, f32[64,384]{1,0:T(8,128)S(1)}, u32[]{:S(2)}, u32[]{:S(2)}) %collective-permute-start.1) | collective-permute-done | bytes 98336 | tf_op jit(solution)/shard_map/ppermute | solution.py:288
  14.4 1.0 %collective-permute-done.value = f32[64,384]{1,0:T(8,128)S(1)} collective-permute-done((f32[64,384]{1,0:T(8,128)S(1)}, f32[64,384]{1,0:T(8,128)S(1)}, u32[]{:S(2)}, u32[]{:S(2)}) %collective-permute-start) | collective-permute-done | bytes 98336 | tf_op jit(solution)/shard_map/ppermute | solution.py:288
  15.4 1.8 %collective-permute-start.4 = (f32[64,384]{1,0:T(8,128)S(1)}, f32[64,384]{1,0:T(8,128)S(1)}, u32[]{:S(2)}, u32[]{:S(2)}) collective-permute-start(f32[64,384]{1,0:T(8,128)S(1)} %shard_map.76.refs_1_), channel_id=1, source_target_pairs={{0,2},{1,3},{2,0},{3,1},{4,6},{5,7},{6,4},{7,5},{8,10},{9,11},{10,... | collective-permute-start | bytes 294920 | tf_op jit(solution)/shard_map/ppermute | solution.py:288
  17.2 0.3 collective-permute-start.3
  17.5 0.5 %shard_map.78 = (f32[4,40,128]{2,1,0:T(8,128)S(1)}, f32[4,40,128]{2,1,0:T(8,128)S(1)}) custom-call(f32[3,64,128]{2,1,0:T(8,128)S(1)} %collective-permute-done.8.even, f32[3,64,128]{2,1,0:T(8,128)S(1)} %shard_map.77.middle, f32[3,64,128]{2,1,0:T(8,128)S(1)} %collective-permute-done.9.odd, f32[128,320]{1,0:T(8,128)S(1)} %get-tuple-element.28.refs_2_.base, ...), custom_call_target="tpu_custom_call" | custom-call | flops 10000000000 | bytes 10000000 | tf_op jit(solution)/shard_map/pallas_call | solution.py:276
  18.0 1.7 %collective-permute-start.10 = (f32[4,40,128]{2,1,0:T(8,128)S(1)}, f32[4,40,128]{2,1,0:T(8,128)S(1)}, u32[]{:S(2)}, u32[]{:S(2)}) collective-permute-start(f32[4,40,128]{2,1,0:T(8,128)S(1)} %get-tuple-element.33), channel_id=1, source_target_pairs={{0,1},{1,0},{2,3},{3,2},{4,5},{5,4},{6,7},{7,6},{8,9},{9,8},{10,11... | collective-permute-start | bytes 245768 | tf_op jit(solution)/shard_map/ppermute | solution.py:288
  19.8 0.3 collective-permute-start.5
  20.0 1.8 %collective-permute-done.3.refs_0_.refs_4_ = f32[64,384]{1,0:T(8,128)S(1)} collective-permute-done((f32[64,384]{1,0:T(8,128)S(1)}, f32[64,384]{1,0:T(8,128)S(1)}, u32[]{:S(2)}, u32[]{:S(2)}) %collective-permute-start.3) | collective-permute-done | bytes 98336 | tf_op jit(solution)/shard_map/ppermute | solution.py:288
  21.8 0.9 %collective-permute-done.10.came = f32[4,40,128]{2,1,0:T(8,128)S(1)} collective-permute-done((f32[4,40,128]{2,1,0:T(8,128)S(1)}, f32[4,40,128]{2,1,0:T(8,128)S(1)}, u32[]{:S(2)}, u32[]{:S(2)}) %collective-permute-start.10) | collective-permute-done | bytes 81952 | tf_op jit(solution)/shard_map/ppermute | solution.py:288
  22.7 2.1 %collective-permute-start.11 = (f32[64,384]{1,0:T(8,128)S(1)}, f32[64,384]{1,0:T(8,128)S(1)}, u32[]{:S(2)}, u32[]{:S(2)}) collective-permute-start(f32[64,384]{1,0:T(8,128)S(1)} %shard_map.80), channel_id=1, source_target_pairs={{0,1},{1,0},{2,3},{3,2},{4,5},{5,4},{6,7},{7,6},{8,9},{9,8},{10,11... | collective-permute-start | bytes 294920 | tf_op jit(solution)/shard_map/ppermute | solution.py:288
  24.9 0.4 %collective-permute-start.12 = (f32[2,40,128]{2,1,0:T(8,128)S(1)}, f32[2,40,128]{2,1,0:T(8,128)S(1)}, u32[]{:S(2)}, u32[]{:S(2)}) collective-permute-start(f32[2,40,128]{2,1,0:T(8,128)S(1)} %get-tuple-element.38), channel_id=1, source_target_pairs={{0,6},{1,7},{2,4},{3,5},{4,2},{5,3},{6,0},{7,1},{8,14},{9,15},{10,... | collective-permute-start | bytes 122888 | tf_op jit(solution)/shard_map/ppermute | solution.py:288
  25.3 0.9 %collective-permute-start.13 = (f32[2,40,128]{2,1,0:T(8,128)S(1)}, f32[2,40,128]{2,1,0:T(8,128)S(1)}, u32[]{:S(2)}, u32[]{:S(2)}) collective-permute-start(f32[2,40,128]{2,1,0:T(8,128)S(1)} %get-tuple-element.39), channel_id=1, source_target_pairs={{0,4},{1,5},{2,6},{3,7},{4,0},{5,1},{6,2},{7,3},{8,12},{9,13},{10,... | collective-permute-start | bytes 122888 | tf_op jit(solution)/shard_map/ppermute | solution.py:288
  26.2 3.0 %collective-permute-start.14 = (f32[2,40,128]{2,1,0:T(8,128)S(1)}, f32[2,40,128]{2,1,0:T(8,128)S(1)}, u32[]{:S(2)}, u32[]{:S(2)}) collective-permute-start(f32[2,40,128]{2,1,0:T(8,128)S(1)} %get-tuple-element.40), channel_id=1, source_target_pairs={{0,2},{1,3},{2,0},{3,1},{4,6},{5,7},{6,4},{7,5},{8,10},{9,11},{10,... | collective-permute-start | bytes 122888 | tf_op jit(solution)/shard_map/ppermute | solution.py:288
  29.3 1.2 %shard_map.81 = (bf16[512,512]{1,0:T(8,128)(2,1)S(1)}, bf16[512,512]{1,0:T(8,128)(2,1)S(1)}, bf16[8,192,256]{2,1,0:T(8,128)(2,1)S(1)}) custom-call(f32[64,384]{1,0:T(8,128)S(1)} %shard_map.74.refs_0_, f32[64,384]{1,0:T(8,128)S(1)} %shard_map.76.refs_1_, f32[64,384]{1,0:T(8,128)S(1)} %collective-permute-done.1.refs_0_.refs_2_, ...), custom_call_target="tpu_custom_call" | custom-call | tf_op jit(solution)/shard_map/pallas_call | solution.py:276
  30.4 0.2 collective-permute-done.12.refs_0_
  30.7 0.6 %collective-permute-done.14.refs_2_ = f32[2,40,128]{2,1,0:T(8,128)S(1)} collective-permute-done((f32[2,40,128]{2,1,0:T(8,128)S(1)}, f32[2,40,128]{2,1,0:T(8,128)S(1)}, u32[]{:S(2)}, u32[]{:S(2)}) %collective-permute-start.14) | collective-permute-done | bytes 40992 | tf_op jit(solution)/shard_map/ppermute | solution.py:288
  31.2 1.3 %shard_map.82 = f32[2,16,1024]{2,1,0:T(8,128)} custom-call(bf16[512,512]{1,0:T(8,128)(2,1)S(1)} %get-tuple-element.35.top_high, bf16[512,512]{1,0:T(8,128)(2,1)S(1)} %get-tuple-element.36.top_low, bf16[8,192,256]{2,1,0:T(8,128)(2,1)S(1)} %get-tuple-element.37.local, f32[2,40,128]{2,1,0:T(8,128)S(1)} %collective-permute-done.12.refs_0_, ...), custom_call_target="tpu_custom_call" | custom-call | tf_op jit(solution)/shard_map/pallas_call | solution.py:276
  (20 shorter events, 0.2 us)
Async XLA Ops:
  1.4 9.2 %collective-permute-start.7 = (f32[64,128]{1,0:T(8,128)S(1)}, f32[64,128]{1,0:T(8,128)S(1)}, u32[]{:S(2)}, u32[]{:S(2)}) collective-permute-start(f32[64,128]{1,0:T(8,128)S(1)} %get-tuple-element.29.u), channel_id=1, source_target_pairs={{0,7},{1,2},{2,1},{3,4},{4,3},{5,6},{6,5},{7,0},{8,15},{9,10},{10,... | collective-permute-start | bytes 98312 | tf_op jit(solution)/shard_map/ppermute | solution.py:294
  7.5 3.9 %collective-permute-start.6 = (f32[64,128]{1,0:T(8,128)S(1)}, f32[64,128]{1,0:T(8,128)S(1)}, u32[]{:S(2)}, u32[]{:S(2)}) collective-permute-start(f32[64,128]{1,0:T(8,128)S(1)} %get-tuple-element.29.u), channel_id=1, source_target_pairs={{0,1},{1,0},{2,3},{3,2},{4,5},{5,4},{6,7},{7,6},{8,9},{9,8},{10,11... | collective-permute-start | bytes 98312 | tf_op jit(solution)/shard_map/ppermute | solution.py:293
  7.5 5.6 %copy-start.1 = (f32[1,8,2,32,128]{4,3,2,1,0:T(8,128)S(1)}, f32[1,8,2,32,128]{4,3,2,1,0:T(8,128)}, u32[]{:S(2)}) copy-start(f32[1,8,2,32,128]{4,3,2,1,0:T(8,128)} %coupling.1) | copy-start | bytes 786436
  7.5 5.6 %copy-start = (f32[1,2,128,128]{3,2,1,0:T(8,128)S(1)}, f32[1,2,128,128]{3,2,1,0:T(8,128)}, u32[]{:S(2)}) copy-start(f32[1,2,128,128]{3,2,1,0:T(8,128)} %inverse.1) | copy-start | bytes 393220
  7.5 6.4 %collective-permute-start.2 = (f32[64,384]{1,0:T(8,128)S(1)}, f32[64,384]{1,0:T(8,128)S(1)}, u32[]{:S(2)}, u32[]{:S(2)}) collective-permute-start(f32[64,384]{1,0:T(8,128)S(1)} %shard_map.74.refs_0_), channel_id=1, source_target_pairs={{0,1},{1,0},{2,3},{3,2},{4,5},{5,4},{6,7},{7,6},{8,9},{9,8},{10,11... | collective-permute-start | bytes 294920 | tf_op jit(solution)/shard_map/ppermute | solution.py:288
  9.6 4.8 %collective-permute-start.1 = (f32[64,384]{1,0:T(8,128)S(1)}, f32[64,384]{1,0:T(8,128)S(1)}, u32[]{:S(2)}, u32[]{:S(2)}) collective-permute-start(f32[64,384]{1,0:T(8,128)S(1)} %shard_map.74.refs_0_), channel_id=1, source_target_pairs={{0,2},{1,3},{2,0},{3,1},{4,6},{5,7},{6,4},{7,5},{8,10},{9,11},{10,... | collective-permute-start | bytes 294920 | tf_op jit(solution)/shard_map/ppermute | solution.py:288
  9.6 5.8 %collective-permute-start = (f32[64,384]{1,0:T(8,128)S(1)}, f32[64,384]{1,0:T(8,128)S(1)}, u32[]{:S(2)}, u32[]{:S(2)}) collective-permute-start(f32[64,384]{1,0:T(8,128)S(1)} %shard_map.74.refs_0_), channel_id=1, source_target_pairs={{0,4},{1,5},{2,6},{3,7},{4,0},{5,1},{6,2},{7,3},{8,12},{9,13},{10,... | collective-permute-start | bytes 294920 | tf_op jit(solution)/shard_map/ppermute | solution.py:288
  11.4 6.1 %collective-permute-start.9 = (f32[3,64,128]{2,1,0:T(8,128)S(1)}, f32[3,64,128]{2,1,0:T(8,128)S(1)}, u32[]{:S(2)}, u32[]{:S(2)}) collective-permute-start(f32[3,64,128]{2,1,0:T(8,128)S(1)} %shard_map.77.middle), channel_id=1, source_target_pairs={{0,24},{8,16},{16,8},{24,0},{1,25},{9,17},{17,9},{25,1},{2,26},{10... | collective-permute-start | bytes 294920 | tf_op jit(solution)/shard_map/ppermute | solution.py:294
  11.5 6.0 %collective-permute-start.8 = (f32[3,64,128]{2,1,0:T(8,128)S(1)}, f32[3,64,128]{2,1,0:T(8,128)S(1)}, u32[]{:S(2)}, u32[]{:S(2)}) collective-permute-start(f32[3,64,128]{2,1,0:T(8,128)S(1)} %shard_map.77.middle), channel_id=1, source_target_pairs={{0,8},{8,0},{16,24},{24,16},{1,9},{9,1},{17,25},{25,17},{2,10},{10... | collective-permute-start | bytes 294920 | tf_op jit(solution)/shard_map/ppermute | solution.py:293
  15.4 7.3 %collective-permute-start.4 = (f32[64,384]{1,0:T(8,128)S(1)}, f32[64,384]{1,0:T(8,128)S(1)}, u32[]{:S(2)}, u32[]{:S(2)}) collective-permute-start(f32[64,384]{1,0:T(8,128)S(1)} %shard_map.76.refs_1_), channel_id=1, source_target_pairs={{0,2},{1,3},{2,0},{3,1},{4,6},{5,7},{6,4},{7,5},{8,10},{9,11},{10,... | collective-permute-start | bytes 294920 | tf_op jit(solution)/shard_map/ppermute | solution.py:288
  17.2 4.6 %collective-permute-start.3 = (f32[64,384]{1,0:T(8,128)S(1)}, f32[64,384]{1,0:T(8,128)S(1)}, u32[]{:S(2)}, u32[]{:S(2)}) collective-permute-start(f32[64,384]{1,0:T(8,128)S(1)} %shard_map.76.refs_1_), channel_id=1, source_target_pairs={{0,1},{1,0},{2,3},{3,2},{4,5},{5,4},{6,7},{7,6},{8,9},{9,8},{10,11... | collective-permute-start | bytes 294920 | tf_op jit(solution)/shard_map/ppermute | solution.py:288
  18.0 4.7 %collective-permute-start.10 = (f32[4,40,128]{2,1,0:T(8,128)S(1)}, f32[4,40,128]{2,1,0:T(8,128)S(1)}, u32[]{:S(2)}, u32[]{:S(2)}) collective-permute-start(f32[4,40,128]{2,1,0:T(8,128)S(1)} %get-tuple-element.33), channel_id=1, source_target_pairs={{0,1},{1,0},{2,3},{3,2},{4,5},{5,4},{6,7},{7,6},{8,9},{9,8},{10,11... | collective-permute-start | bytes 245768 | tf_op jit(solution)/shard_map/ppermute | solution.py:288
  19.8 9.5 %collective-permute-start.5 = (f32[64,384]{1,0:T(8,128)S(1)}, f32[64,384]{1,0:T(8,128)S(1)}, u32[]{:S(2)}, u32[]{:S(2)}) collective-permute-start(f32[64,384]{1,0:T(8,128)S(1)} %collective-permute-done.2.refs_1_.refs_3_), channel_id=1, source_target_pairs={{0,2},{1,3},{2,0},{3,1},{4,6},{5,7},{6,4},{7,5},{8,10},{9,11},{10,... | collective-permute-start | bytes 294920 | tf_op jit(solution)/shard_map/ppermute | solution.py:288
  22.7 6.5 %collective-permute-start.11 = (f32[64,384]{1,0:T(8,128)S(1)}, f32[64,384]{1,0:T(8,128)S(1)}, u32[]{:S(2)}, u32[]{:S(2)}) collective-permute-start(f32[64,384]{1,0:T(8,128)S(1)} %shard_map.80), channel_id=1, source_target_pairs={{0,1},{1,0},{2,3},{3,2},{4,5},{5,4},{6,7},{7,6},{8,9},{9,8},{10,11... | collective-permute-start | bytes 294920 | tf_op jit(solution)/shard_map/ppermute | solution.py:288
  24.9 5.8 %collective-permute-start.12 = (f32[2,40,128]{2,1,0:T(8,128)S(1)}, f32[2,40,128]{2,1,0:T(8,128)S(1)}, u32[]{:S(2)}, u32[]{:S(2)}) collective-permute-start(f32[2,40,128]{2,1,0:T(8,128)S(1)} %get-tuple-element.38), channel_id=1, source_target_pairs={{0,6},{1,7},{2,4},{3,5},{4,2},{5,3},{6,0},{7,1},{8,14},{9,15},{10,... | collective-permute-start | bytes 122888 | tf_op jit(solution)/shard_map/ppermute | solution.py:288
  25.3 5.4 %collective-permute-start.13 = (f32[2,40,128]{2,1,0:T(8,128)S(1)}, f32[2,40,128]{2,1,0:T(8,128)S(1)}, u32[]{:S(2)}, u32[]{:S(2)}) collective-permute-start(f32[2,40,128]{2,1,0:T(8,128)S(1)} %get-tuple-element.39), channel_id=1, source_target_pairs={{0,4},{1,5},{2,6},{3,7},{4,0},{5,1},{6,2},{7,3},{8,12},{9,13},{10,... | collective-permute-start | bytes 122888 | tf_op jit(solution)/shard_map/ppermute | solution.py:288
  26.2 5.0 %collective-permute-start.14 = (f32[2,40,128]{2,1,0:T(8,128)S(1)}, f32[2,40,128]{2,1,0:T(8,128)S(1)}, u32[]{:S(2)}, u32[]{:S(2)}) collective-permute-start(f32[2,40,128]{2,1,0:T(8,128)S(1)} %get-tuple-element.40), channel_id=1, source_target_pairs={{0,2},{1,3},{2,0},{3,1},{4,6},{5,7},{6,4},{7,5},{8,10},{9,11},{10,... | collective-permute-start | bytes 122888 | tf_op jit(solution)/shard_map/ppermute | solution.py:288

commit v6 on v5

--- a/solution.py
+++ b/solution.py
@@ -162,6 +162,12 @@
     out[...] = static[...]
 
 
+def pack_kernel(four, two, one, base, four_out, pair_out):
+    four_out[...] = four[...]
+    pair_out[0] = two[...]
+    pair_out[1] = four[...]
+
+
 def copy_kernel(value, *refs):
     out = refs[-1]
     out[...] = value[...]
@@ -174,13 +180,13 @@
     row_out[2] = jnp.where(first, even[...], odd[...])
 
 
-def message_kernel(even, middle, odd, base, high, low, keep_out, send_out):
+def message_kernel(even, middle, odd, base, high, low, *refs):
+    outs, natural = refs[:-1], refs[-1]
     first = lax.axis_index("blk") % 2 == 0
     up = jnp.where(first, odd[...], even[...])
     down = jnp.where(first, even[...], odd[...])
-    boxes = 2 * keep_out.shape[0]
+    boxes, _, width = natural.shape
     count = base.shape[0]
-    width = keep_out.shape[2]
     rank = up.shape[1] // 2
     share = count // boxes
     half = share // 2
@@ -188,27 +194,21 @@
     stacked = cat([v[:rank] for v in order] + [v[rank:] for v in order], 0)
     near = split(stacked.T)
     w = base[...] - dot3(near, (high[...], low[...]))
-    lower = lax.axis_index("box") % 2 == 0
-    for pair in range(boxes // 2):
-        at = 2 * pair * share
-        mine = w[at : at + share]
-        other = w[at + share : at + 2 * share]
-        for out, rows in (
-            (keep_out, jnp.where(lower, mine, other)),
-            (send_out, jnp.where(lower, other, mine)),
-        ):
-            out[pair, :share] = rows[:, :width]
-            out[pair, share : 2 * share] = rows[:, width : 2 * width]
-            t = rows[:, 2 * width :]
-            out[pair, 2 * share : 2 * share + half] = cat([t[:half], t[half:]], 1)
-
-
-def forward_kernel(count, keep, came, *refs):
-    outs = refs[-count:]
-    place = lax.axis_index("box") // 2
-    for k, out in enumerate(outs):
-        out[0] = keep[place ^ k]
-        out[1] = came[place ^ k]
+    for box in range(boxes):
+        rows = w[box * share : (box + 1) * share]
+        natural[box, :share] = rows[:, :width]
+        natural[box, share : 2 * share] = rows[:, width : 2 * width]
+        t = rows[:, 2 * width :]
+        natural[box, 2 * share : 2 * share + half] = cat([t[:half], t[half:]], 1)
+    me = lax.axis_index("box")
+    for k in range(boxes):
+        outs[k // 2][k % 2] = natural[me ^ k]
+
+
+def forward_kernel(count, *refs):
+    out = refs[-1]
+    for k in range(count):
+        out[k] = refs[k][1]
 
 
 def blocks_of(refs):
@@ -222,30 +222,28 @@
 
 def prepare_kernel(*refs):
     top_high, top_low, local_out = refs[-3:]
-    depth = top_high.shape[0] // 2
+    depth = top_high.shape[1] // 2
     rank = local_out.shape[1] // 6
     for k, block in enumerate(blocks_of(refs[:-3])):
         at = slice(2 * k * rank, 2 * (k + 1) * rank)
-        re = block[:rank, :depth]
-        im = block[rank:, :depth]
-        high, low = split(cat([cat([re, im], 0).T, cat([-im, re], 0).T], 0))
-        top_high[:, at] = high
-        top_low[:, at] = low
-        local_out[k] = stacked_form(split(block), rank, depth)
+        parts = split(block)
+        for part, top_out in zip(parts, (top_high, top_low)):
+            top_out[at] = rows_form(part[:rank, :depth], part[rank:, :depth])
+        local_out[k] = stacked_form(parts, rank, depth)
 
 
 def top_kernel(offsets, top_high, top_low, local, *refs):
-    pieces = refs[:-2][::-1]
-    out, packed = refs[-2:]
+    pieces = refs[:-3][::-1]
+    came, out, packed = refs[-3:]
     boxes = 2 * len(pieces)
-    width = pieces[0].shape[2]
+    width = came.shape[2]
     share = out.shape[1]
     half = share // 2
     rank = local.shape[1] // 6
     rows = 2 * rank
     me = lax.axis_index("box")
     for k in range(boxes):
-        packed[me ^ k] = pieces[k // 2][k % 2, 2 * share : 2 * share + half]
+        packed[me ^ k] = came[k // 2, 2 * share : 2 * share + half] if k % 2 else pieces[k // 2][0, 2 * share : 2 * share + half]
     t_re = []
     t_im = []
     for box in range(boxes):
@@ -253,16 +251,16 @@
         t_re.append(t[:, :rank])
         t_im.append(t[:, rank:])
     t = split(cat(t_re + t_im, 1))
-    first = dot(cat(t, 0), top_high[...])
-    y = split(first[:share] + (first[share:] + dot(t[0], top_low[...])))
+    first = dot(cat(t, 0), top_high[...], NT)
+    y = split(first[:share] + (first[share:] + dot(t[0], top_low[...], NT)))
     for k in range(boxes):
         at = slice(k * rows, (k + 1) * rows)
         x = dot(cat([y[0][:, at], y[1][:, at], y[0][:, at]], 1), local[k])
         offset = offsets[k]
-        piece = pieces[offset // 2]
+        piece, side = (came, offset // 2) if offset % 2 else (pieces[offset // 2], 0)
         at = pl.ds(pl.multiple_of((me ^ offset) * width, width), width)
-        out[0, :, at] = piece[offset % 2, :share] + x[:, :width]
-        out[1, :, at] = piece[offset % 2, share : 2 * share] + x[:, width:]
+        out[0, :, at] = piece[side, :share] + x[:, :width]
+        out[1, :, at] = piece[side, share : 2 * share] + x[:, width:]
 
 
 def call(kernel, outs, *arrays, hbm=(), copied=(), extra=(), cost=None):
@@ -329,11 +327,15 @@
     (row,) = call(join_kernel, [((3,) + u.shape, F32)], even, odd, u)
     (static,) = call(hold_kernel, [(static.shape, F32)], static, cost=COST)
     if boxes == 8:
-        four, two, one = [swapped(static, "box", k) for k in (4, 2, 1)]
-        (four,) = call(copy_kernel, [(static.shape, F32)], four, two, one, base, hbm=(1, 2, 3))
-        five, six, three = swapped(four, "box", 1), swapped(four, "box", 2), swapped(one, "box", 2)
-        early, late, waited = [static, four, two, one, five, six], [three], [five]
-        offsets = (0, 4, 2, 1, 5, 6, 3, 7)
+        four = swapped(static, "box", 4)
+        (again,) = call(hold_kernel, [(static.shape, F32)], static, cost=COST)
+        two, one = swapped(again, "box", 2), swapped(again, "box", 1)
+        four, pair = call(
+            pack_kernel, [(static.shape, F32), ((2,) + static.shape, F32)], four, two, one, base, hbm=(2, 3)
+        )
+        six, others = swapped(four, "box", 2), swapped(pair, "box", 1)
+        early, late, waited = [static, four, two, one, others, six], [], [others]
+        offsets = (0, 4, 2, 1, 3, 5, 6, 7)
     else:
         early, late, waited = [static[None]], [], []
         offsets = [0]
@@ -344,25 +346,25 @@
             step //= 2
     even, odd = beside(row, "blk")
     length = 2 * share + -(-share // 16) * 8
-    message = ((boxes // 2, length, width), F32)
-    keep, send = call(
-        message_kernel, [message, message],
+    pieces = call(
+        message_kernel, [((2, length, width), F32)] * (boxes // 2),
         even, row, odd, base, matrix_high, matrix_low,
-        cost=COST,
-    )
-    pieces = call(
-        functools.partial(forward_kernel, boxes // 2), [((2, length, width), F32)] * (boxes // 2),
-        keep, swapped(send, "box", 1), *waited, hbm=range(2, 2 + len(waited)),
-    )
-    if late:
+        cost=COST, extra=[pltpu.VMEM((boxes, length, width), F32)],
+    )
+    pieces = [swapped(pieces[k], "box", 2 * k) for k in reversed(range(1, boxes // 2))] + [pieces[0]]
+    (send,) = call(
+        functools.partial(forward_kernel, boxes // 2), [((boxes // 2, length, width), F32)],
+        *pieces[::-1], *waited, hbm=range(boxes // 2, boxes // 2 + len(waited)),
+    )
+    came = swapped(send, "box", 1)
+    if boxes == 8:
         (six,) = call(copy_kernel, [(six.shape, F32)], six, pieces[0], hbm=(1,))
         late.append(swapped(six, "box", 1))
-    pieces = [swapped(pieces[k], "box", 2 * k) for k in reversed(range(1, boxes // 2))] + [pieces[0]]
     top = ((2 * depth, 2 * depth), BF16)
     local = ((boxes, 6 * rank, 2 * width), BF16)
     prepared = call(prepare_kernel, [top, top, local], *early, *late)
     (out,) = call(
-        functools.partial(top_kernel, offsets), [((2, share, boxes * width), F32)], *prepared, *pieces,
+        functools.partial(top_kernel, offsets), [((2, share, boxes * width), F32)], *prepared, *pieces, came,
         extra=[pltpu.VMEM((boxes, share // 2, width), F32)],
     )
     return out

time: 32.7 us -> 30.6 us (0.936)
  starting transfers between devices: 21.5 us -> 19.3 us
  waiting for transfers between devices: 5.69 us -> 6.63 us
  Pallas kernels: 5.27 us -> 4.35 us
    ppermute x11 -> x10, starting transfers between devices: 13.8 us -> 11.1 us  [swapped(): lax.ppermute(value, axis, [(i, i ^ bit) for i in range(lax.axis_size(axis...]
    ppermute x2, starting transfers between devices: 1.6 us -> 3.1 us  [beside(): even = lax.ppermute(value, axis, [(i, i ^ 1) for i in range(count)])]
    ppermute x2, starting transfers between devices: 6.14 us -> 5.14 us  [beside(): lax.ppermute(value, axis, [(i, (i + 1) % count if i % 2 else (i - 1) % co...]
    ppermute x2, waiting for transfers between devices: 0.01 us -> 0.98 us  [beside(): lax.ppermute(value, axis, [(i, (i + 1) % count if i % 2 else (i - 1) % co...]
    pallas_call x10 -> x11, Pallas kernels: 5.27 us -> 4.35 us  [call(): pl.pallas_call(kernel, out_shape=[jax.ShapeDtypeStruct(shape, dtype) for...]
    ppermute x2, waiting for transfers between devices: 0.78 us -> 0.01 us  [beside(): even = lax.ppermute(value, axis, [(i, i ^ 1) for i in range(count)])]
    ppermute x11 -> x10, waiting for transfers between devices: 4.9 us -> 5.65 us  [swapped(): lax.ppermute(value, axis, [(i, i ^ bit) for i in range(lax.axis_size(axis...]
  transfers between devices with their start and end apart: 15 -> 14, of which waited for: 7 -> 7; matrix products, arithmetic and copies ran while one was open for 0% -> 0% of each run, Pallas kernels for 8% -> 5%
where the time goes in v6:
time: 30.6 us; the launch traced here: 30.4 us
  starting transfers between devices  19.3 us (63%)
  waiting for transfers between devices  6.63 us (22%)
  Pallas kernels  4.35 us (14%)
    ppermute x10, starting transfers between devices, swapped(): lax.ppermute(value, axis, [(i, i ^ bit) for i in range(lax.axis_size(axis...  11.1 us
    ppermute x10, waiting for transfers between devices, swapped(): lax.ppermute(value, axis, [(i, i ^ bit) for i in range(lax.axis_size(axis...  5.65 us
    ppermute x2, starting transfers between devices, beside(): lax.ppermute(value, axis, [(i, (i + 1) % count if i % 2 else (i - 1) % co...  5.14 us
    pallas_call x11, Pallas kernels, call(): pl.pallas_call(kernel, out_shape=[jax.ShapeDtypeStruct(shape, dtype) for...  4.35 us
    ppermute x2, starting transfers between devices, beside(): even = lax.ppermute(value, axis, [(i, i ^ 1) for i in range(count)])  3.1 us
    ppermute x2, waiting for transfers between devices, beside(): lax.ppermute(value, axis, [(i, (i + 1) % count if i % 2 else (i - 1) % co...  0.98 us
  transfers between devices with their start and end apart: 14, of which 7 were waited for; matrix products, arithmetic and copies ran while one was open for 0% of the time, Pallas kernels for 5%

profile of v6, /device:TPU:0, one launch (start us, length us, event | category | flops | bytes accessed | tf_op | source)
XLA Modules:
  0.0 30.4 jit_solution(3800850101044872624)
XLA Ops:
  0.0 1.4 %shard_map.73 = (f32[64,128]{1,0:T(8,128)S(1)}, f32[64,384]{1,0:T(8,128)S(1)}, bf16[128,256]{1,0:T(8,128)(2,1)S(1)}, bf16[128,256]{1,0:T(8,128)(2,1)S(1)}, bf16[...) custom-call(f32[3,128]{1,0:T(4,128)} %points_in.1, s32[1,128]{1,0:T(1,128)} %bitcast.1, s32[1,32]{1,0:T(1,128)} %skeleton_in.1, ...), custom_call_target="tpu_custom_call" | custom-call | tf_op jit(solution)/shard_map/pallas_call | solution.py:274
  1.4 3.0 %collective-permute-start.5 = (f32[64,128]{1,0:T(8,128)S(1)}, f32[64,128]{1,0:T(8,128)S(1)}, u32[]{:S(2)}, u32[]{:S(2)}) collective-permute-start(f32[64,128]{1,0:T(8,128)S(1)} %get-tuple-element.31.u), channel_id=1, source_target_pairs={{0,1},{1,0},{2,3},{3,2},{4,5},{5,4},{6,7},{7,6},{8,9},{9,8},{10,11... | collective-permute-start | bytes 98312 | tf_op jit(solution)/shard_map/ppermute | solution.py:291
  4.4 3.5 %collective-permute-start.6 = (f32[64,128]{1,0:T(8,128)S(1)}, f32[64,128]{1,0:T(8,128)S(1)}, u32[]{:S(2)}, u32[]{:S(2)}) collective-permute-start(f32[64,128]{1,0:T(8,128)S(1)} %get-tuple-element.31.u), channel_id=1, source_target_pairs={{0,7},{1,2},{2,1},{3,4},{4,3},{5,6},{6,5},{7,0},{8,15},{9,10},{10,... | collective-permute-start | bytes 98312 | tf_op jit(solution)/shard_map/ppermute | solution.py:292
  8.1 1.1 %collective-permute-start.1 = (f32[64,384]{1,0:T(8,128)S(1)}, f32[64,384]{1,0:T(8,128)S(1)}, u32[]{:S(2)}, u32[]{:S(2)}) collective-permute-start(f32[64,384]{1,0:T(8,128)S(1)} %shard_map.75), channel_id=1, source_target_pairs={{0,2},{1,3},{2,0},{3,1},{4,6},{5,7},{6,4},{7,5},{8,10},{9,11},{10,... | collective-permute-start | bytes 294920 | tf_op jit(solution)/shard_map/ppermute | solution.py:286
  9.1 1.3 %collective-permute-start.2 = (f32[64,384]{1,0:T(8,128)S(1)}, f32[64,384]{1,0:T(8,128)S(1)}, u32[]{:S(2)}, u32[]{:S(2)}) collective-permute-start(f32[64,384]{1,0:T(8,128)S(1)} %shard_map.75), channel_id=1, source_target_pairs={{0,1},{1,0},{2,3},{3,2},{4,5},{5,4},{6,7},{7,6},{8,9},{9,8},{10,11... | collective-permute-start | bytes 294920 | tf_op jit(solution)/shard_map/ppermute | solution.py:286
  10.4 1.0 %collective-permute-done.6.odd = f32[64,128]{1,0:T(8,128)S(1)} collective-permute-done((f32[64,128]{1,0:T(8,128)S(1)}, f32[64,128]{1,0:T(8,128)S(1)}, u32[]{:S(2)}, u32[]{:S(2)}) %collective-permute-start.6) | collective-permute-done | bytes 32800 | tf_op jit(solution)/shard_map/ppermute | solution.py:292
  11.5 1.6 %collective-permute-start.8 = (f32[3,64,128]{2,1,0:T(8,128)S(1)}, f32[3,64,128]{2,1,0:T(8,128)S(1)}, u32[]{:S(2)}, u32[]{:S(2)}) collective-permute-start(f32[3,64,128]{2,1,0:T(8,128)S(1)} %shard_map.78.middle), channel_id=1, source_target_pairs={{0,24},{8,16},{16,8},{24,0},{1,25},{9,17},{17,9},{25,1},{2,26},{10... | collective-permute-start | bytes 294920 | tf_op jit(solution)/shard_map/ppermute | solution.py:292
  13.1 0.8 %shard_map.76 = (f32[128,320]{1,0:T(8,128)S(1)}, bf16[512,320]{1,0:T(8,128)(2,1)S(1)}, bf16[512,320]{1,0:T(8,128)(2,1)S(1)}) custom-call(bf16[128,256]{1,0:T(8,128)(2,1)S(1)} %get-tuple-element.24.high, bf16[128,256]{1,0:T(8,128)(2,1)S(1)} %get-tuple-element.25.low, bf16[128,32]{1,0:T(8,128)(2,1)S(1)} %get-tuple-element.26.picker_in, ...), custom_call_target="tpu_custom_call" | custom-call | flops 10000000000 | bytes 10000000 | tf_op jit(solution)/shard_map/pallas_call | solution.py:274
  14.0 0.5 %collective-permute-done.1.two.refs_2_ = f32[64,384]{1,0:T(8,128)S(1)} collective-permute-done((f32[64,384]{1,0:T(8,128)S(1)}, f32[64,384]{1,0:T(8,128)S(1)}, u32[]{:S(2)}, u32[]{:S(2)}) %collective-permute-start.1) | collective-permute-done | bytes 98336 | tf_op jit(solution)/shard_map/ppermute | solution.py:286
  14.5 0.8 %collective-permute-start.3 = (f32[2,64,384]{2,1,0:T(8,128)S(1)}, f32[2,64,384]{2,1,0:T(8,128)S(1)}, u32[]{:S(2)}, u32[]{:S(2)}) collective-permute-start(f32[2,64,384]{2,1,0:T(8,128)S(1)} %get-tuple-element.30), channel_id=1, source_target_pairs={{0,1},{1,0},{2,3},{3,2},{4,5},{5,4},{6,7},{7,6},{8,9},{9,8},{10,11... | collective-permute-start | bytes 589832 | tf_op jit(solution)/shard_map/ppermute | solution.py:286
  15.3 1.6 %collective-permute-start.4 = (f32[64,384]{1,0:T(8,128)S(1)}, f32[64,384]{1,0:T(8,128)S(1)}, u32[]{:S(2)}, u32[]{:S(2)}) collective-permute-start(f32[64,384]{1,0:T(8,128)S(1)} %get-tuple-element.29.refs_1_), channel_id=1, source_target_pairs={{0,2},{1,3},{2,0},{3,1},{4,6},{5,7},{6,4},{7,5},{8,10},{9,11},{10,... | collective-permute-start | bytes 294920 | tf_op jit(solution)/shard_map/ppermute | solution.py:286
  17.0 0.5 %shard_map.79 = (f32[2,40,128]{2,1,0:T(8,128)S(1)}, f32[2,40,128]{2,1,0:T(8,128)S(1)}, f32[2,40,128]{2,1,0:T(8,128)S(1)}, f32[2,40,128]{2,1,0:T(8,128)S(1)}) custom-call(f32[3,64,128]{2,1,0:T(8,128)S(1)} %collective-permute-done.7.even, f32[3,64,128]{2,1,0:T(8,128)S(1)} %shard_map.78.middle, f32[3,64,128]{2,1,0:T(8,128)S(1)} %collective-permute-done.8.odd, ...), custom_call_target="tpu_custom_call" | custom-call | flops 10000000000 | bytes 10000000 | tf_op jit(solution)/shard_map/pallas_call | solution.py:274
  17.5 1.6 %collective-permute-start.9 = (f32[2,40,128]{2,1,0:T(8,128)S(1)}, f32[2,40,128]{2,1,0:T(8,128)S(1)}, u32[]{:S(2)}, u32[]{:S(2)}) collective-permute-start(f32[2,40,128]{2,1,0:T(8,128)S(1)} %get-tuple-element.34), channel_id=1, source_target_pairs={{0,6},{1,7},{2,4},{3,5},{4,2},{5,3},{6,0},{7,1},{8,14},{9,15},{10,... | collective-permute-start | bytes 122888 | tf_op jit(solution)/shard_map/ppermute | solution.py:286
  19.0 0.5 %collective-permute-start.11 = (f32[2,40,128]{2,1,0:T(8,128)S(1)}, f32[2,40,128]{2,1,0:T(8,128)S(1)}, u32[]{:S(2)}, u32[]{:S(2)}) collective-permute-start(f32[2,40,128]{2,1,0:T(8,128)S(1)} %get-tuple-element.38), channel_id=1, source_target_pairs={{0,4},{1,5},{2,6},{3,7},{4,0},{5,1},{6,2},{7,3},{8,12},{9,13},{10,... | collective-permute-start | bytes 122888 | tf_op jit(solution)/shard_map/ppermute | solution.py:286
  19.5 2.4 %collective-permute-start.12 = (f32[2,40,128]{2,1,0:T(8,128)S(1)}, f32[2,40,128]{2,1,0:T(8,128)S(1)}, u32[]{:S(2)}, u32[]{:S(2)}) collective-permute-start(f32[2,40,128]{2,1,0:T(8,128)S(1)} %get-tuple-element.39), channel_id=1, source_target_pairs={{0,2},{1,3},{2,0},{3,1},{4,6},{5,7},{6,4},{7,5},{8,10},{9,11},{10,... | collective-permute-start | bytes 122888 | tf_op jit(solution)/shard_map/ppermute | solution.py:286
  21.9 1.5 %collective-permute-done.9.refs_0_.refs_3_ = f32[2,40,128]{2,1,0:T(8,128)S(1)} collective-permute-done((f32[2,40,128]{2,1,0:T(8,128)S(1)}, f32[2,40,128]{2,1,0:T(8,128)S(1)}, u32[]{:S(2)}, u32[]{:S(2)}) %collective-permute-start.9) | collective-permute-done | bytes 40992 | tf_op jit(solution)/shard_map/ppermute | solution.py:286
  23.5 0.4 %collective-permute-start.10 = (f32[64,384]{1,0:T(8,128)S(1)}, f32[64,384]{1,0:T(8,128)S(1)}, u32[]{:S(2)}, u32[]{:S(2)}) collective-permute-start(f32[64,384]{1,0:T(8,128)S(1)} %shard_map.80), channel_id=1, source_target_pairs={{0,1},{1,0},{2,3},{3,2},{4,5},{5,4},{6,7},{7,6},{8,9},{9,8},{10,11... | collective-permute-start | bytes 294920 | tf_op jit(solution)/shard_map/ppermute | solution.py:286
  23.8 0.2 collective-permute-done.11.refs_2_.refs_1_
  24.0 0.4 %collective-permute-done.12.refs_1_.refs_2_ = f32[2,40,128]{2,1,0:T(8,128)S(1)} collective-permute-done((f32[2,40,128]{2,1,0:T(8,128)S(1)}, f32[2,40,128]{2,1,0:T(8,128)S(1)}, u32[]{:S(2)}, u32[]{:S(2)}) %collective-permute-start.12) | collective-permute-done | bytes 40992 | tf_op jit(solution)/shard_map/ppermute | solution.py:286
  24.4 1.5 %collective-permute-start.13 = (f32[4,40,128]{2,1,0:T(8,128)S(1)}, f32[4,40,128]{2,1,0:T(8,128)S(1)}, u32[]{:S(2)}, u32[]{:S(2)}) collective-permute-start(f32[4,40,128]{2,1,0:T(8,128)S(1)} %shard_map.82), channel_id=1, source_target_pairs={{0,1},{1,0},{2,3},{3,2},{4,5},{5,4},{6,7},{7,6},{8,9},{9,8},{10,11... | collective-permute-start | bytes 245768 | tf_op jit(solution)/shard_map/ppermute | solution.py:286
  25.8 2.3 %collective-permute-done.10.refs_6_ = f32[64,384]{1,0:T(8,128)S(1)} collective-permute-done((f32[64,384]{1,0:T(8,128)S(1)}, f32[64,384]{1,0:T(8,128)S(1)}, u32[]{:S(2)}, u32[]{:S(2)}) %collective-permute-start.10) | collective-permute-done | bytes 98336 | tf_op jit(solution)/shard_map/ppermute | solution.py:286
  28.1 0.1 shard_map.81
  28.3 0.7 %collective-permute-done.13.refs_4_ = f32[4,40,128]{2,1,0:T(8,128)S(1)} collective-permute-done((f32[4,40,128]{2,1,0:T(8,128)S(1)}, f32[4,40,128]{2,1,0:T(8,128)S(1)}, u32[]{:S(2)}, u32[]{:S(2)}) %collective-permute-start.13) | collective-permute-done | bytes 81952 | tf_op jit(solution)/shard_map/ppermute | solution.py:286
  29.0 1.4 %shard_map.83 = f32[2,16,1024]{2,1,0:T(8,128)} custom-call(bf16[512,512]{1,0:T(8,128)(2,1)S(1)} %get-tuple-element.35.top_high, bf16[512,512]{1,0:T(8,128)(2,1)S(1)} %get-tuple-element.36.top_low, bf16[8,192,256]{2,1,0:T(8,128)(2,1)S(1)} %get-tuple-element.37.local, f32[2,40,128]{2,1,0:T(8,128)S(1)} %collective-permute-done.9.refs_0_.refs_3_, ...), custom_call_target="tpu_custom_call" | custom-call | tf_op jit(solution)/shard_map/pallas_call | solution.py:274
  (19 shorter events, 0.2 us)
Async XLA Ops:
  1.4 9.0 %collective-permute-start.5 = (f32[64,128]{1,0:T(8,128)S(1)}, f32[64,128]{1,0:T(8,128)S(1)}, u32[]{:S(2)}, u32[]{:S(2)}) collective-permute-start(f32[64,128]{1,0:T(8,128)S(1)} %get-tuple-element.31.u), channel_id=1, source_target_pairs={{0,1},{1,0},{2,3},{3,2},{4,5},{5,4},{6,7},{7,6},{8,9},{9,8},{10,11... | collective-permute-start | bytes 98312 | tf_op jit(solution)/shard_map/ppermute | solution.py:291
  4.4 7.0 %collective-permute-start.6 = (f32[64,128]{1,0:T(8,128)S(1)}, f32[64,128]{1,0:T(8,128)S(1)}, u32[]{:S(2)}, u32[]{:S(2)}) collective-permute-start(f32[64,128]{1,0:T(8,128)S(1)} %get-tuple-element.31.u), channel_id=1, source_target_pairs={{0,7},{1,2},{2,1},{3,4},{4,3},{5,6},{6,5},{7,0},{8,15},{9,10},{10,... | collective-permute-start | bytes 98312 | tf_op jit(solution)/shard_map/ppermute | solution.py:292
  8.0 5.1 %copy-start.1 = (f32[1,8,2,32,128]{4,3,2,1,0:T(8,128)S(1)}, f32[1,8,2,32,128]{4,3,2,1,0:T(8,128)}, u32[]{:S(2)}) copy-start(f32[1,8,2,32,128]{4,3,2,1,0:T(8,128)} %coupling.1) | copy-start | bytes 786436
  8.0 6.0 %collective-permute-start = (f32[64,384]{1,0:T(8,128)S(1)}, f32[64,384]{1,0:T(8,128)S(1)}, u32[]{:S(2)}, u32[]{:S(2)}) collective-permute-start(f32[64,384]{1,0:T(8,128)S(1)} %shard_map.74.static.refs_0_), channel_id=1, source_target_pairs={{0,4},{1,5},{2,6},{3,7},{4,0},{5,1},{6,2},{7,3},{8,12},{9,13},{10,... | collective-permute-start | bytes 294920 | tf_op jit(solution)/shard_map/ppermute | solution.py:286
  8.1 5.0 %copy-start = (f32[1,2,128,128]{3,2,1,0:T(8,128)S(1)}, f32[1,2,128,128]{3,2,1,0:T(8,128)}, u32[]{:S(2)}) copy-start(f32[1,2,128,128]{3,2,1,0:T(8,128)} %inverse.1) | copy-start | bytes 393220
  8.1 6.4 %collective-permute-start.1 = (f32[64,384]{1,0:T(8,128)S(1)}, f32[64,384]{1,0:T(8,128)S(1)}, u32[]{:S(2)}, u32[]{:S(2)}) collective-permute-start(f32[64,384]{1,0:T(8,128)S(1)} %shard_map.75), channel_id=1, source_target_pairs={{0,2},{1,3},{2,0},{3,1},{4,6},{5,7},{6,4},{7,5},{8,10},{9,11},{10,... | collective-permute-start | bytes 294920 | tf_op jit(solution)/shard_map/ppermute | solution.py:286
  9.1 5.4 %collective-permute-start.2 = (f32[64,384]{1,0:T(8,128)S(1)}, f32[64,384]{1,0:T(8,128)S(1)}, u32[]{:S(2)}, u32[]{:S(2)}) collective-permute-start(f32[64,384]{1,0:T(8,128)S(1)} %shard_map.75), channel_id=1, source_target_pairs={{0,1},{1,0},{2,3},{3,2},{4,5},{5,4},{6,7},{7,6},{8,9},{9,8},{10,11... | collective-permute-start | bytes 294920 | tf_op jit(solution)/shard_map/ppermute | solution.py:286
  11.4 5.5 %collective-permute-start.7 = (f32[3,64,128]{2,1,0:T(8,128)S(1)}, f32[3,64,128]{2,1,0:T(8,128)S(1)}, u32[]{:S(2)}, u32[]{:S(2)}) collective-permute-start(f32[3,64,128]{2,1,0:T(8,128)S(1)} %shard_map.78.middle), channel_id=1, source_target_pairs={{0,8},{8,0},{16,24},{24,16},{1,9},{9,1},{17,25},{25,17},{2,10},{10... | collective-permute-start | bytes 294920 | tf_op jit(solution)/shard_map/ppermute | solution.py:291
  11.5 5.4 %collective-permute-start.8 = (f32[3,64,128]{2,1,0:T(8,128)S(1)}, f32[3,64,128]{2,1,0:T(8,128)S(1)}, u32[]{:S(2)}, u32[]{:S(2)}) collective-permute-start(f32[3,64,128]{2,1,0:T(8,128)S(1)} %shard_map.78.middle), channel_id=1, source_target_pairs={{0,24},{8,16},{16,8},{24,0},{1,25},{9,17},{17,9},{25,1},{2,26},{10... | collective-permute-start | bytes 294920 | tf_op jit(solution)/shard_map/ppermute | solution.py:292
  14.5 9.8 %collective-permute-start.3 = (f32[2,64,384]{2,1,0:T(8,128)S(1)}, f32[2,64,384]{2,1,0:T(8,128)S(1)}, u32[]{:S(2)}, u32[]{:S(2)}) collective-permute-start(f32[2,64,384]{2,1,0:T(8,128)S(1)} %get-tuple-element.30), channel_id=1, source_target_pairs={{0,1},{1,0},{2,3},{3,2},{4,5},{5,4},{6,7},{7,6},{8,9},{9,8},{10,11... | collective-permute-start | bytes 589832 | tf_op jit(solution)/shard_map/ppermute | solution.py:286
  15.3 8.1 %collective-permute-start.4 = (f32[64,384]{1,0:T(8,128)S(1)}, f32[64,384]{1,0:T(8,128)S(1)}, u32[]{:S(2)}, u32[]{:S(2)}) collective-permute-start(f32[64,384]{1,0:T(8,128)S(1)} %get-tuple-element.29.refs_1_), channel_id=1, source_target_pairs={{0,2},{1,3},{2,0},{3,1},{4,6},{5,7},{6,4},{7,5},{8,10},{9,11},{10,... | collective-permute-start | bytes 294920 | tf_op jit(solution)/shard_map/ppermute | solution.py:286
  17.5 6.0 %collective-permute-start.9 = (f32[2,40,128]{2,1,0:T(8,128)S(1)}, f32[2,40,128]{2,1,0:T(8,128)S(1)}, u32[]{:S(2)}, u32[]{:S(2)}) collective-permute-start(f32[2,40,128]{2,1,0:T(8,128)S(1)} %get-tuple-element.34), channel_id=1, source_target_pairs={{0,6},{1,7},{2,4},{3,5},{4,2},{5,3},{6,0},{7,1},{8,14},{9,15},{10,... | collective-permute-start | bytes 122888 | tf_op jit(solution)/shard_map/ppermute | solution.py:286
  19.0 5.0 %collective-permute-start.11 = (f32[2,40,128]{2,1,0:T(8,128)S(1)}, f32[2,40,128]{2,1,0:T(8,128)S(1)}, u32[]{:S(2)}, u32[]{:S(2)}) collective-permute-start(f32[2,40,128]{2,1,0:T(8,128)S(1)} %get-tuple-element.38), channel_id=1, source_target_pairs={{0,4},{1,5},{2,6},{3,7},{4,0},{5,1},{6,2},{7,3},{8,12},{9,13},{10,... | collective-permute-start | bytes 122888 | tf_op jit(solution)/shard_map/ppermute | solution.py:286
  19.5 4.9 %collective-permute-start.12 = (f32[2,40,128]{2,1,0:T(8,128)S(1)}, f32[2,40,128]{2,1,0:T(8,128)S(1)}, u32[]{:S(2)}, u32[]{:S(2)}) collective-permute-start(f32[2,40,128]{2,1,0:T(8,128)S(1)} %get-tuple-element.39), channel_id=1, source_target_pairs={{0,2},{1,3},{2,0},{3,1},{4,6},{5,7},{6,4},{7,5},{8,10},{9,11},{10,... | collective-permute-start | bytes 122888 | tf_op jit(solution)/shard_map/ppermute | solution.py:286
  23.5 4.7 %collective-permute-start.10 = (f32[64,384]{1,0:T(8,128)S(1)}, f32[64,384]{1,0:T(8,128)S(1)}, u32[]{:S(2)}, u32[]{:S(2)}) collective-permute-start(f32[64,384]{1,0:T(8,128)S(1)} %shard_map.80), channel_id=1, source_target_pairs={{0,1},{1,0},{2,3},{3,2},{4,5},{5,4},{6,7},{7,6},{8,9},{9,8},{10,11... | collective-permute-start | bytes 294920 | tf_op jit(solution)/shard_map/ppermute | solution.py:286
  24.4 4.6 %collective-permute-start.13 = (f32[4,40,128]{2,1,0:T(8,128)S(1)}, f32[4,40,128]{2,1,0:T(8,128)S(1)}, u32[]{:S(2)}, u32[]{:S(2)}) collective-permute-start(f32[4,40,128]{2,1,0:T(8,128)S(1)} %shard_map.82), channel_id=1, source_target_pairs={{0,1},{1,0},{2,3},{3,2},{4,5},{5,4},{6,7},{7,6},{8,9},{9,8},{10,11... | collective-permute-start | bytes 245768 | tf_op jit(solution)/shard_map/ppermute | solution.py:286

commit v7 on v6

--- a/solution.py
+++ b/solution.py
@@ -73,15 +73,17 @@
     return cat([cat([re, im], 1), cat([-im, re], 1)], 0)
 
 
-def field_kernel(points_in, angles_in, skeleton_in, inverse_in, top_in, mask_in, u_out, static_out, high_out, low_out,
-                 picker_out, mask_out, points, angles, skeleton, inverse, top, mask, sems):
+def field_kernel(points_in, angles_in, skeleton_in, top_in, mask_in, inverse_in, coupling_in,
+                 u_out, static_out, high_out, low_out, picker_out, mask_out, inverse, coupling,
+                 points, angles, skeleton, top, mask, sems, more_sems):
     copies = [
         pltpu.make_async_copy(source, target, sems.at[k])
         for k, (source, target) in enumerate((
-            (angles_in, angles), (points_in, points), (skeleton_in, skeleton), (inverse_in, inverse), (top_in, top),
-            (mask_in, mask),
+            (angles_in, angles), (points_in, points), (skeleton_in, skeleton), (top_in, top), (mask_in, mask),
         ))
     ]
+    copies.append(pltpu.make_async_copy(inverse_in, inverse, more_sems.at[0]))
+    copies.append(pltpu.make_async_copy(coupling_in, coupling, more_sems.at[1]))
     for copy in copies:
         copy.start()
     count = angles.shape[1]
@@ -109,9 +111,9 @@
     copies[2].wait()
     picker = one_hot(skeleton[...], width)
     picker_out[...] = picker
+    copies[4].wait()
+    mask_out[...] = mask[...].astype(F32)
     copies[5].wait()
-    mask_out[...] = mask[...].astype(F32)
-    copies[3].wait()
     parts = split(cat([inverse[0, 0], inverse[0, 1]], 1))
     rows = dot(picker, cat(parts, 1), TN)
     rows_high = rows[:, : 2 * width]
@@ -120,11 +122,12 @@
     form = both((rows_high, rows_low), lambda v: rows_form(v[:, :width], v[:, width:]).astype(BF16))
     u_out[...] = dot3(form, field, NT)
     depth = top.shape[3]
-    copies[4].wait()
+    copies[3].wait()
     for part in range(2):
         at = slice(part * rank, (part + 1) * rank)
         static_out[at, :depth] = top[0, part]
         static_out[at, depth:] = whole[:, part * width : (part + 1) * width]
+    copies[6].wait()
 
 
 def coupling_kernel(high, low, picker_in, mask, inverse, coupling, base_out, high_out, low_out):
@@ -158,11 +161,11 @@
             out[depth:, at + part : at + 2 * part] = matrix[:, :part]
 
 
-def hold_kernel(static, out):
+def hold_kernel(static, before, out):
     out[...] = static[...]
 
 
-def pack_kernel(four, two, one, base, four_out, pair_out):
+def pack_kernel(four, two, one, four_out, pair_out):
     four_out[...] = four[...]
     pair_out[0] = two[...]
     pair_out[1] = four[...]
@@ -170,10 +173,10 @@
 
 def copy_kernel(value, *refs):
     out = refs[-1]
-    out[...] = value[...]
-
-
-def join_kernel(even, odd, u, row_out):
+    out[...] = value[1]
+
+
+def join_kernel(odd, even, u, row_out):
     first = lax.axis_index("box") % 2 == 0
     row_out[0] = jnp.where(first, odd[...], even[...])
     row_out[1] = u[...]
@@ -263,14 +266,14 @@
         out[1, :, at] = piece[side, share : 2 * share] + x[:, width:]
 
 
-def call(kernel, outs, *arrays, hbm=(), copied=(), extra=(), cost=None):
+def call(kernel, outs, *arrays, hbm=(), copied=(), held=(), extra=(), cost=None):
     spaces = {i: pl.BlockSpec(memory_space=pl.ANY) for i in hbm}
-    spaces.update({i: pl.BlockSpec(memory_space=pltpu.HBM) for i in copied})
+    spaces.update({i: pl.BlockSpec(memory_space=pltpu.HBM) for i in (*copied, *held)})
     scratch = [pltpu.VMEM(arrays[i].shape, arrays[i].dtype) for i in copied]
     if scratch:
         scratch.append(pltpu.SemaphoreType.DMA((len(scratch),)))
     scratch += extra
-    arrays = [pltpu.with_memory_space_constraint(v, pltpu.HBM) if i in copied else v for i, v in enumerate(arrays)]
+    arrays = [pltpu.with_memory_space_constraint(v, pltpu.HBM) if i in (*copied, *held) else v for i, v in enumerate(arrays)]
     return pl.pallas_call(
         kernel,
         out_shape=[jax.ShapeDtypeStruct(shape, dtype) for shape, dtype in outs],
@@ -301,7 +304,7 @@
     sides = near_mask.shape[1]
     depth = top_inverse.shape[3]
     share = count // boxes
-    u, static, high, low, picker, mask = call(
+    u, static, high, low, picker, mask, inverse, coupling = call(
         field_kernel,
         [
             ((2 * rank, count), F32),
@@ -310,9 +313,11 @@
             ((count, 2 * width), BF16),
             ((width, rank), BF16),
             (near_mask.shape, F32),
+            (box_inverse_parts.shape, F32),
+            (near_coupling.shape, F32),
         ],
-        surface_points, angle_ids.reshape(1, count), skeleton, box_inverse_parts, top_inverse,
-        near_mask, copied=range(6),
+        surface_points, angle_ids.reshape(1, count), skeleton, top_inverse, near_mask,
+        box_inverse_parts, near_coupling, copied=range(5), held=(5, 6), extra=[pltpu.SemaphoreType.DMA((2,))],
     )
     base, matrix_high, matrix_low = call(
         coupling_kernel,
@@ -321,20 +326,20 @@
             ((2 * sides * rank, 2 * width + 2 * rank), BF16),
             ((2 * sides * rank, 2 * width + 2 * rank), BF16),
         ],
-        high, low, picker, mask, box_inverse_parts, near_coupling, cost=COST,
+        high, low, picker, mask, inverse, coupling, cost=COST,
     )
     even, odd = beside(u, "box")
-    (row,) = call(join_kernel, [((3,) + u.shape, F32)], even, odd, u)
-    (static,) = call(hold_kernel, [(static.shape, F32)], static, cost=COST)
+    (row,) = call(join_kernel, [((3,) + u.shape, F32)], odd, even, u)
+    (static,) = call(hold_kernel, [(static.shape, F32)], static, base, hbm=(1,), cost=COST)
     if boxes == 8:
         four = swapped(static, "box", 4)
-        (again,) = call(hold_kernel, [(static.shape, F32)], static, cost=COST)
+        (again,) = call(hold_kernel, [(static.shape, F32)], static, base, hbm=(1,), cost=COST)
         two, one = swapped(again, "box", 2), swapped(again, "box", 1)
         four, pair = call(
-            pack_kernel, [(static.shape, F32), ((2,) + static.shape, F32)], four, two, one, base, hbm=(2, 3)
+            pack_kernel, [(static.shape, F32), ((2,) + static.shape, F32)], four, two, one, hbm=(2,)
         )
         six, others = swapped(four, "box", 2), swapped(pair, "box", 1)
-        early, late, waited = [static, four, two, one, others, six], [], [others]
+        early, late, waited = [static, four, two, one, others, six], [], [others, six]
         offsets = (0, 4, 2, 1, 3, 5, 6, 7)
     else:
         early, late, waited = [static[None]], [], []
@@ -358,8 +363,8 @@
     )
     came = swapped(send, "box", 1)
     if boxes == 8:
-        (six,) = call(copy_kernel, [(six.shape, F32)], six, pieces[0], hbm=(1,))
-        late.append(swapped(six, "box", 1))
+        (five,) = call(copy_kernel, [(six.shape, F32)], others, pieces[0], hbm=(1,))
+        late.append(swapped(five, "box", 2))
     top = ((2 * depth, 2 * depth), BF16)
     local = ((boxes, 6 * rank, 2 * width), BF16)
     prepared = call(prepare_kernel, [top, top, local], *early, *late)

time: 30.6 us -> 32.1 us (1.049)
  waiting for transfers between devices: 6.63 us -> 9.29 us
  starting transfers between devices: 19.3 us -> 18.2 us
    ppermute x10, waiting for transfers between devices: 5.65 us -> 9.28 us  [swapped(): lax.ppermute(value, axis, [(i, i ^ bit) for i in range(lax.axis_size(axis...]
    ppermute x2, starting transfers between devices: 3.1 us -> 0.07 us  [beside(): even = lax.ppermute(value, axis, [(i, i ^ 1) for i in range(count)])]
    ppermute x2, starting transfers between devices: 5.14 us -> 7.67 us  [beside(): lax.ppermute(value, axis, [(i, (i + 1) % count if i % 2 else (i - 1) % co...]
    ppermute x2, waiting for transfers between devices: 0.98 us -> 0.01 us  [beside(): lax.ppermute(value, axis, [(i, (i + 1) % count if i % 2 else (i - 1) % co...]
    ppermute x10, starting transfers between devices: 11.1 us -> 10.4 us  [swapped(): lax.ppermute(value, axis, [(i, i ^ bit) for i in range(lax.axis_size(axis...]
where the time goes in v7:
time: 32.1 us; the launch traced here: 31.9 us
  starting transfers between devices  18.2 us (57%)
  waiting for transfers between devices  9.29 us (29%)
  Pallas kernels  4.39 us (14%)
    ppermute x10, starting transfers between devices, swapped(): lax.ppermute(value, axis, [(i, i ^ bit) for i in range(lax.axis_size(axis...  10.4 us
    ppermute x10, waiting for transfers between devices, swapped(): lax.ppermute(value, axis, [(i, i ^ bit) for i in range(lax.axis_size(axis...  9.28 us
    ppermute x2, starting transfers between devices, beside(): lax.ppermute(value, axis, [(i, (i + 1) % count if i % 2 else (i - 1) % co...  7.67 us
    pallas_call x11, Pallas kernels, call(): pl.pallas_call(kernel, out_shape=[jax.ShapeDtypeStruct(shape, dtype) for...  4.39 us
  transfers between devices with their start and end apart: 14, of which 7 were waited for; matrix products, arithmetic and copies ran while one was open for 0% of the time, Pallas kernels for 5%

profile of v7, /device:TPU:0, one launch (start us, length us, event | category | flops | bytes accessed | tf_op | source)
XLA Modules:
  0.0 31.9 jit_solution(8257519437683431939)
XLA Ops:
  0.0 1.4 %shard_map.73 = (f32[64,128]{1,0:T(8,128)S(1)}, f32[64,384]{1,0:T(8,128)S(1)}, bf16[128,256]{1,0:T(8,128)(2,1)S(1)}, bf16[128,256]{1,0:T(8,128)(2,1)S(1)}, bf16[...) custom-call(f32[3,128]{1,0:T(4,128)} %points_in.1, ...), custom_call_target="tpu_custom_call" | custom-call | tf_op jit(solution)/shard_map/pallas_call | solution.py:277
  1.4 6.1 %collective-permute-start.5 = (f32[64,128]{1,0:T(8,128)S(1)}, f32[64,128]{1,0:T(8,128)S(1)}, u32[]{:S(2)}, u32[]{:S(2)}) collective-permute-start(f32[64,128]{1,0:T(8,128)S(1)} %get-tuple-element.35.u), channel_id=1, source_target_pairs={{0,7},{1,2},{2,1},{3,4},{4,3},{5,6},{6,5},{7,0},{8,15},{9,10},{10,... | collective-permute-start | bytes 98312 | tf_op jit(solution)/shard_map/ppermute | solution.py:295
  7.5 0.9 %shard_map.74 = (f32[128,320]{1,0:T(8,128)S(1)}, bf16[512,320]{1,0:T(8,128)(2,1)S(1)}, bf16[512,320]{1,0:T(8,128)(2,1)S(1)}) custom-call(bf16[128,256]{1,0:T(8,128)(2,1)S(1)} %get-tuple-element.26.high, bf16[128,256]{1,0:T(8,128)(2,1)S(1)} %get-tuple-element.27.low, bf16[128,32]{1,0:T(8,128)(2,1)S(1)} %get-tuple-element.28.picker_in, ...), custom_call_target="tpu_custom_call" | custom-call | flops 10000000000 | bytes 10000000 | tf_op jit(solution)/shard_map/pallas_call | solution.py:277
  8.4 1.1 %collective-permute-start = (f32[64,384]{1,0:T(8,128)S(1)}, f32[64,384]{1,0:T(8,128)S(1)}, u32[]{:S(2)}, u32[]{:S(2)}) collective-permute-start(f32[64,384]{1,0:T(8,128)S(1)} %shard_map.75.static.refs_0_), channel_id=1, source_target_pairs={{0,4},{1,5},{2,6},{3,7},{4,0},{5,1},{6,2},{7,3},{8,12},{9,13},{10,... | collective-permute-start | bytes 294920 | tf_op jit(solution)/shard_map/ppermute | solution.py:289
  9.5 0.2 collective-permute-start.1
  9.7 1.8 %collective-permute-start.2 = (f32[64,384]{1,0:T(8,128)S(1)}, f32[64,384]{1,0:T(8,128)S(1)}, u32[]{:S(2)}, u32[]{:S(2)}) collective-permute-start(f32[64,384]{1,0:T(8,128)S(1)} %shard_map.76), channel_id=1, source_target_pairs={{0,1},{1,0},{2,3},{3,2},{4,5},{5,4},{6,7},{7,6},{8,9},{9,8},{10,11... | collective-permute-start | bytes 294920 | tf_op jit(solution)/shard_map/ppermute | solution.py:289
  11.6 1.6 %collective-permute-start.8 = (f32[3,64,128]{2,1,0:T(8,128)S(1)}, f32[3,64,128]{2,1,0:T(8,128)S(1)}, u32[]{:S(2)}, u32[]{:S(2)}) collective-permute-start(f32[3,64,128]{2,1,0:T(8,128)S(1)} %shard_map.78.middle), channel_id=1, source_target_pairs={{0,24},{8,16},{16,8},{24,0},{1,25},{9,17},{17,9},{25,1},{2,26},{10... | collective-permute-start | bytes 294920 | tf_op jit(solution)/shard_map/ppermute | solution.py:295
  13.2 1.7 %collective-permute-done.four = f32[64,384]{1,0:T(8,128)S(1)} collective-permute-done((f32[64,384]{1,0:T(8,128)S(1)}, f32[64,384]{1,0:T(8,128)S(1)}, u32[]{:S(2)}, u32[]{:S(2)}) %collective-permute-start) | collective-permute-done | bytes 98336 | tf_op jit(solution)/shard_map/ppermute | solution.py:289
  14.9 0.5 %collective-permute-done.1.two.refs_2_ = f32[64,384]{1,0:T(8,128)S(1)} collective-permute-done((f32[64,384]{1,0:T(8,128)S(1)}, f32[64,384]{1,0:T(8,128)S(1)}, u32[]{:S(2)}, u32[]{:S(2)}) %collective-permute-start.1) | collective-permute-done | bytes 98336 | tf_op jit(solution)/shard_map/ppermute | solution.py:289
  15.5 1.6 %collective-permute-start.3 = (f32[2,64,384]{2,1,0:T(8,128)S(1)}, f32[2,64,384]{2,1,0:T(8,128)S(1)}, u32[]{:S(2)}, u32[]{:S(2)}) collective-permute-start(f32[2,64,384]{2,1,0:T(8,128)S(1)} %get-tuple-element.34), channel_id=1, source_target_pairs={{0,1},{1,0},{2,3},{3,2},{4,5},{5,4},{6,7},{7,6},{8,9},{9,8},{10,11... | collective-permute-start | bytes 589832 | tf_op jit(solution)/shard_map/ppermute | solution.py:289
  17.1 0.2 collective-permute-start.4
  17.3 0.5 %shard_map.79 = (f32[2,40,128]{2,1,0:T(8,128)S(1)}, f32[2,40,128]{2,1,0:T(8,128)S(1)}, f32[2,40,128]{2,1,0:T(8,128)S(1)}, f32[2,40,128]{2,1,0:T(8,128)S(1)}) custom-call(f32[3,64,128]{2,1,0:T(8,128)S(1)} %collective-permute-done.7.even, f32[3,64,128]{2,1,0:T(8,128)S(1)} %shard_map.78.middle, f32[3,64,128]{2,1,0:T(8,128)S(1)} %collective-permute-done.8.odd, ...), custom_call_target="tpu_custom_call" | custom-call | flops 10000000000 | bytes 10000000 | tf_op jit(solution)/shard_map/pallas_call | solution.py:277
  17.8 2.5 %collective-permute-start.9 = (f32[2,40,128]{2,1,0:T(8,128)S(1)}, f32[2,40,128]{2,1,0:T(8,128)S(1)}, u32[]{:S(2)}, u32[]{:S(2)}) collective-permute-start(f32[2,40,128]{2,1,0:T(8,128)S(1)} %get-tuple-element.38), channel_id=1, source_target_pairs={{0,6},{1,7},{2,4},{3,5},{4,2},{5,3},{6,0},{7,1},{8,14},{9,15},{10,... | collective-permute-start | bytes 122888 | tf_op jit(solution)/shard_map/ppermute | solution.py:289
  20.3 0.9 %collective-permute-start.11 = (f32[2,40,128]{2,1,0:T(8,128)S(1)}, f32[2,40,128]{2,1,0:T(8,128)S(1)}, u32[]{:S(2)}, u32[]{:S(2)}) collective-permute-start(f32[2,40,128]{2,1,0:T(8,128)S(1)} %get-tuple-element.42), channel_id=1, source_target_pairs={{0,4},{1,5},{2,6},{3,7},{4,0},{5,1},{6,2},{7,3},{8,12},{9,13},{10,... | collective-permute-start | bytes 122888 | tf_op jit(solution)/shard_map/ppermute | solution.py:289
  21.2 1.1 %collective-permute-start.12 = (f32[2,40,128]{2,1,0:T(8,128)S(1)}, f32[2,40,128]{2,1,0:T(8,128)S(1)}, u32[]{:S(2)}, u32[]{:S(2)}) collective-permute-start(f32[2,40,128]{2,1,0:T(8,128)S(1)} %get-tuple-element.43), channel_id=1, source_target_pairs={{0,2},{1,3},{2,0},{3,1},{4,6},{5,7},{6,4},{7,5},{8,10},{9,11},{10,... | collective-permute-start | bytes 122888 | tf_op jit(solution)/shard_map/ppermute | solution.py:289
  22.3 1.5 %collective-permute-done.9.refs_0_.refs_3_ = f32[2,40,128]{2,1,0:T(8,128)S(1)} collective-permute-done((f32[2,40,128]{2,1,0:T(8,128)S(1)}, f32[2,40,128]{2,1,0:T(8,128)S(1)}, u32[]{:S(2)}, u32[]{:S(2)}) %collective-permute-start.9) | collective-permute-done | bytes 40992 | tf_op jit(solution)/shard_map/ppermute | solution.py:289
  23.8 0.8 %collective-permute-start.10 = (f32[64,384]{1,0:T(8,128)S(1)}, f32[64,384]{1,0:T(8,128)S(1)}, u32[]{:S(2)}, u32[]{:S(2)}) collective-permute-start(f32[64,384]{1,0:T(8,128)S(1)} %shard_map.80), channel_id=1, source_target_pairs={{0,2},{1,3},{2,0},{3,1},{4,6},{5,7},{6,4},{7,5},{8,10},{9,11},{10,... | collective-permute-start | bytes 294920 | tf_op jit(solution)/shard_map/ppermute | solution.py:289
  24.6 0.6 %collective-permute-done.11.refs_2_.refs_1_ = f32[2,40,128]{2,1,0:T(8,128)S(1)} collective-permute-done((f32[2,40,128]{2,1,0:T(8,128)S(1)}, f32[2,40,128]{2,1,0:T(8,128)S(1)}, u32[]{:S(2)}, u32[]{:S(2)}) %collective-permute-start.11) | collective-permute-done | bytes 40992 | tf_op jit(solution)/shard_map/ppermute | solution.py:289
  25.2 0.8 %collective-permute-done.12.refs_1_.refs_2_ = f32[2,40,128]{2,1,0:T(8,128)S(1)} collective-permute-done((f32[2,40,128]{2,1,0:T(8,128)S(1)}, f32[2,40,128]{2,1,0:T(8,128)S(1)}, u32[]{:S(2)}, u32[]{:S(2)}) %collective-permute-start.12) | collective-permute-done | bytes 40992 | tf_op jit(solution)/shard_map/ppermute | solution.py:289
  26.0 0.2 collective-permute-start.13
  26.2 2.3 %collective-permute-done.10.refs_6_ = f32[64,384]{1,0:T(8,128)S(1)} collective-permute-done((f32[64,384]{1,0:T(8,128)S(1)}, f32[64,384]{1,0:T(8,128)S(1)}, u32[]{:S(2)}, u32[]{:S(2)}) %collective-permute-start.10) | collective-permute-done | bytes 98336 | tf_op jit(solution)/shard_map/ppermute | solution.py:289
  28.5 0.1 shard_map.81
  28.6 1.9 %collective-permute-done.13.refs_4_ = f32[4,40,128]{2,1,0:T(8,128)S(1)} collective-permute-done((f32[4,40,128]{2,1,0:T(8,128)S(1)}, f32[4,40,128]{2,1,0:T(8,128)S(1)}, u32[]{:S(2)}, u32[]{:S(2)}) %collective-permute-start.13) | collective-permute-done | bytes 81952 | tf_op jit(solution)/shard_map/ppermute | solution.py:289
  30.5 1.4 %shard_map.83 = f32[2,16,1024]{2,1,0:T(8,128)} custom-call(bf16[512,512]{1,0:T(8,128)(2,1)S(1)} %get-tuple-element.39.top_high, bf16[512,512]{1,0:T(8,128)(2,1)S(1)} %get-tuple-element.40.top_low, bf16[8,192,256]{2,1,0:T(8,128)(2,1)S(1)} %get-tuple-element.41.local, f32[2,40,128]{2,1,0:T(8,128)S(1)} %collective-permute-done.9.refs_0_.refs_3_, ...), custom_call_target="tpu_custom_call" | custom-call | tf_op jit(solution)/shard_map/pallas_call | solution.py:277
  (15 shorter events, 0.2 us)
Async XLA Ops:
  1.4 10.1 %collective-permute-start.5 = (f32[64,128]{1,0:T(8,128)S(1)}, f32[64,128]{1,0:T(8,128)S(1)}, u32[]{:S(2)}, u32[]{:S(2)}) collective-permute-start(f32[64,128]{1,0:T(8,128)S(1)} %get-tuple-element.35.u), channel_id=1, source_target_pairs={{0,7},{1,2},{2,1},{3,4},{4,3},{5,6},{6,5},{7,0},{8,15},{9,10},{10,... | collective-permute-start | bytes 98312 | tf_op jit(solution)/shard_map/ppermute | solution.py:295
  7.5 4.1 %collective-permute-start.6 = (f32[64,128]{1,0:T(8,128)S(1)}, f32[64,128]{1,0:T(8,128)S(1)}, u32[]{:S(2)}, u32[]{:S(2)}) collective-permute-start(f32[64,128]{1,0:T(8,128)S(1)} %get-tuple-element.35.u), channel_id=1, source_target_pairs={{0,1},{1,0},{2,3},{3,2},{4,5},{5,4},{6,7},{7,6},{8,9},{9,8},{10,11... | collective-permute-start | bytes 98312 | tf_op jit(solution)/shard_map/ppermute | solution.py:294
  8.4 6.6 %collective-permute-start = (f32[64,384]{1,0:T(8,128)S(1)}, f32[64,384]{1,0:T(8,128)S(1)}, u32[]{:S(2)}, u32[]{:S(2)}) collective-permute-start(f32[64,384]{1,0:T(8,128)S(1)} %shard_map.75.static.refs_0_), channel_id=1, source_target_pairs={{0,4},{1,5},{2,6},{3,7},{4,0},{5,1},{6,2},{7,3},{8,12},{9,13},{10,... | collective-permute-start | bytes 294920 | tf_op jit(solution)/shard_map/ppermute | solution.py:289
  9.5 5.9 %collective-permute-start.1 = (f32[64,384]{1,0:T(8,128)S(1)}, f32[64,384]{1,0:T(8,128)S(1)}, u32[]{:S(2)}, u32[]{:S(2)}) collective-permute-start(f32[64,384]{1,0:T(8,128)S(1)} %shard_map.76), channel_id=1, source_target_pairs={{0,2},{1,3},{2,0},{3,1},{4,6},{5,7},{6,4},{7,5},{8,10},{9,11},{10,... | collective-permute-start | bytes 294920 | tf_op jit(solution)/shard_map/ppermute | solution.py:289
  9.7 5.8 %collective-permute-start.2 = (f32[64,384]{1,0:T(8,128)S(1)}, f32[64,384]{1,0:T(8,128)S(1)}, u32[]{:S(2)}, u32[]{:S(2)}) collective-permute-start(f32[64,384]{1,0:T(8,128)S(1)} %shard_map.76), channel_id=1, source_target_pairs={{0,1},{1,0},{2,3},{3,2},{4,5},{5,4},{6,7},{7,6},{8,9},{9,8},{10,11... | collective-permute-start | bytes 294920 | tf_op jit(solution)/shard_map/ppermute | solution.py:289
  11.6 5.7 %collective-permute-start.7 = (f32[3,64,128]{2,1,0:T(8,128)S(1)}, f32[3,64,128]{2,1,0:T(8,128)S(1)}, u32[]{:S(2)}, u32[]{:S(2)}) collective-permute-start(f32[3,64,128]{2,1,0:T(8,128)S(1)} %shard_map.78.middle), channel_id=1, source_target_pairs={{0,8},{8,0},{16,24},{24,16},{1,9},{9,1},{17,25},{25,17},{2,10},{10... | collective-permute-start | bytes 294920 | tf_op jit(solution)/shard_map/ppermute | solution.py:294
  11.6 5.6 %collective-permute-start.8 = (f32[3,64,128]{2,1,0:T(8,128)S(1)}, f32[3,64,128]{2,1,0:T(8,128)S(1)}, u32[]{:S(2)}, u32[]{:S(2)}) collective-permute-start(f32[3,64,128]{2,1,0:T(8,128)S(1)} %shard_map.78.middle), channel_id=1, source_target_pairs={{0,24},{8,16},{16,8},{24,0},{1,25},{9,17},{17,9},{25,1},{2,26},{10... | collective-permute-start | bytes 294920 | tf_op jit(solution)/shard_map/ppermute | solution.py:295
  15.5 8.3 %collective-permute-start.3 = (f32[2,64,384]{2,1,0:T(8,128)S(1)}, f32[2,64,384]{2,1,0:T(8,128)S(1)}, u32[]{:S(2)}, u32[]{:S(2)}) collective-permute-start(f32[2,64,384]{2,1,0:T(8,128)S(1)} %get-tuple-element.34), channel_id=1, source_target_pairs={{0,1},{1,0},{2,3},{3,2},{4,5},{5,4},{6,7},{7,6},{8,9},{9,8},{10,11... | collective-permute-start | bytes 589832 | tf_op jit(solution)/shard_map/ppermute | solution.py:289
  17.1 8.9 %collective-permute-start.4 = (f32[64,384]{1,0:T(8,128)S(1)}, f32[64,384]{1,0:T(8,128)S(1)}, u32[]{:S(2)}, u32[]{:S(2)}) collective-permute-start(f32[64,384]{1,0:T(8,128)S(1)} %get-tuple-element.33.refs_1_), channel_id=1, source_target_pairs={{0,2},{1,3},{2,0},{3,1},{4,6},{5,7},{6,4},{7,5},{8,10},{9,11},{10,... | collective-permute-start | bytes 294920 | tf_op jit(solution)/shard_map/ppermute | solution.py:289
  17.8 6.0 %collective-permute-start.9 = (f32[2,40,128]{2,1,0:T(8,128)S(1)}, f32[2,40,128]{2,1,0:T(8,128)S(1)}, u32[]{:S(2)}, u32[]{:S(2)}) collective-permute-start(f32[2,40,128]{2,1,0:T(8,128)S(1)} %get-tuple-element.38), channel_id=1, source_target_pairs={{0,6},{1,7},{2,4},{3,5},{4,2},{5,3},{6,0},{7,1},{8,14},{9,15},{10,... | collective-permute-start | bytes 122888 | tf_op jit(solution)/shard_map/ppermute | solution.py:289
  20.3 5.0 %collective-permute-start.11 = (f32[2,40,128]{2,1,0:T(8,128)S(1)}, f32[2,40,128]{2,1,0:T(8,128)S(1)}, u32[]{:S(2)}, u32[]{:S(2)}) collective-permute-start(f32[2,40,128]{2,1,0:T(8,128)S(1)} %get-tuple-element.42), channel_id=1, source_target_pairs={{0,4},{1,5},{2,6},{3,7},{4,0},{5,1},{6,2},{7,3},{8,12},{9,13},{10,... | collective-permute-start | bytes 122888 | tf_op jit(solution)/shard_map/ppermute | solution.py:289
  21.2 4.8 %collective-permute-start.12 = (f32[2,40,128]{2,1,0:T(8,128)S(1)}, f32[2,40,128]{2,1,0:T(8,128)S(1)}, u32[]{:S(2)}, u32[]{:S(2)}) collective-permute-start(f32[2,40,128]{2,1,0:T(8,128)S(1)} %get-tuple-element.43), channel_id=1, source_target_pairs={{0,2},{1,3},{2,0},{3,1},{4,6},{5,7},{6,4},{7,5},{8,10},{9,11},{10,... | collective-permute-start | bytes 122888 | tf_op jit(solution)/shard_map/ppermute | solution.py:289
  23.8 4.7 %collective-permute-start.10 = (f32[64,384]{1,0:T(8,128)S(1)}, f32[64,384]{1,0:T(8,128)S(1)}, u32[]{:S(2)}, u32[]{:S(2)}) collective-permute-start(f32[64,384]{1,0:T(8,128)S(1)} %shard_map.80), channel_id=1, source_target_pairs={{0,2},{1,3},{2,0},{3,1},{4,6},{5,7},{6,4},{7,5},{8,10},{9,11},{10,... | collective-permute-start | bytes 294920 | tf_op jit(solution)/shard_map/ppermute | solution.py:289
  26.0 4.5 %collective-permute-start.13 = (f32[4,40,128]{2,1,0:T(8,128)S(1)}, f32[4,40,128]{2,1,0:T(8,128)S(1)}, u32[]{:S(2)}, u32[]{:S(2)}) collective-permute-start(f32[4,40,128]{2,1,0:T(8,128)S(1)} %shard_map.82), channel_id=1, source_target_pairs={{0,1},{1,0},{2,3},{3,2},{4,5},{5,4},{6,7},{7,6},{8,9},{9,8},{10,11... | collective-permute-start | bytes 245768 | tf_op jit(solution)/shard_map/ppermute | solution.py:289

commit v8 on v7

--- a/solution.py
+++ b/solution.py
@@ -161,11 +161,11 @@
             out[depth:, at + part : at + 2 * part] = matrix[:, :part]
 
 
-def hold_kernel(static, before, out):
+def hold_kernel(static, out):
     out[...] = static[...]
 
 
-def pack_kernel(four, two, one, four_out, pair_out):
+def pack_kernel(four, two, one, base, four_out, pair_out):
     four_out[...] = four[...]
     pair_out[0] = two[...]
     pair_out[1] = four[...]
@@ -176,7 +176,7 @@
     out[...] = value[1]
 
 
-def join_kernel(odd, even, u, row_out):
+def join_kernel(even, odd, u, row_out):
     first = lax.axis_index("box") % 2 == 0
     row_out[0] = jnp.where(first, odd[...], even[...])
     row_out[1] = u[...]
@@ -329,17 +329,17 @@
         high, low, picker, mask, inverse, coupling, cost=COST,
     )
     even, odd = beside(u, "box")
-    (row,) = call(join_kernel, [((3,) + u.shape, F32)], odd, even, u)
-    (static,) = call(hold_kernel, [(static.shape, F32)], static, base, hbm=(1,), cost=COST)
+    (row,) = call(join_kernel, [((3,) + u.shape, F32)], even, odd, u)
+    (static,) = call(hold_kernel, [(static.shape, F32)], static, cost=COST)
     if boxes == 8:
         four = swapped(static, "box", 4)
-        (again,) = call(hold_kernel, [(static.shape, F32)], static, base, hbm=(1,), cost=COST)
+        (again,) = call(hold_kernel, [(static.shape, F32)], static, cost=COST)
         two, one = swapped(again, "box", 2), swapped(again, "box", 1)
         four, pair = call(
-            pack_kernel, [(static.shape, F32), ((2,) + static.shape, F32)], four, two, one, hbm=(2,)
+            pack_kernel, [(static.shape, F32), ((2,) + static.shape, F32)], four, two, one, base, hbm=(2, 3)
         )
         six, others = swapped(four, "box", 2), swapped(pair, "box", 1)
-        early, late, waited = [static, four, two, one, others, six], [], [others, six]
+        early, late, waited = [static, four, two, one, others, six], [], [others]
         offsets = (0, 4, 2, 1, 3, 5, 6, 7)
     else:
         early, late, waited = [static[None]], [], []

time: 32.1 us -> 30.3 us (0.944)
  waiting for transfers between devices: 9.29 us -> 7.47 us
    ppermute x10, waiting for transfers between devices: 9.28 us -> 5.64 us  [swapped(): lax.ppermute(value, axis, [(i, i ^ bit) for i in range(lax.axis_size(axis...]
    ppermute x2, starting transfers between devices: 0.07 us -> 3.1 us  [beside(): even = lax.ppermute(value, axis, [(i, i ^ 1) for i in range(count)])]
    ppermute x2, starting transfers between devices: 7.67 us -> 5.15 us  [beside(): lax.ppermute(value, axis, [(i, (i + 1) % count if i % 2 else (i - 1) % co...]
    ppermute x2, waiting for transfers between devices: 0.01 us -> 1.82 us  [beside(): lax.ppermute(value, axis, [(i, (i + 1) % count if i % 2 else (i - 1) % co...]
    ppermute x10, starting transfers between devices: 10.4 us -> 9.98 us  [swapped(): lax.ppermute(value, axis, [(i, i ^ bit) for i in range(lax.axis_size(axis...]
  transfers between devices with their start and end apart: 14 -> 14, of which waited for: 7 -> 9; matrix products, arithmetic and copies ran while one was open for 0% -> 0% of each run, Pallas kernels for 5% -> 5%
where the time goes in v8:
time: 30.3 us; the launch traced here: 30.2 us
  starting transfers between devices  18.2 us (60%)
  waiting for transfers between devices  7.47 us (25%)
  Pallas kernels  4.37 us (14%)
    ppermute x10, starting transfers between devices, swapped(): lax.ppermute(value, axis, [(i, i ^ bit) for i in range(lax.axis_size(axis...  9.98 us
    ppermute x10, waiting for transfers between devices, swapped(): lax.ppermute(value, axis, [(i, i ^ bit) for i in range(lax.axis_size(axis...  5.64 us
    ppermute x2, starting transfers between devices, beside(): lax.ppermute(value, axis, [(i, (i + 1) % count if i % 2 else (i - 1) % co...  5.15 us
    pallas_call x11, Pallas kernels, call(): pl.pallas_call(kernel, out_shape=[jax.ShapeDtypeStruct(shape, dtype) for...  4.37 us
    ppermute x2, starting transfers between devices, beside(): even = lax.ppermute(value, axis, [(i, i ^ 1) for i in range(count)])  3.1 us
    ppermute x2, waiting for transfers between devices, beside(): lax.ppermute(value, axis, [(i, (i + 1) % count if i % 2 else (i - 1) % co...  1.82 us
  transfers between devices with their start and end apart: 14, of which 9 were waited for; matrix products, arithmetic and copies ran while one was open for 0% of the time, Pallas kernels for 5%

profile of v8, /device:TPU:0, one launch (start us, length us, event | category | flops | bytes accessed | tf_op | source)
XLA Modules:
  0.0 30.2 jit_solution(13676943727606935698)
XLA Ops:
  0.0 1.4 %shard_map.73 = (f32[64,128]{1,0:T(8,128)S(1)}, f32[64,384]{1,0:T(8,128)S(1)}, bf16[128,256]{1,0:T(8,128)(2,1)S(1)}, bf16[128,256]{1,0:T(8,128)(2,1)S(1)}, bf16[...) custom-call(f32[3,128]{1,0:T(4,128)} %points_in.1, ...), custom_call_target="tpu_custom_call" | custom-call | tf_op jit(solution)/shard_map/pallas_call | solution.py:277
  1.4 3.0 %collective-permute-start.5 = (f32[64,128]{1,0:T(8,128)S(1)}, f32[64,128]{1,0:T(8,128)S(1)}, u32[]{:S(2)}, u32[]{:S(2)}) collective-permute-start(f32[64,128]{1,0:T(8,128)S(1)} %get-tuple-element.35.u), channel_id=1, source_target_pairs={{0,1},{1,0},{2,3},{3,2},{4,5},{5,4},{6,7},{7,6},{8,9},{9,8},{10,11... | collective-permute-start | bytes 98312 | tf_op jit(solution)/shard_map/ppermute | solution.py:294
  4.4 3.5 %collective-permute-start.6 = (f32[64,128]{1,0:T(8,128)S(1)}, f32[64,128]{1,0:T(8,128)S(1)}, u32[]{:S(2)}, u32[]{:S(2)}) collective-permute-start(f32[64,128]{1,0:T(8,128)S(1)} %get-tuple-element.35.u), channel_id=1, source_target_pairs={{0,7},{1,2},{2,1},{3,4},{4,3},{5,6},{6,5},{7,0},{8,15},{9,10},{10,... | collective-permute-start | bytes 98312 | tf_op jit(solution)/shard_map/ppermute | solution.py:295
  8.1 1.1 %collective-permute-start.1 = (f32[64,384]{1,0:T(8,128)S(1)}, f32[64,384]{1,0:T(8,128)S(1)}, u32[]{:S(2)}, u32[]{:S(2)}) collective-permute-start(f32[64,384]{1,0:T(8,128)S(1)} %shard_map.75), channel_id=1, source_target_pairs={{0,2},{1,3},{2,0},{3,1},{4,6},{5,7},{6,4},{7,5},{8,10},{9,11},{10,... | collective-permute-start | bytes 294920 | tf_op jit(solution)/shard_map/ppermute | solution.py:289
  9.1 1.3 %collective-permute-start.2 = (f32[64,384]{1,0:T(8,128)S(1)}, f32[64,384]{1,0:T(8,128)S(1)}, u32[]{:S(2)}, u32[]{:S(2)}) collective-permute-start(f32[64,384]{1,0:T(8,128)S(1)} %shard_map.75), channel_id=1, source_target_pairs={{0,1},{1,0},{2,3},{3,2},{4,5},{5,4},{6,7},{7,6},{8,9},{9,8},{10,11... | collective-permute-start | bytes 294920 | tf_op jit(solution)/shard_map/ppermute | solution.py:289
  10.4 1.0 %collective-permute-done.6.odd = f32[64,128]{1,0:T(8,128)S(1)} collective-permute-done((f32[64,128]{1,0:T(8,128)S(1)}, f32[64,128]{1,0:T(8,128)S(1)}, u32[]{:S(2)}, u32[]{:S(2)}) %collective-permute-start.6) | collective-permute-done | bytes 32800 | tf_op jit(solution)/shard_map/ppermute | solution.py:295
  11.5 0.1 collective-permute-start.7
  11.5 1.6 %collective-permute-start.8 = (f32[3,64,128]{2,1,0:T(8,128)S(1)}, f32[3,64,128]{2,1,0:T(8,128)S(1)}, u32[]{:S(2)}, u32[]{:S(2)}) collective-permute-start(f32[3,64,128]{2,1,0:T(8,128)S(1)} %shard_map.78.middle), channel_id=1, source_target_pairs={{0,24},{8,16},{16,8},{24,0},{1,25},{9,17},{17,9},{25,1},{2,26},{10... | collective-permute-start | bytes 294920 | tf_op jit(solution)/shard_map/ppermute | solution.py:295
  13.1 0.8 %shard_map.76 = (f32[128,320]{1,0:T(8,128)S(1)}, bf16[512,320]{1,0:T(8,128)(2,1)S(1)}, bf16[512,320]{1,0:T(8,128)(2,1)S(1)}) custom-call(bf16[128,256]{1,0:T(8,128)(2,1)S(1)} %get-tuple-element.26.high, bf16[128,256]{1,0:T(8,128)(2,1)S(1)} %get-tuple-element.27.low, bf16[128,32]{1,0:T(8,128)(2,1)S(1)} %get-tuple-element.28.picker_in, ...), custom_call_target="tpu_custom_call" | custom-call | flops 10000000000 | bytes 10000000 | tf_op jit(solution)/shard_map/pallas_call | solution.py:277
  14.0 0.5 %collective-permute-done.1.two.refs_2_ = f32[64,384]{1,0:T(8,128)S(1)} collective-permute-done((f32[64,384]{1,0:T(8,128)S(1)}, f32[64,384]{1,0:T(8,128)S(1)}, u32[]{:S(2)}, u32[]{:S(2)}) %collective-permute-start.1) | collective-permute-done | bytes 98336 | tf_op jit(solution)/shard_map/ppermute | solution.py:289
  14.6 0.7 %collective-permute-start.3 = (f32[2,64,384]{2,1,0:T(8,128)S(1)}, f32[2,64,384]{2,1,0:T(8,128)S(1)}, u32[]{:S(2)}, u32[]{:S(2)}) collective-permute-start(f32[2,64,384]{2,1,0:T(8,128)S(1)} %get-tuple-element.34), channel_id=1, source_target_pairs={{0,1},{1,0},{2,3},{3,2},{4,5},{5,4},{6,7},{7,6},{8,9},{9,8},{10,11... | collective-permute-start | bytes 589832 | tf_op jit(solution)/shard_map/ppermute | solution.py:289
  15.3 0.8 %collective-permute-done.8.odd = f32[3,64,128]{2,1,0:T(8,128)S(1)} collective-permute-done((f32[3,64,128]{2,1,0:T(8,128)S(1)}, f32[3,64,128]{2,1,0:T(8,128)S(1)}, u32[]{:S(2)}, u32[]{:S(2)}) %collective-permute-start.8) | collective-permute-done | bytes 98336 | tf_op jit(solution)/shard_map/ppermute | solution.py:295
  16.1 0.5 %shard_map.79 = (f32[2,40,128]{2,1,0:T(8,128)S(1)}, f32[2,40,128]{2,1,0:T(8,128)S(1)}, f32[2,40,128]{2,1,0:T(8,128)S(1)}, f32[2,40,128]{2,1,0:T(8,128)S(1)}) custom-call(f32[3,64,128]{2,1,0:T(8,128)S(1)} %collective-permute-done.7.even, f32[3,64,128]{2,1,0:T(8,128)S(1)} %shard_map.78.middle, f32[3,64,128]{2,1,0:T(8,128)S(1)} %collective-permute-done.8.odd, ...), custom_call_target="tpu_custom_call" | custom-call | flops 10000000000 | bytes 10000000 | tf_op jit(solution)/shard_map/pallas_call | solution.py:277
  16.7 2.4 %collective-permute-start.9 = (f32[2,40,128]{2,1,0:T(8,128)S(1)}, f32[2,40,128]{2,1,0:T(8,128)S(1)}, u32[]{:S(2)}, u32[]{:S(2)}) collective-permute-start(f32[2,40,128]{2,1,0:T(8,128)S(1)} %get-tuple-element.38), channel_id=1, source_target_pairs={{0,6},{1,7},{2,4},{3,5},{4,2},{5,3},{6,0},{7,1},{8,14},{9,15},{10,... | collective-permute-start | bytes 122888 | tf_op jit(solution)/shard_map/ppermute | solution.py:289
  19.1 2.1 %collective-permute-start.12 = (f32[2,40,128]{2,1,0:T(8,128)S(1)}, f32[2,40,128]{2,1,0:T(8,128)S(1)}, u32[]{:S(2)}, u32[]{:S(2)}) collective-permute-start(f32[2,40,128]{2,1,0:T(8,128)S(1)} %get-tuple-element.43), channel_id=1, source_target_pairs={{0,2},{1,3},{2,0},{3,1},{4,6},{5,7},{6,4},{7,5},{8,10},{9,11},{10,... | collective-permute-start | bytes 122888 | tf_op jit(solution)/shard_map/ppermute | solution.py:289
  21.2 1.7 %collective-permute-done.9.refs_0_.refs_3_ = f32[2,40,128]{2,1,0:T(8,128)S(1)} collective-permute-done((f32[2,40,128]{2,1,0:T(8,128)S(1)}, f32[2,40,128]{2,1,0:T(8,128)S(1)}, u32[]{:S(2)}, u32[]{:S(2)}) %collective-permute-start.9) | collective-permute-done | bytes 40992 | tf_op jit(solution)/shard_map/ppermute | solution.py:289
  22.9 0.4 %collective-permute-start.10 = (f32[64,384]{1,0:T(8,128)S(1)}, f32[64,384]{1,0:T(8,128)S(1)}, u32[]{:S(2)}, u32[]{:S(2)}) collective-permute-start(f32[64,384]{1,0:T(8,128)S(1)} %shard_map.80), channel_id=1, source_target_pairs={{0,2},{1,3},{2,0},{3,1},{4,6},{5,7},{6,4},{7,5},{8,10},{9,11},{10,... | collective-permute-start | bytes 294920 | tf_op jit(solution)/shard_map/ppermute | solution.py:289
  23.2 0.9 %collective-permute-done.11.refs_2_.refs_1_ = f32[2,40,128]{2,1,0:T(8,128)S(1)} collective-permute-done((f32[2,40,128]{2,1,0:T(8,128)S(1)}, f32[2,40,128]{2,1,0:T(8,128)S(1)}, u32[]{:S(2)}, u32[]{:S(2)}) %collective-permute-start.11) | collective-permute-done | bytes 40992 | tf_op jit(solution)/shard_map/ppermute | solution.py:289
  24.3 1.9 %collective-permute-start.13 = (f32[4,40,128]{2,1,0:T(8,128)S(1)}, f32[4,40,128]{2,1,0:T(8,128)S(1)}, u32[]{:S(2)}, u32[]{:S(2)}) collective-permute-start(f32[4,40,128]{2,1,0:T(8,128)S(1)} %shard_map.82), channel_id=1, source_target_pairs={{0,1},{1,0},{2,3},{3,2},{4,5},{5,4},{6,7},{7,6},{8,9},{9,8},{10,11... | collective-permute-start | bytes 245768 | tf_op jit(solution)/shard_map/ppermute | solution.py:289
  26.2 0.7 %collective-permute-done.4.refs_5_ = f32[64,384]{1,0:T(8,128)S(1)} collective-permute-done((f32[64,384]{1,0:T(8,128)S(1)}, f32[64,384]{1,0:T(8,128)S(1)}, u32[]{:S(2)}, u32[]{:S(2)}) %collective-permute-start.4) | collective-permute-done | bytes 98336 | tf_op jit(solution)/shard_map/ppermute | solution.py:289
  26.9 1.5 %collective-permute-done.10.refs_6_ = f32[64,384]{1,0:T(8,128)S(1)} collective-permute-done((f32[64,384]{1,0:T(8,128)S(1)}, f32[64,384]{1,0:T(8,128)S(1)}, u32[]{:S(2)}, u32[]{:S(2)}) %collective-permute-start.10) | collective-permute-done | bytes 98336 | tf_op jit(solution)/shard_map/ppermute | solution.py:289
  28.3 0.1 shard_map.81
  28.5 0.3 collective-permute-done.13.refs_4_
  28.8 1.4 %shard_map.83 = f32[2,16,1024]{2,1,0:T(8,128)} custom-call(bf16[512,512]{1,0:T(8,128)(2,1)S(1)} %get-tuple-element.39.top_high, bf16[512,512]{1,0:T(8,128)(2,1)S(1)} %get-tuple-element.40.top_low, bf16[8,192,256]{2,1,0:T(8,128)(2,1)S(1)} %get-tuple-element.41.local, f32[2,40,128]{2,1,0:T(8,128)S(1)} %collective-permute-done.9.refs_0_.refs_3_, ...), custom_call_target="tpu_custom_call" | custom-call | tf_op jit(solution)/shard_map/pallas_call | solution.py:277
  (15 shorter events, 0.2 us)
Async XLA Ops:
  1.4 9.0 %collective-permute-start.5 = (f32[64,128]{1,0:T(8,128)S(1)}, f32[64,128]{1,0:T(8,128)S(1)}, u32[]{:S(2)}, u32[]{:S(2)}) collective-permute-start(f32[64,128]{1,0:T(8,128)S(1)} %get-tuple-element.35.u), channel_id=1, source_target_pairs={{0,1},{1,0},{2,3},{3,2},{4,5},{5,4},{6,7},{7,6},{8,9},{9,8},{10,11... | collective-permute-start | bytes 98312 | tf_op jit(solution)/shard_map/ppermute | solution.py:294
  4.4 7.0 %collective-permute-start.6 = (f32[64,128]{1,0:T(8,128)S(1)}, f32[64,128]{1,0:T(8,128)S(1)}, u32[]{:S(2)}, u32[]{:S(2)}) collective-permute-start(f32[64,128]{1,0:T(8,128)S(1)} %get-tuple-element.35.u), channel_id=1, source_target_pairs={{0,7},{1,2},{2,1},{3,4},{4,3},{5,6},{6,5},{7,0},{8,15},{9,10},{10,... | collective-permute-start | bytes 98312 | tf_op jit(solution)/shard_map/ppermute | solution.py:295
  8.0 6.0 %collective-permute-start = (f32[64,384]{1,0:T(8,128)S(1)}, f32[64,384]{1,0:T(8,128)S(1)}, u32[]{:S(2)}, u32[]{:S(2)}) collective-permute-start(f32[64,384]{1,0:T(8,128)S(1)} %shard_map.74.static.refs_0_), channel_id=1, source_target_pairs={{0,4},{1,5},{2,6},{3,7},{4,0},{5,1},{6,2},{7,3},{8,12},{9,13},{10,... | collective-permute-start | bytes 294920 | tf_op jit(solution)/shard_map/ppermute | solution.py:289
  8.1 6.5 %collective-permute-start.1 = (f32[64,384]{1,0:T(8,128)S(1)}, f32[64,384]{1,0:T(8,128)S(1)}, u32[]{:S(2)}, u32[]{:S(2)}) collective-permute-start(f32[64,384]{1,0:T(8,128)S(1)} %shard_map.75), channel_id=1, source_target_pairs={{0,2},{1,3},{2,0},{3,1},{4,6},{5,7},{6,4},{7,5},{8,10},{9,11},{10,... | collective-permute-start | bytes 294920 | tf_op jit(solution)/shard_map/ppermute | solution.py:289
  9.1 5.4 %collective-permute-start.2 = (f32[64,384]{1,0:T(8,128)S(1)}, f32[64,384]{1,0:T(8,128)S(1)}, u32[]{:S(2)}, u32[]{:S(2)}) collective-permute-start(f32[64,384]{1,0:T(8,128)S(1)} %shard_map.75), channel_id=1, source_target_pairs={{0,1},{1,0},{2,3},{3,2},{4,5},{5,4},{6,7},{7,6},{8,9},{9,8},{10,11... | collective-permute-start | bytes 294920 | tf_op jit(solution)/shard_map/ppermute | solution.py:289
  11.5 3.9 %collective-permute-start.7 = (f32[3,64,128]{2,1,0:T(8,128)S(1)}, f32[3,64,128]{2,1,0:T(8,128)S(1)}, u32[]{:S(2)}, u32[]{:S(2)}) collective-permute-start(f32[3,64,128]{2,1,0:T(8,128)S(1)} %shard_map.78.middle), channel_id=1, source_target_pairs={{0,8},{8,0},{16,24},{24,16},{1,9},{9,1},{17,25},{25,17},{2,10},{10... | collective-permute-start | bytes 294920 | tf_op jit(solution)/shard_map/ppermute | solution.py:294
  11.5 4.6 %collective-permute-start.8 = (f32[3,64,128]{2,1,0:T(8,128)S(1)}, f32[3,64,128]{2,1,0:T(8,128)S(1)}, u32[]{:S(2)}, u32[]{:S(2)}) collective-permute-start(f32[3,64,128]{2,1,0:T(8,128)S(1)} %shard_map.78.middle), channel_id=1, source_target_pairs={{0,24},{8,16},{16,8},{24,0},{1,25},{9,17},{17,9},{25,1},{2,26},{10... | collective-permute-start | bytes 294920 | tf_op jit(solution)/shard_map/ppermute | solution.py:295
  14.6 8.3 %collective-permute-start.3 = (f32[2,64,384]{2,1,0:T(8,128)S(1)}, f32[2,64,384]{2,1,0:T(8,128)S(1)}, u32[]{:S(2)}, u32[]{:S(2)}) collective-permute-start(f32[2,64,384]{2,1,0:T(8,128)S(1)} %get-tuple-element.34), channel_id=1, source_target_pairs={{0,1},{1,0},{2,3},{3,2},{4,5},{5,4},{6,7},{7,6},{8,9},{9,8},{10,11... | collective-permute-start | bytes 589832 | tf_op jit(solution)/shard_map/ppermute | solution.py:289
  16.7 6.2 %collective-permute-start.9 = (f32[2,40,128]{2,1,0:T(8,128)S(1)}, f32[2,40,128]{2,1,0:T(8,128)S(1)}, u32[]{:S(2)}, u32[]{:S(2)}) collective-permute-start(f32[2,40,128]{2,1,0:T(8,128)S(1)} %get-tuple-element.38), channel_id=1, source_target_pairs={{0,6},{1,7},{2,4},{3,5},{4,2},{5,3},{6,0},{7,1},{8,14},{9,15},{10,... | collective-permute-start | bytes 122888 | tf_op jit(solution)/shard_map/ppermute | solution.py:289
  19.1 5.1 %collective-permute-start.11 = (f32[2,40,128]{2,1,0:T(8,128)S(1)}, f32[2,40,128]{2,1,0:T(8,128)S(1)}, u32[]{:S(2)}, u32[]{:S(2)}) collective-permute-start(f32[2,40,128]{2,1,0:T(8,128)S(1)} %get-tuple-element.42), channel_id=1, source_target_pairs={{0,4},{1,5},{2,6},{3,7},{4,0},{5,1},{6,2},{7,3},{8,12},{9,13},{10,... | collective-permute-start | bytes 122888 | tf_op jit(solution)/shard_map/ppermute | solution.py:289
  19.1 5.2 %collective-permute-start.12 = (f32[2,40,128]{2,1,0:T(8,128)S(1)}, f32[2,40,128]{2,1,0:T(8,128)S(1)}, u32[]{:S(2)}, u32[]{:S(2)}) collective-permute-start(f32[2,40,128]{2,1,0:T(8,128)S(1)} %get-tuple-element.43), channel_id=1, source_target_pairs={{0,2},{1,3},{2,0},{3,1},{4,6},{5,7},{6,4},{7,5},{8,10},{9,11},{10,... | collective-permute-start | bytes 122888 | tf_op jit(solution)/shard_map/ppermute | solution.py:289
  21.1 5.7 %collective-permute-start.4 = (f32[64,384]{1,0:T(8,128)S(1)}, f32[64,384]{1,0:T(8,128)S(1)}, u32[]{:S(2)}, u32[]{:S(2)}) collective-permute-start(f32[64,384]{1,0:T(8,128)S(1)} %get-tuple-element.33.refs_1_), channel_id=1, source_target_pairs={{0,2},{1,3},{2,0},{3,1},{4,6},{5,7},{6,4},{7,5},{8,10},{9,11},{10,... | collective-permute-start | bytes 294920 | tf_op jit(solution)/shard_map/ppermute | solution.py:289
  22.9 5.5 %collective-permute-start.10 = (f32[64,384]{1,0:T(8,128)S(1)}, f32[64,384]{1,0:T(8,128)S(1)}, u32[]{:S(2)}, u32[]{:S(2)}) collective-permute-start(f32[64,384]{1,0:T(8,128)S(1)} %shard_map.80), channel_id=1, source_target_pairs={{0,2},{1,3},{2,0},{3,1},{4,6},{5,7},{6,4},{7,5},{8,10},{9,11},{10,... | collective-permute-start | bytes 294920 | tf_op jit(solution)/shard_map/ppermute | solution.py:289
  24.3 4.5 %collective-permute-start.13 = (f32[4,40,128]{2,1,0:T(8,128)S(1)}, f32[4,40,128]{2,1,0:T(8,128)S(1)}, u32[]{:S(2)}, u32[]{:S(2)}) collective-permute-start(f32[4,40,128]{2,1,0:T(8,128)S(1)} %shard_map.82), channel_id=1, source_target_pairs={{0,1},{1,0},{2,3},{3,2},{4,5},{5,4},{6,7},{7,6},{8,9},{9,8},{10,11... | collective-permute-start | bytes 245768 | tf_op jit(solution)/shard_map/ppermute | solution.py:289

commit v9 on v8

--- a/solution.py
+++ b/solution.py
@@ -165,7 +165,7 @@
     out[...] = static[...]
 
 
-def pack_kernel(four, two, one, base, four_out, pair_out):
+def pack_kernel(one, base, four, two, four_out, pair_out):
     four_out[...] = four[...]
     pair_out[0] = two[...]
     pair_out[1] = four[...]
@@ -208,10 +208,10 @@
         outs[k // 2][k % 2] = natural[me ^ k]
 
 
-def forward_kernel(count, *refs):
+def forward_kernel(order, *refs):
     out = refs[-1]
-    for k in range(count):
-        out[k] = refs[k][1]
+    for k, piece in zip(order, refs):
+        out[k] = piece[1]
 
 
 def blocks_of(refs):
@@ -235,8 +235,8 @@
         local_out[k] = stacked_form(parts, rank, depth)
 
 
-def top_kernel(offsets, top_high, top_low, local, *refs):
-    pieces = refs[:-3][::-1]
+def top_kernel(offsets, order, top_high, top_low, local, *refs):
+    pieces = dict(zip(order, refs))
     came, out, packed = refs[-3:]
     boxes = 2 * len(pieces)
     width = came.shape[2]
@@ -332,15 +332,15 @@
     (row,) = call(join_kernel, [((3,) + u.shape, F32)], even, odd, u)
     (static,) = call(hold_kernel, [(static.shape, F32)], static, cost=COST)
     if boxes == 8:
-        four = swapped(static, "box", 4)
+        one = swapped(static, "box", 1)
         (again,) = call(hold_kernel, [(static.shape, F32)], static, cost=COST)
-        two, one = swapped(again, "box", 2), swapped(again, "box", 1)
+        four, two = swapped(again, "box", 4), swapped(again, "box", 2)
         four, pair = call(
-            pack_kernel, [(static.shape, F32), ((2,) + static.shape, F32)], four, two, one, base, hbm=(2, 3)
+            pack_kernel, [(static.shape, F32), ((2,) + static.shape, F32)], one, base, four, two, hbm=(0, 1)
         )
         six, others = swapped(four, "box", 2), swapped(pair, "box", 1)
-        early, late, waited = [static, four, two, one, others, six], [], [others]
-        offsets = (0, 4, 2, 1, 3, 5, 6, 7)
+        early, late, waited = [static, one, four, two, others, six], [], [others]
+        offsets = (0, 1, 4, 2, 3, 5, 6, 7)
     else:
         early, late, waited = [static[None]], [], []
         offsets = [0]
@@ -356,20 +356,22 @@
         even, row, odd, base, matrix_high, matrix_low,
         cost=COST, extra=[pltpu.VMEM((boxes, length, width), F32)],
     )
-    pieces = [swapped(pieces[k], "box", 2 * k) for k in reversed(range(1, boxes // 2))] + [pieces[0]]
+    order = (2, 3, 1) if boxes == 8 else tuple(range(1, boxes // 2))
+    pieces = {0: pieces[0], **{k: swapped(pieces[k], "box", 2 * k) for k in order}}
+    order += (0,)
     (send,) = call(
-        functools.partial(forward_kernel, boxes // 2), [((boxes // 2, length, width), F32)],
-        *pieces[::-1], *waited, hbm=range(boxes // 2, boxes // 2 + len(waited)),
+        functools.partial(forward_kernel, order), [((boxes // 2, length, width), F32)],
+        *[pieces[k] for k in order], *waited, hbm=range(boxes // 2, boxes // 2 + len(waited)),
     )
     came = swapped(send, "box", 1)
     if boxes == 8:
-        (five,) = call(copy_kernel, [(six.shape, F32)], others, pieces[0], hbm=(1,))
+        (five,) = call(copy_kernel, [(six.shape, F32)], others, pieces[order[0]], hbm=(1,))
         late.append(swapped(five, "box", 2))
     top = ((2 * depth, 2 * depth), BF16)
     local = ((boxes, 6 * rank, 2 * width), BF16)
     prepared = call(prepare_kernel, [top, top, local], *early, *late)
     (out,) = call(
-        functools.partial(top_kernel, offsets), [((2, share, boxes * width), F32)], *prepared, *pieces, came,
+        functools.partial(top_kernel, offsets, order), [((2, share, boxes * width), F32)], *prepared, *[pieces[k] for k in order], came,
         extra=[pltpu.VMEM((boxes, share // 2, width), F32)],
     )
     return out

time: 30.3 us -> 30.8 us (1.017)
  waiting for transfers between devices: 7.47 us -> 8.74 us
  starting transfers between devices: 18.2 us -> 17.5 us
    ppermute x10, waiting for transfers between devices: 5.64 us -> 7.91 us  [swapped(): lax.ppermute(value, axis, [(i, i ^ bit) for i in range(lax.axis_size(axis...]
    ppermute x2, waiting for transfers between devices: 1.82 us -> 0.82 us  [beside(): lax.ppermute(value, axis, [(i, (i + 1) % count if i % 2 else (i - 1) % co...]
    ppermute x10, starting transfers between devices: 9.98 us -> 9.21 us  [swapped(): lax.ppermute(value, axis, [(i, i ^ bit) for i in range(lax.axis_size(axis...]
where the time goes in v9:
time: 30.8 us; the launch traced here: 30.7 us
  starting transfers between devices  17.5 us (57%)
  waiting for transfers between devices  8.74 us (28%)
  Pallas kernels  4.39 us (14%)
    ppermute x10, starting transfers between devices, swapped(): lax.ppermute(value, axis, [(i, i ^ bit) for i in range(lax.axis_size(axis...  9.21 us
    ppermute x10, waiting for transfers between devices, swapped(): lax.ppermute(value, axis, [(i, i ^ bit) for i in range(lax.axis_size(axis...  7.91 us
    ppermute x2, starting transfers between devices, beside(): lax.ppermute(value, axis, [(i, (i + 1) % count if i % 2 else (i - 1) % co...  5.14 us
    pallas_call x11, Pallas kernels, call(): pl.pallas_call(kernel, out_shape=[jax.ShapeDtypeStruct(shape, dtype) for...  4.39 us
    ppermute x2, starting transfers between devices, beside(): even = lax.ppermute(value, axis, [(i, i ^ 1) for i in range(count)])  3.1 us
    ppermute x2, waiting for transfers between devices, beside(): lax.ppermute(value, axis, [(i, (i + 1) % count if i % 2 else (i - 1) % co...  0.82 us
  transfers between devices with their start and end apart: 14, of which 9 were waited for; matrix products, arithmetic and copies ran while one was open for 0% of the time, Pallas kernels for 5%

profile of v9, /device:TPU:0, one launch (start us, length us, event | category | flops | bytes accessed | tf_op | source)
XLA Modules:
  0.0 30.7 jit_solution(17256343189790484840)
XLA Ops:
  0.0 1.4 %shard_map.73 = (f32[64,128]{1,0:T(8,128)S(1)}, f32[64,384]{1,0:T(8,128)S(1)}, bf16[128,256]{1,0:T(8,128)(2,1)S(1)}, bf16[128,256]{1,0:T(8,128)(2,1)S(1)}, bf16[...) custom-call(f32[3,128]{1,0:T(4,128)} %points_in.1, ...), custom_call_target="tpu_custom_call" | custom-call | tf_op jit(solution)/shard_map/pallas_call | solution.py:277
  1.4 3.0 %collective-permute-start.5 = (f32[64,128]{1,0:T(8,128)S(1)}, f32[64,128]{1,0:T(8,128)S(1)}, u32[]{:S(2)}, u32[]{:S(2)}) collective-permute-start(f32[64,128]{1,0:T(8,128)S(1)} %get-tuple-element.35.u), channel_id=1, source_target_pairs={{0,1},{1,0},{2,3},{3,2},{4,5},{5,4},{6,7},{7,6},{8,9},{9,8},{10,11... | collective-permute-start | bytes 98312 | tf_op jit(solution)/shard_map/ppermute | solution.py:294
  4.4 3.5 %collective-permute-start.6 = (f32[64,128]{1,0:T(8,128)S(1)}, f32[64,128]{1,0:T(8,128)S(1)}, u32[]{:S(2)}, u32[]{:S(2)}) collective-permute-start(f32[64,128]{1,0:T(8,128)S(1)} %get-tuple-element.35.u), channel_id=1, source_target_pairs={{0,7},{1,2},{2,1},{3,4},{4,3},{5,6},{6,5},{7,0},{8,15},{9,10},{10,... | collective-permute-start | bytes 98312 | tf_op jit(solution)/shard_map/ppermute | solution.py:295
  8.1 2.1 %collective-permute-start.1 = (f32[64,384]{1,0:T(8,128)S(1)}, f32[64,384]{1,0:T(8,128)S(1)}, u32[]{:S(2)}, u32[]{:S(2)}) collective-permute-start(f32[64,384]{1,0:T(8,128)S(1)} %shard_map.76), channel_id=1, source_target_pairs={{0,4},{1,5},{2,6},{3,7},{4,0},{5,1},{6,2},{7,3},{8,12},{9,13},{10,... | collective-permute-start | bytes 294920 | tf_op jit(solution)/shard_map/ppermute | solution.py:289
  10.2 0.2 collective-permute-start.2
  10.4 0.8 %collective-permute-done.6.odd = f32[64,128]{1,0:T(8,128)S(1)} collective-permute-done((f32[64,128]{1,0:T(8,128)S(1)}, f32[64,128]{1,0:T(8,128)S(1)}, u32[]{:S(2)}, u32[]{:S(2)}) %collective-permute-start.6) | collective-permute-done | bytes 32800 | tf_op jit(solution)/shard_map/ppermute | solution.py:295
  11.3 1.6 %collective-permute-start.8 = (f32[3,64,128]{2,1,0:T(8,128)S(1)}, f32[3,64,128]{2,1,0:T(8,128)S(1)}, u32[]{:S(2)}, u32[]{:S(2)}) collective-permute-start(f32[3,64,128]{2,1,0:T(8,128)S(1)} %shard_map.78.middle), channel_id=1, source_target_pairs={{0,24},{8,16},{16,8},{24,0},{1,25},{9,17},{17,9},{25,1},{2,26},{10... | collective-permute-start | bytes 294920 | tf_op jit(solution)/shard_map/ppermute | solution.py:295
  12.9 0.9 %shard_map.75 = (f32[128,320]{1,0:T(8,128)S(1)}, bf16[512,320]{1,0:T(8,128)(2,1)S(1)}, bf16[512,320]{1,0:T(8,128)(2,1)S(1)}) custom-call(bf16[128,256]{1,0:T(8,128)(2,1)S(1)} %get-tuple-element.26.high, bf16[128,256]{1,0:T(8,128)(2,1)S(1)} %get-tuple-element.27.low, bf16[128,32]{1,0:T(8,128)(2,1)S(1)} %get-tuple-element.28.picker_in, ...), custom_call_target="tpu_custom_call" | custom-call | flops 10000000000 | bytes 10000000 | tf_op jit(solution)/shard_map/pallas_call | solution.py:277
  13.8 1.4 %collective-permute-done.1.four = f32[64,384]{1,0:T(8,128)S(1)} collective-permute-done((f32[64,384]{1,0:T(8,128)S(1)}, f32[64,384]{1,0:T(8,128)S(1)}, u32[]{:S(2)}, u32[]{:S(2)}) %collective-permute-start.1) | collective-permute-done | bytes 98336 | tf_op jit(solution)/shard_map/ppermute | solution.py:289
  15.2 0.3 collective-permute-done.2.two.refs_3_
  15.6 0.9 %collective-permute-start.3 = (f32[2,64,384]{2,1,0:T(8,128)S(1)}, f32[2,64,384]{2,1,0:T(8,128)S(1)}, u32[]{:S(2)}, u32[]{:S(2)}) collective-permute-start(f32[2,64,384]{2,1,0:T(8,128)S(1)} %get-tuple-element.34), channel_id=1, source_target_pairs={{0,1},{1,0},{2,3},{3,2},{4,5},{5,4},{6,7},{7,6},{8,9},{9,8},{10,11... | collective-permute-start | bytes 589832 | tf_op jit(solution)/shard_map/ppermute | solution.py:289
  16.5 0.5 %shard_map.79 = (f32[2,40,128]{2,1,0:T(8,128)S(1)}, f32[2,40,128]{2,1,0:T(8,128)S(1)}, f32[2,40,128]{2,1,0:T(8,128)S(1)}, f32[2,40,128]{2,1,0:T(8,128)S(1)}) custom-call(f32[3,64,128]{2,1,0:T(8,128)S(1)} %collective-permute-done.7.even, f32[3,64,128]{2,1,0:T(8,128)S(1)} %shard_map.78.middle, f32[3,64,128]{2,1,0:T(8,128)S(1)} %collective-permute-done.8.odd, ...), custom_call_target="tpu_custom_call" | custom-call | flops 10000000000 | bytes 10000000 | tf_op jit(solution)/shard_map/pallas_call | solution.py:277
  17.0 1.3 %collective-permute-start.9 = (f32[2,40,128]{2,1,0:T(8,128)S(1)}, f32[2,40,128]{2,1,0:T(8,128)S(1)}, u32[]{:S(2)}, u32[]{:S(2)}) collective-permute-start(f32[2,40,128]{2,1,0:T(8,128)S(1)} %get-tuple-element.38), channel_id=1, source_target_pairs={{0,4},{1,5},{2,6},{3,7},{4,0},{5,1},{6,2},{7,3},{8,12},{9,13},{10,... | collective-permute-start | bytes 122888 | tf_op jit(solution)/shard_map/ppermute | solution.py:289
  18.4 1.5 %collective-permute-start.11 = (f32[2,40,128]{2,1,0:T(8,128)S(1)}, f32[2,40,128]{2,1,0:T(8,128)S(1)}, u32[]{:S(2)}, u32[]{:S(2)}) collective-permute-start(f32[2,40,128]{2,1,0:T(8,128)S(1)} %get-tuple-element.42), channel_id=1, source_target_pairs={{0,6},{1,7},{2,4},{3,5},{4,2},{5,3},{6,0},{7,1},{8,14},{9,15},{10,... | collective-permute-start | bytes 122888 | tf_op jit(solution)/shard_map/ppermute | solution.py:289
  19.9 0.7 %collective-permute-start.12 = (f32[2,40,128]{2,1,0:T(8,128)S(1)}, f32[2,40,128]{2,1,0:T(8,128)S(1)}, u32[]{:S(2)}, u32[]{:S(2)}) collective-permute-start(f32[2,40,128]{2,1,0:T(8,128)S(1)} %get-tuple-element.43), channel_id=1, source_target_pairs={{0,2},{1,3},{2,0},{3,1},{4,6},{5,7},{6,4},{7,5},{8,10},{9,11},{10,... | collective-permute-start | bytes 122888 | tf_op jit(solution)/shard_map/ppermute | solution.py:289
  20.6 1.4 %collective-permute-start.4 = (f32[64,384]{1,0:T(8,128)S(1)}, f32[64,384]{1,0:T(8,128)S(1)}, u32[]{:S(2)}, u32[]{:S(2)}) collective-permute-start(f32[64,384]{1,0:T(8,128)S(1)} %get-tuple-element.33.refs_2_), channel_id=1, source_target_pairs={{0,2},{1,3},{2,0},{3,1},{4,6},{5,7},{6,4},{7,5},{8,10},{9,11},{10,... | collective-permute-start | bytes 294920 | tf_op jit(solution)/shard_map/ppermute | solution.py:289
  21.9 1.3 %collective-permute-done.9.refs_0_ = f32[2,40,128]{2,1,0:T(8,128)S(1)} collective-permute-done((f32[2,40,128]{2,1,0:T(8,128)S(1)}, f32[2,40,128]{2,1,0:T(8,128)S(1)}, u32[]{:S(2)}, u32[]{:S(2)}) %collective-permute-start.9) | collective-permute-done | bytes 40992 | tf_op jit(solution)/shard_map/ppermute | solution.py:289
  23.3 1.2 %collective-permute-done.11.refs_1_ = f32[2,40,128]{2,1,0:T(8,128)S(1)} collective-permute-done((f32[2,40,128]{2,1,0:T(8,128)S(1)}, f32[2,40,128]{2,1,0:T(8,128)S(1)}, u32[]{:S(2)}, u32[]{:S(2)}) %collective-permute-start.11) | collective-permute-done | bytes 40992 | tf_op jit(solution)/shard_map/ppermute | solution.py:289
  24.5 0.3 collective-permute-done.12.refs_2_
  24.8 0.9 %collective-permute-start.13 = (f32[4,40,128]{2,1,0:T(8,128)S(1)}, f32[4,40,128]{2,1,0:T(8,128)S(1)}, u32[]{:S(2)}, u32[]{:S(2)}) collective-permute-start(f32[4,40,128]{2,1,0:T(8,128)S(1)} %shard_map.82), channel_id=1, source_target_pairs={{0,1},{1,0},{2,3},{3,2},{4,5},{5,4},{6,7},{7,6},{8,9},{9,8},{10,11... | collective-permute-start | bytes 245768 | tf_op jit(solution)/shard_map/ppermute | solution.py:289
  25.7 1.2 %collective-permute-done.4.refs_5_ = f32[64,384]{1,0:T(8,128)S(1)} collective-permute-done((f32[64,384]{1,0:T(8,128)S(1)}, f32[64,384]{1,0:T(8,128)S(1)}, u32[]{:S(2)}, u32[]{:S(2)}) %collective-permute-start.4) | collective-permute-done | bytes 98336 | tf_op jit(solution)/shard_map/ppermute | solution.py:289
  26.9 1.4 %collective-permute-done.10.refs_6_ = f32[64,384]{1,0:T(8,128)S(1)} collective-permute-done((f32[64,384]{1,0:T(8,128)S(1)}, f32[64,384]{1,0:T(8,128)S(1)}, u32[]{:S(2)}, u32[]{:S(2)}) %collective-permute-start.10) | collective-permute-done | bytes 98336 | tf_op jit(solution)/shard_map/ppermute | solution.py:289
  28.5 0.8 %collective-permute-done.13.refs_4_ = f32[4,40,128]{2,1,0:T(8,128)S(1)} collective-permute-done((f32[4,40,128]{2,1,0:T(8,128)S(1)}, f32[4,40,128]{2,1,0:T(8,128)S(1)}, u32[]{:S(2)}, u32[]{:S(2)}) %collective-permute-start.13) | collective-permute-done | bytes 81952 | tf_op jit(solution)/shard_map/ppermute | solution.py:289
  29.3 1.4 %shard_map.83 = f32[2,16,1024]{2,1,0:T(8,128)} custom-call(bf16[512,512]{1,0:T(8,128)(2,1)S(1)} %get-tuple-element.39.top_high, bf16[512,512]{1,0:T(8,128)(2,1)S(1)} %get-tuple-element.40.top_low, bf16[8,192,256]{2,1,0:T(8,128)(2,1)S(1)} %get-tuple-element.41.local, f32[2,40,128]{2,1,0:T(8,128)S(1)} %collective-permute-done.9.refs_0_, ...), custom_call_target="tpu_custom_call" | custom-call | tf_op jit(solution)/shard_map/pallas_call | solution.py:277
  (15 shorter events, 0.4 us)
Async XLA Ops:
  1.4 9.0 %collective-permute-start.5 = (f32[64,128]{1,0:T(8,128)S(1)}, f32[64,128]{1,0:T(8,128)S(1)}, u32[]{:S(2)}, u32[]{:S(2)}) collective-permute-start(f32[64,128]{1,0:T(8,128)S(1)} %get-tuple-element.35.u), channel_id=1, source_target_pairs={{0,1},{1,0},{2,3},{3,2},{4,5},{5,4},{6,7},{7,6},{8,9},{9,8},{10,11... | collective-permute-start | bytes 98312 | tf_op jit(solution)/shard_map/ppermute | solution.py:294
  4.4 6.8 %collective-permute-start.6 = (f32[64,128]{1,0:T(8,128)S(1)}, f32[64,128]{1,0:T(8,128)S(1)}, u32[]{:S(2)}, u32[]{:S(2)}) collective-permute-start(f32[64,128]{1,0:T(8,128)S(1)} %get-tuple-element.35.u), channel_id=1, source_target_pairs={{0,7},{1,2},{2,1},{3,4},{4,3},{5,6},{6,5},{7,0},{8,15},{9,10},{10,... | collective-permute-start | bytes 98312 | tf_op jit(solution)/shard_map/ppermute | solution.py:295
  8.0 5.8 %collective-permute-start = (f32[64,384]{1,0:T(8,128)S(1)}, f32[64,384]{1,0:T(8,128)S(1)}, u32[]{:S(2)}, u32[]{:S(2)}) collective-permute-start(f32[64,384]{1,0:T(8,128)S(1)} %shard_map.74.static.refs_0_), channel_id=1, source_target_pairs={{0,1},{1,0},{2,3},{3,2},{4,5},{5,4},{6,7},{7,6},{8,9},{9,8},{10,11... | collective-permute-start | bytes 294920 | tf_op jit(solution)/shard_map/ppermute | solution.py:289
  8.1 7.2 %collective-permute-start.1 = (f32[64,384]{1,0:T(8,128)S(1)}, f32[64,384]{1,0:T(8,128)S(1)}, u32[]{:S(2)}, u32[]{:S(2)}) collective-permute-start(f32[64,384]{1,0:T(8,128)S(1)} %shard_map.76), channel_id=1, source_target_pairs={{0,4},{1,5},{2,6},{3,7},{4,0},{5,1},{6,2},{7,3},{8,12},{9,13},{10,... | collective-permute-start | bytes 294920 | tf_op jit(solution)/shard_map/ppermute | solution.py:289
  10.2 5.3 %collective-permute-start.2 = (f32[64,384]{1,0:T(8,128)S(1)}, f32[64,384]{1,0:T(8,128)S(1)}, u32[]{:S(2)}, u32[]{:S(2)}) collective-permute-start(f32[64,384]{1,0:T(8,128)S(1)} %shard_map.76), channel_id=1, source_target_pairs={{0,2},{1,3},{2,0},{3,1},{4,6},{5,7},{6,4},{7,5},{8,10},{9,11},{10,... | collective-permute-start | bytes 294920 | tf_op jit(solution)/shard_map/ppermute | solution.py:289
  11.3 5.2 %collective-permute-start.7 = (f32[3,64,128]{2,1,0:T(8,128)S(1)}, f32[3,64,128]{2,1,0:T(8,128)S(1)}, u32[]{:S(2)}, u32[]{:S(2)}) collective-permute-start(f32[3,64,128]{2,1,0:T(8,128)S(1)} %shard_map.78.middle), channel_id=1, source_target_pairs={{0,8},{8,0},{16,24},{24,16},{1,9},{9,1},{17,25},{25,17},{2,10},{10... | collective-permute-start | bytes 294920 | tf_op jit(solution)/shard_map/ppermute | solution.py:294
  11.3 5.2 %collective-permute-start.8 = (f32[3,64,128]{2,1,0:T(8,128)S(1)}, f32[3,64,128]{2,1,0:T(8,128)S(1)}, u32[]{:S(2)}, u32[]{:S(2)}) collective-permute-start(f32[3,64,128]{2,1,0:T(8,128)S(1)} %shard_map.78.middle), channel_id=1, source_target_pairs={{0,24},{8,16},{16,8},{24,0},{1,25},{9,17},{17,9},{25,1},{2,26},{10... | collective-permute-start | bytes 294920 | tf_op jit(solution)/shard_map/ppermute | solution.py:295
  15.6 7.7 %collective-permute-start.3 = (f32[2,64,384]{2,1,0:T(8,128)S(1)}, f32[2,64,384]{2,1,0:T(8,128)S(1)}, u32[]{:S(2)}, u32[]{:S(2)}) collective-permute-start(f32[2,64,384]{2,1,0:T(8,128)S(1)} %get-tuple-element.34), channel_id=1, source_target_pairs={{0,1},{1,0},{2,3},{3,2},{4,5},{5,4},{6,7},{7,6},{8,9},{9,8},{10,11... | collective-permute-start | bytes 589832 | tf_op jit(solution)/shard_map/ppermute | solution.py:289
  17.0 6.2 %collective-permute-start.9 = (f32[2,40,128]{2,1,0:T(8,128)S(1)}, f32[2,40,128]{2,1,0:T(8,128)S(1)}, u32[]{:S(2)}, u32[]{:S(2)}) collective-permute-start(f32[2,40,128]{2,1,0:T(8,128)S(1)} %get-tuple-element.38), channel_id=1, source_target_pairs={{0,4},{1,5},{2,6},{3,7},{4,0},{5,1},{6,2},{7,3},{8,12},{9,13},{10,... | collective-permute-start | bytes 122888 | tf_op jit(solution)/shard_map/ppermute | solution.py:289
  18.4 6.1 %collective-permute-start.11 = (f32[2,40,128]{2,1,0:T(8,128)S(1)}, f32[2,40,128]{2,1,0:T(8,128)S(1)}, u32[]{:S(2)}, u32[]{:S(2)}) collective-permute-start(f32[2,40,128]{2,1,0:T(8,128)S(1)} %get-tuple-element.42), channel_id=1, source_target_pairs={{0,6},{1,7},{2,4},{3,5},{4,2},{5,3},{6,0},{7,1},{8,14},{9,15},{10,... | collective-permute-start | bytes 122888 | tf_op jit(solution)/shard_map/ppermute | solution.py:289
  19.9 4.9 %collective-permute-start.12 = (f32[2,40,128]{2,1,0:T(8,128)S(1)}, f32[2,40,128]{2,1,0:T(8,128)S(1)}, u32[]{:S(2)}, u32[]{:S(2)}) collective-permute-start(f32[2,40,128]{2,1,0:T(8,128)S(1)} %get-tuple-element.43), channel_id=1, source_target_pairs={{0,2},{1,3},{2,0},{3,1},{4,6},{5,7},{6,4},{7,5},{8,10},{9,11},{10,... | collective-permute-start | bytes 122888 | tf_op jit(solution)/shard_map/ppermute | solution.py:289
  20.6 6.3 %collective-permute-start.4 = (f32[64,384]{1,0:T(8,128)S(1)}, f32[64,384]{1,0:T(8,128)S(1)}, u32[]{:S(2)}, u32[]{:S(2)}) collective-permute-start(f32[64,384]{1,0:T(8,128)S(1)} %get-tuple-element.33.refs_2_), channel_id=1, source_target_pairs={{0,2},{1,3},{2,0},{3,1},{4,6},{5,7},{6,4},{7,5},{8,10},{9,11},{10,... | collective-permute-start | bytes 294920 | tf_op jit(solution)/shard_map/ppermute | solution.py:289
  23.2 5.1 %collective-permute-start.10 = (f32[64,384]{1,0:T(8,128)S(1)}, f32[64,384]{1,0:T(8,128)S(1)}, u32[]{:S(2)}, u32[]{:S(2)}) collective-permute-start(f32[64,384]{1,0:T(8,128)S(1)} %shard_map.80), channel_id=1, source_target_pairs={{0,2},{1,3},{2,0},{3,1},{4,6},{5,7},{6,4},{7,5},{8,10},{9,11},{10,... | collective-permute-start | bytes 294920 | tf_op jit(solution)/shard_map/ppermute | solution.py:289
  24.8 4.4 %collective-permute-start.13 = (f32[4,40,128]{2,1,0:T(8,128)S(1)}, f32[4,40,128]{2,1,0:T(8,128)S(1)}, u32[]{:S(2)}, u32[]{:S(2)}) collective-permute-start(f32[4,40,128]{2,1,0:T(8,128)S(1)} %shard_map.82), channel_id=1, source_target_pairs={{0,1},{1,0},{2,3},{3,2},{4,5},{5,4},{6,7},{7,6},{8,9},{9,8},{10,11... | collective-permute-start | bytes 245768 | tf_op jit(solution)/shard_map/ppermute | solution.py:289

commit v10 on v8

--- a/solution.py
+++ b/solution.py
@@ -176,7 +176,7 @@
     out[...] = value[1]
 
 
-def join_kernel(even, odd, u, row_out):
+def join_kernel(odd, even, u, row_out):
     first = lax.axis_index("box") % 2 == 0
     row_out[0] = jnp.where(first, odd[...], even[...])
     row_out[1] = u[...]
@@ -329,7 +329,7 @@
         high, low, picker, mask, inverse, coupling, cost=COST,
     )
     even, odd = beside(u, "box")
-    (row,) = call(join_kernel, [((3,) + u.shape, F32)], even, odd, u)
+    (row,) = call(join_kernel, [((3,) + u.shape, F32)], odd, even, u)
     (static,) = call(hold_kernel, [(static.shape, F32)], static, cost=COST)
     if boxes == 8:
         four = swapped(static, "box", 4)

time: 30.3 us -> 30.6 us (level)
    ppermute x2, starting transfers between devices: 3.1 us -> 0.07 us  [beside(): even = lax.ppermute(value, axis, [(i, i ^ 1) for i in range(count)])]
    ppermute x2, starting transfers between devices: 5.15 us -> 7.68 us  [beside(): lax.ppermute(value, axis, [(i, (i + 1) % count if i % 2 else (i - 1) % co...]
    ppermute x2, waiting for transfers between devices: 1.82 us -> 0.17 us  [beside(): lax.ppermute(value, axis, [(i, (i + 1) % count if i % 2 else (i - 1) % co...]
    ppermute x2, waiting for transfers between devices: 0.01 us -> 1.03 us  [beside(): even = lax.ppermute(value, axis, [(i, i ^ 1) for i in range(count)])]
    ppermute x10, starting transfers between devices: 9.98 us -> 10.8 us  [swapped(): lax.ppermute(value, axis, [(i, i ^ bit) for i in range(lax.axis_size(axis...]
    ppermute x10, waiting for transfers between devices: 5.64 us -> 6.24 us  [swapped(): lax.ppermute(value, axis, [(i, i ^ bit) for i in range(lax.axis_size(axis...]
where the time goes in v10:
time: 30.6 us; the launch traced here: 30.4 us
  starting transfers between devices  18.5 us (60%)
  waiting for transfers between devices  7.44 us (24%)
  Pallas kernels  4.37 us (14%)
    ppermute x10, starting transfers between devices, swapped(): lax.ppermute(value, axis, [(i, i ^ bit) for i in range(lax.axis_size(axis...  10.8 us
    ppermute x2, starting transfers between devices, beside(): lax.ppermute(value, axis, [(i, (i + 1) % count if i % 2 else (i - 1) % co...  7.68 us
    ppermute x10, waiting for transfers between devices, swapped(): lax.ppermute(value, axis, [(i, i ^ bit) for i in range(lax.axis_size(axis...  6.24 us
    pallas_call x11, Pallas kernels, call(): pl.pallas_call(kernel, out_shape=[jax.ShapeDtypeStruct(shape, dtype) for...  4.37 us
    ppermute x2, waiting for transfers between devices, beside(): even = lax.ppermute(value, axis, [(i, i ^ 1) for i in range(count)])  1.03 us
  transfers between devices with their start and end apart: 14, of which 9 were waited for; matrix products, arithmetic and copies ran while one was open for 0% of the time, Pallas kernels for 5%

profile of v10, /device:TPU:0, one launch (start us, length us, event | category | flops | bytes accessed | tf_op | source)
XLA Modules:
  0.0 30.4 jit_solution(13798583071667740714)
XLA Ops:
  0.0 1.4 %shard_map.73 = (f32[64,128]{1,0:T(8,128)S(1)}, f32[64,384]{1,0:T(8,128)S(1)}, bf16[128,256]{1,0:T(8,128)(2,1)S(1)}, bf16[128,256]{1,0:T(8,128)(2,1)S(1)}, bf16[...) custom-call(f32[3,128]{1,0:T(4,128)} %points_in.1, ...), custom_call_target="tpu_custom_call" | custom-call | tf_op jit(solution)/shard_map/pallas_call | solution.py:277
  1.4 6.1 %collective-permute-start.5 = (f32[64,128]{1,0:T(8,128)S(1)}, f32[64,128]{1,0:T(8,128)S(1)}, u32[]{:S(2)}, u32[]{:S(2)}) collective-permute-start(f32[64,128]{1,0:T(8,128)S(1)} %get-tuple-element.35.u), channel_id=1, source_target_pairs={{0,7},{1,2},{2,1},{3,4},{4,3},{5,6},{6,5},{7,0},{8,15},{9,10},{10,... | collective-permute-start | bytes 98312 | tf_op jit(solution)/shard_map/ppermute | solution.py:295
  7.5 1.1 %collective-permute-start = (f32[64,384]{1,0:T(8,128)S(1)}, f32[64,384]{1,0:T(8,128)S(1)}, u32[]{:S(2)}, u32[]{:S(2)}) collective-permute-start(f32[64,384]{1,0:T(8,128)S(1)} %shard_map.74.static.refs_0_), channel_id=1, source_target_pairs={{0,4},{1,5},{2,6},{3,7},{4,0},{5,1},{6,2},{7,3},{8,12},{9,13},{10,... | collective-permute-start | bytes 294920 | tf_op jit(solution)/shard_map/ppermute | solution.py:289
  8.6 0.2 collective-permute-start.1
  8.8 1.8 %collective-permute-start.2 = (f32[64,384]{1,0:T(8,128)S(1)}, f32[64,384]{1,0:T(8,128)S(1)}, u32[]{:S(2)}, u32[]{:S(2)}) collective-permute-start(f32[64,384]{1,0:T(8,128)S(1)} %shard_map.75), channel_id=1, source_target_pairs={{0,1},{1,0},{2,3},{3,2},{4,5},{5,4},{6,7},{7,6},{8,9},{9,8},{10,11... | collective-permute-start | bytes 294920 | tf_op jit(solution)/shard_map/ppermute | solution.py:289
  10.7 1.0 %collective-permute-done.6.even = f32[64,128]{1,0:T(8,128)S(1)} collective-permute-done((f32[64,128]{1,0:T(8,128)S(1)}, f32[64,128]{1,0:T(8,128)S(1)}, u32[]{:S(2)}, u32[]{:S(2)}) %collective-permute-start.6) | collective-permute-done | bytes 32800 | tf_op jit(solution)/shard_map/ppermute | solution.py:294
  11.7 0.1 collective-permute-start.7
  11.8 1.6 %collective-permute-start.8 = (f32[3,64,128]{2,1,0:T(8,128)S(1)}, f32[3,64,128]{2,1,0:T(8,128)S(1)}, u32[]{:S(2)}, u32[]{:S(2)}) collective-permute-start(f32[3,64,128]{2,1,0:T(8,128)S(1)} %shard_map.78.middle), channel_id=1, source_target_pairs={{0,24},{8,16},{16,8},{24,0},{1,25},{9,17},{17,9},{25,1},{2,26},{10... | collective-permute-start | bytes 294920 | tf_op jit(solution)/shard_map/ppermute | solution.py:295
  13.4 0.8 %shard_map.76 = (f32[128,320]{1,0:T(8,128)S(1)}, bf16[512,320]{1,0:T(8,128)(2,1)S(1)}, bf16[512,320]{1,0:T(8,128)(2,1)S(1)}) custom-call(bf16[128,256]{1,0:T(8,128)(2,1)S(1)} %get-tuple-element.26.high, bf16[128,256]{1,0:T(8,128)(2,1)S(1)} %get-tuple-element.27.low, bf16[128,32]{1,0:T(8,128)(2,1)S(1)} %get-tuple-element.28.picker_in, ...), custom_call_target="tpu_custom_call" | custom-call | flops 10000000000 | bytes 10000000 | tf_op jit(solution)/shard_map/pallas_call | solution.py:277
  14.2 0.3 collective-permute-done.1.two.refs_2_
  14.6 1.6 %collective-permute-start.3 = (f32[2,64,384]{2,1,0:T(8,128)S(1)}, f32[2,64,384]{2,1,0:T(8,128)S(1)}, u32[]{:S(2)}, u32[]{:S(2)}) collective-permute-start(f32[2,64,384]{2,1,0:T(8,128)S(1)} %get-tuple-element.34), channel_id=1, source_target_pairs={{0,1},{1,0},{2,3},{3,2},{4,5},{5,4},{6,7},{7,6},{8,9},{9,8},{10,11... | collective-permute-start | bytes 589832 | tf_op jit(solution)/shard_map/ppermute | solution.py:289
  16.2 0.2 collective-permute-done.8.odd
  16.4 0.5 %shard_map.79 = (f32[2,40,128]{2,1,0:T(8,128)S(1)}, f32[2,40,128]{2,1,0:T(8,128)S(1)}, f32[2,40,128]{2,1,0:T(8,128)S(1)}, f32[2,40,128]{2,1,0:T(8,128)S(1)}) custom-call(f32[3,64,128]{2,1,0:T(8,128)S(1)} %collective-permute-done.7.even, f32[3,64,128]{2,1,0:T(8,128)S(1)} %shard_map.78.middle, f32[3,64,128]{2,1,0:T(8,128)S(1)} %collective-permute-done.8.odd, ...), custom_call_target="tpu_custom_call" | custom-call | flops 10000000000 | bytes 10000000 | tf_op jit(solution)/shard_map/pallas_call | solution.py:277
  16.9 2.5 %collective-permute-start.9 = (f32[2,40,128]{2,1,0:T(8,128)S(1)}, f32[2,40,128]{2,1,0:T(8,128)S(1)}, u32[]{:S(2)}, u32[]{:S(2)}) collective-permute-start(f32[2,40,128]{2,1,0:T(8,128)S(1)} %get-tuple-element.38), channel_id=1, source_target_pairs={{0,6},{1,7},{2,4},{3,5},{4,2},{5,3},{6,0},{7,1},{8,14},{9,15},{10,... | collective-permute-start | bytes 122888 | tf_op jit(solution)/shard_map/ppermute | solution.py:289
  19.4 2.0 %collective-permute-start.12 = (f32[2,40,128]{2,1,0:T(8,128)S(1)}, f32[2,40,128]{2,1,0:T(8,128)S(1)}, u32[]{:S(2)}, u32[]{:S(2)}) collective-permute-start(f32[2,40,128]{2,1,0:T(8,128)S(1)} %get-tuple-element.43), channel_id=1, source_target_pairs={{0,2},{1,3},{2,0},{3,1},{4,6},{5,7},{6,4},{7,5},{8,10},{9,11},{10,... | collective-permute-start | bytes 122888 | tf_op jit(solution)/shard_map/ppermute | solution.py:289
  21.4 1.7 %collective-permute-done.9.refs_0_.refs_3_ = f32[2,40,128]{2,1,0:T(8,128)S(1)} collective-permute-done((f32[2,40,128]{2,1,0:T(8,128)S(1)}, f32[2,40,128]{2,1,0:T(8,128)S(1)}, u32[]{:S(2)}, u32[]{:S(2)}) %collective-permute-start.9) | collective-permute-done | bytes 40992 | tf_op jit(solution)/shard_map/ppermute | solution.py:289
  23.1 0.4 %collective-permute-start.10 = (f32[64,384]{1,0:T(8,128)S(1)}, f32[64,384]{1,0:T(8,128)S(1)}, u32[]{:S(2)}, u32[]{:S(2)}) collective-permute-start(f32[64,384]{1,0:T(8,128)S(1)} %shard_map.80), channel_id=1, source_target_pairs={{0,2},{1,3},{2,0},{3,1},{4,6},{5,7},{6,4},{7,5},{8,10},{9,11},{10,... | collective-permute-start | bytes 294920 | tf_op jit(solution)/shard_map/ppermute | solution.py:289
  23.5 0.9 %collective-permute-done.11.refs_2_.refs_1_ = f32[2,40,128]{2,1,0:T(8,128)S(1)} collective-permute-done((f32[2,40,128]{2,1,0:T(8,128)S(1)}, f32[2,40,128]{2,1,0:T(8,128)S(1)}, u32[]{:S(2)}, u32[]{:S(2)}) %collective-permute-start.11) | collective-permute-done | bytes 40992 | tf_op jit(solution)/shard_map/ppermute | solution.py:289
  24.5 1.1 %collective-permute-start.13 = (f32[4,40,128]{2,1,0:T(8,128)S(1)}, f32[4,40,128]{2,1,0:T(8,128)S(1)}, u32[]{:S(2)}, u32[]{:S(2)}) collective-permute-start(f32[4,40,128]{2,1,0:T(8,128)S(1)} %shard_map.82), channel_id=1, source_target_pairs={{0,1},{1,0},{2,3},{3,2},{4,5},{5,4},{6,7},{7,6},{8,9},{9,8},{10,11... | collective-permute-start | bytes 245768 | tf_op jit(solution)/shard_map/ppermute | solution.py:289
  25.6 1.5 %collective-permute-done.4.refs_5_ = f32[64,384]{1,0:T(8,128)S(1)} collective-permute-done((f32[64,384]{1,0:T(8,128)S(1)}, f32[64,384]{1,0:T(8,128)S(1)}, u32[]{:S(2)}, u32[]{:S(2)}) %collective-permute-start.4) | collective-permute-done | bytes 98336 | tf_op jit(solution)/shard_map/ppermute | solution.py:289
  27.1 1.5 %collective-permute-done.10.refs_6_ = f32[64,384]{1,0:T(8,128)S(1)} collective-permute-done((f32[64,384]{1,0:T(8,128)S(1)}, f32[64,384]{1,0:T(8,128)S(1)}, u32[]{:S(2)}, u32[]{:S(2)}) %collective-permute-start.10) | collective-permute-done | bytes 98336 | tf_op jit(solution)/shard_map/ppermute | solution.py:289
  28.6 0.1 shard_map.81
  28.7 0.3 collective-permute-done.13.refs_4_
  29.0 1.4 %shard_map.83 = f32[2,16,1024]{2,1,0:T(8,128)} custom-call(bf16[512,512]{1,0:T(8,128)(2,1)S(1)} %get-tuple-element.39.top_high, bf16[512,512]{1,0:T(8,128)(2,1)S(1)} %get-tuple-element.40.top_low, bf16[8,192,256]{2,1,0:T(8,128)(2,1)S(1)} %get-tuple-element.41.local, f32[2,40,128]{2,1,0:T(8,128)S(1)} %collective-permute-done.9.refs_0_.refs_3_, ...), custom_call_target="tpu_custom_call" | custom-call | tf_op jit(solution)/shard_map/pallas_call | solution.py:277
  (15 shorter events, 0.2 us)
Async XLA Ops:
  1.4 9.3 %collective-permute-start.5 = (f32[64,128]{1,0:T(8,128)S(1)}, f32[64,128]{1,0:T(8,128)S(1)}, u32[]{:S(2)}, u32[]{:S(2)}) collective-permute-start(f32[64,128]{1,0:T(8,128)S(1)} %get-tuple-element.35.u), channel_id=1, source_target_pairs={{0,7},{1,2},{2,1},{3,4},{4,3},{5,6},{6,5},{7,0},{8,15},{9,10},{10,... | collective-permute-start | bytes 98312 | tf_op jit(solution)/shard_map/ppermute | solution.py:295
  7.5 4.2 %collective-permute-start.6 = (f32[64,128]{1,0:T(8,128)S(1)}, f32[64,128]{1,0:T(8,128)S(1)}, u32[]{:S(2)}, u32[]{:S(2)}) collective-permute-start(f32[64,128]{1,0:T(8,128)S(1)} %get-tuple-element.35.u), channel_id=1, source_target_pairs={{0,1},{1,0},{2,3},{3,2},{4,5},{5,4},{6,7},{7,6},{8,9},{9,8},{10,11... | collective-permute-start | bytes 98312 | tf_op jit(solution)/shard_map/ppermute | solution.py:294
  7.5 6.7 %collective-permute-start = (f32[64,384]{1,0:T(8,128)S(1)}, f32[64,384]{1,0:T(8,128)S(1)}, u32[]{:S(2)}, u32[]{:S(2)}) collective-permute-start(f32[64,384]{1,0:T(8,128)S(1)} %shard_map.74.static.refs_0_), channel_id=1, source_target_pairs={{0,4},{1,5},{2,6},{3,7},{4,0},{5,1},{6,2},{7,3},{8,12},{9,13},{10,... | collective-permute-start | bytes 294920 | tf_op jit(solution)/shard_map/ppermute | solution.py:289
  8.6 5.9 %collective-permute-start.1 = (f32[64,384]{1,0:T(8,128)S(1)}, f32[64,384]{1,0:T(8,128)S(1)}, u32[]{:S(2)}, u32[]{:S(2)}) collective-permute-start(f32[64,384]{1,0:T(8,128)S(1)} %shard_map.75), channel_id=1, source_target_pairs={{0,2},{1,3},{2,0},{3,1},{4,6},{5,7},{6,4},{7,5},{8,10},{9,11},{10,... | collective-permute-start | bytes 294920 | tf_op jit(solution)/shard_map/ppermute | solution.py:289
  8.8 5.7 %collective-permute-start.2 = (f32[64,384]{1,0:T(8,128)S(1)}, f32[64,384]{1,0:T(8,128)S(1)}, u32[]{:S(2)}, u32[]{:S(2)}) collective-permute-start(f32[64,384]{1,0:T(8,128)S(1)} %shard_map.75), channel_id=1, source_target_pairs={{0,1},{1,0},{2,3},{3,2},{4,5},{5,4},{6,7},{7,6},{8,9},{9,8},{10,11... | collective-permute-start | bytes 294920 | tf_op jit(solution)/shard_map/ppermute | solution.py:289
  11.7 4.5 %collective-permute-start.7 = (f32[3,64,128]{2,1,0:T(8,128)S(1)}, f32[3,64,128]{2,1,0:T(8,128)S(1)}, u32[]{:S(2)}, u32[]{:S(2)}) collective-permute-start(f32[3,64,128]{2,1,0:T(8,128)S(1)} %shard_map.78.middle), channel_id=1, source_target_pairs={{0,8},{8,0},{16,24},{24,16},{1,9},{9,1},{17,25},{25,17},{2,10},{10... | collective-permute-start | bytes 294920 | tf_op jit(solution)/shard_map/ppermute | solution.py:294
  11.8 4.6 %collective-permute-start.8 = (f32[3,64,128]{2,1,0:T(8,128)S(1)}, f32[3,64,128]{2,1,0:T(8,128)S(1)}, u32[]{:S(2)}, u32[]{:S(2)}) collective-permute-start(f32[3,64,128]{2,1,0:T(8,128)S(1)} %shard_map.78.middle), channel_id=1, source_target_pairs={{0,24},{8,16},{16,8},{24,0},{1,25},{9,17},{17,9},{25,1},{2,26},{10... | collective-permute-start | bytes 294920 | tf_op jit(solution)/shard_map/ppermute | solution.py:295
  14.6 8.5 %collective-permute-start.3 = (f32[2,64,384]{2,1,0:T(8,128)S(1)}, f32[2,64,384]{2,1,0:T(8,128)S(1)}, u32[]{:S(2)}, u32[]{:S(2)}) collective-permute-start(f32[2,64,384]{2,1,0:T(8,128)S(1)} %get-tuple-element.34), channel_id=1, source_target_pairs={{0,1},{1,0},{2,3},{3,2},{4,5},{5,4},{6,7},{7,6},{8,9},{9,8},{10,11... | collective-permute-start | bytes 589832 | tf_op jit(solution)/shard_map/ppermute | solution.py:289
  16.9 6.2 %collective-permute-start.9 = (f32[2,40,128]{2,1,0:T(8,128)S(1)}, f32[2,40,128]{2,1,0:T(8,128)S(1)}, u32[]{:S(2)}, u32[]{:S(2)}) collective-permute-start(f32[2,40,128]{2,1,0:T(8,128)S(1)} %get-tuple-element.38), channel_id=1, source_target_pairs={{0,6},{1,7},{2,4},{3,5},{4,2},{5,3},{6,0},{7,1},{8,14},{9,15},{10,... | collective-permute-start | bytes 122888 | tf_op jit(solution)/shard_map/ppermute | solution.py:289
  19.4 5.1 %collective-permute-start.11 = (f32[2,40,128]{2,1,0:T(8,128)S(1)}, f32[2,40,128]{2,1,0:T(8,128)S(1)}, u32[]{:S(2)}, u32[]{:S(2)}) collective-permute-start(f32[2,40,128]{2,1,0:T(8,128)S(1)} %get-tuple-element.42), channel_id=1, source_target_pairs={{0,4},{1,5},{2,6},{3,7},{4,0},{5,1},{6,2},{7,3},{8,12},{9,13},{10,... | collective-permute-start | bytes 122888 | tf_op jit(solution)/shard_map/ppermute | solution.py:289
  19.4 5.1 %collective-permute-start.12 = (f32[2,40,128]{2,1,0:T(8,128)S(1)}, f32[2,40,128]{2,1,0:T(8,128)S(1)}, u32[]{:S(2)}, u32[]{:S(2)}) collective-permute-start(f32[2,40,128]{2,1,0:T(8,128)S(1)} %get-tuple-element.43), channel_id=1, source_target_pairs={{0,2},{1,3},{2,0},{3,1},{4,6},{5,7},{6,4},{7,5},{8,10},{9,11},{10,... | collective-permute-start | bytes 122888 | tf_op jit(solution)/shard_map/ppermute | solution.py:289
  21.4 5.7 %collective-permute-start.4 = (f32[64,384]{1,0:T(8,128)S(1)}, f32[64,384]{1,0:T(8,128)S(1)}, u32[]{:S(2)}, u32[]{:S(2)}) collective-permute-start(f32[64,384]{1,0:T(8,128)S(1)} %get-tuple-element.33.refs_1_), channel_id=1, source_target_pairs={{0,2},{1,3},{2,0},{3,1},{4,6},{5,7},{6,4},{7,5},{8,10},{9,11},{10,... | collective-permute-start | bytes 294920 | tf_op jit(solution)/shard_map/ppermute | solution.py:289
  23.1 5.5 %collective-permute-start.10 = (f32[64,384]{1,0:T(8,128)S(1)}, f32[64,384]{1,0:T(8,128)S(1)}, u32[]{:S(2)}, u32[]{:S(2)}) collective-permute-start(f32[64,384]{1,0:T(8,128)S(1)} %shard_map.80), channel_id=1, source_target_pairs={{0,2},{1,3},{2,0},{3,1},{4,6},{5,7},{6,4},{7,5},{8,10},{9,11},{10,... | collective-permute-start | bytes 294920 | tf_op jit(solution)/shard_map/ppermute | solution.py:289
  24.5 4.5 %collective-permute-start.13 = (f32[4,40,128]{2,1,0:T(8,128)S(1)}, f32[4,40,128]{2,1,0:T(8,128)S(1)}, u32[]{:S(2)}, u32[]{:S(2)}) collective-permute-start(f32[4,40,128]{2,1,0:T(8,128)S(1)} %shard_map.82), channel_id=1, source_target_pairs={{0,1},{1,0},{2,3},{3,2},{4,5},{5,4},{6,7},{7,6},{8,9},{9,8},{10,11... | collective-permute-start | bytes 245768 | tf_op jit(solution)/shard_map/ppermute | solution.py:289

commit v11 on v8

--- a/solution.py
+++ b/solution.py
@@ -183,7 +183,7 @@
     row_out[2] = jnp.where(first, even[...], odd[...])
 
 
-def message_kernel(even, middle, odd, base, high, low, *refs):
+def message_kernel(odd, middle, even, base, high, low, *refs):
     outs, natural = refs[:-1], refs[-1]
     first = lax.axis_index("blk") % 2 == 0
     up = jnp.where(first, odd[...], even[...])
@@ -353,7 +353,7 @@
     length = 2 * share + -(-share // 16) * 8
     pieces = call(
         message_kernel, [((2, length, width), F32)] * (boxes // 2),
-        even, row, odd, base, matrix_high, matrix_low,
+        odd, row, even, base, matrix_high, matrix_low,
         cost=COST, extra=[pltpu.VMEM((boxes, length, width), F32)],
     )
     pieces = [swapped(pieces[k], "box", 2 * k) for k in reversed(range(1, boxes // 2))] + [pieces[0]]

time: 30.3 us -> 30.6 us (level)
    ppermute x2, starting transfers between devices: 5.15 us -> 3.61 us  [beside(): lax.ppermute(value, axis, [(i, (i + 1) % count if i % 2 else (i - 1) % co...]
    ppermute x2, starting transfers between devices: 3.1 us -> 4.63 us  [beside(): even = lax.ppermute(value, axis, [(i, i ^ 1) for i in range(count)])]
    ppermute x10, waiting for transfers between devices: 5.64 us -> 5.17 us  [swapped(): lax.ppermute(value, axis, [(i, i ^ bit) for i in range(lax.axis_size(axis...]
    ppermute x2, waiting for transfers between devices: 1.82 us -> 2.26 us  [beside(): lax.ppermute(value, axis, [(i, (i + 1) % count if i % 2 else (i - 1) % co...]
where the time goes in v11:
time: 30.6 us; the launch traced here: 30.4 us
  starting transfers between devices  18.5 us (60%)
  waiting for transfers between devices  7.44 us (24%)
  Pallas kernels  4.39 us (14%)
    ppermute x10, starting transfers between devices, swapped(): lax.ppermute(value, axis, [(i, i ^ bit) for i in range(lax.axis_size(axis...  10.3 us
    ppermute x10, waiting for transfers between devices, swapped(): lax.ppermute(value, axis, [(i, i ^ bit) for i in range(lax.axis_size(axis...  5.17 us
    ppermute x2, starting transfers between devices, beside(): even = lax.ppermute(value, axis, [(i, i ^ 1) for i in range(count)])  4.63 us
    pallas_call x11, Pallas kernels, call(): pl.pallas_call(kernel, out_shape=[jax.ShapeDtypeStruct(shape, dtype) for...  4.39 us
    ppermute x2, starting transfers between devices, beside(): lax.ppermute(value, axis, [(i, (i + 1) % count if i % 2 else (i - 1) % co...  3.61 us
    ppermute x2, waiting for transfers between devices, beside(): lax.ppermute(value, axis, [(i, (i + 1) % count if i % 2 else (i - 1) % co...  2.26 us
  transfers between devices with their start and end apart: 14, of which 9 were waited for; matrix products, arithmetic and copies ran while one was open for 0% of the time, Pallas kernels for 5%

profile of v11, /device:TPU:0, one launch (start us, length us, event | category | flops | bytes accessed | tf_op | source)
XLA Modules:
  0.0 30.4 jit_solution(3583468648448951778)
XLA Ops:
  0.0 1.4 %shard_map.73 = (f32[64,128]{1,0:T(8,128)S(1)}, f32[64,384]{1,0:T(8,128)S(1)}, bf16[128,256]{1,0:T(8,128)(2,1)S(1)}, bf16[128,256]{1,0:T(8,128)(2,1)S(1)}, bf16[...) custom-call(f32[3,128]{1,0:T(4,128)} %points_in.1, ...), custom_call_target="tpu_custom_call" | custom-call | tf_op jit(solution)/shard_map/pallas_call | solution.py:277
  1.4 3.0 %collective-permute-start.5 = (f32[64,128]{1,0:T(8,128)S(1)}, f32[64,128]{1,0:T(8,128)S(1)}, u32[]{:S(2)}, u32[]{:S(2)}) collective-permute-start(f32[64,128]{1,0:T(8,128)S(1)} %get-tuple-element.35.u), channel_id=1, source_target_pairs={{0,1},{1,0},{2,3},{3,2},{4,5},{5,4},{6,7},{7,6},{8,9},{9,8},{10,11... | collective-permute-start | bytes 98312 | tf_op jit(solution)/shard_map/ppermute | solution.py:294
  4.4 3.5 %collective-permute-start.6 = (f32[64,128]{1,0:T(8,128)S(1)}, f32[64,128]{1,0:T(8,128)S(1)}, u32[]{:S(2)}, u32[]{:S(2)}) collective-permute-start(f32[64,128]{1,0:T(8,128)S(1)} %get-tuple-element.35.u), channel_id=1, source_target_pairs={{0,7},{1,2},{2,1},{3,4},{4,3},{5,6},{6,5},{7,0},{8,15},{9,10},{10,... | collective-permute-start | bytes 98312 | tf_op jit(solution)/shard_map/ppermute | solution.py:295
  8.1 1.1 %collective-permute-start.1 = (f32[64,384]{1,0:T(8,128)S(1)}, f32[64,384]{1,0:T(8,128)S(1)}, u32[]{:S(2)}, u32[]{:S(2)}) collective-permute-start(f32[64,384]{1,0:T(8,128)S(1)} %shard_map.75), channel_id=1, source_target_pairs={{0,2},{1,3},{2,0},{3,1},{4,6},{5,7},{6,4},{7,5},{8,10},{9,11},{10,... | collective-permute-start | bytes 294920 | tf_op jit(solution)/shard_map/ppermute | solution.py:289
  9.1 1.3 %collective-permute-start.2 = (f32[64,384]{1,0:T(8,128)S(1)}, f32[64,384]{1,0:T(8,128)S(1)}, u32[]{:S(2)}, u32[]{:S(2)}) collective-permute-start(f32[64,384]{1,0:T(8,128)S(1)} %shard_map.75), channel_id=1, source_target_pairs={{0,1},{1,0},{2,3},{3,2},{4,5},{5,4},{6,7},{7,6},{8,9},{9,8},{10,11... | collective-permute-start | bytes 294920 | tf_op jit(solution)/shard_map/ppermute | solution.py:289
  10.4 1.0 %collective-permute-done.6.odd = f32[64,128]{1,0:T(8,128)S(1)} collective-permute-done((f32[64,128]{1,0:T(8,128)S(1)}, f32[64,128]{1,0:T(8,128)S(1)}, u32[]{:S(2)}, u32[]{:S(2)}) %collective-permute-start.6) | collective-permute-done | bytes 32800 | tf_op jit(solution)/shard_map/ppermute | solution.py:295
  11.5 1.6 %collective-permute-start.8 = (f32[3,64,128]{2,1,0:T(8,128)S(1)}, f32[3,64,128]{2,1,0:T(8,128)S(1)}, u32[]{:S(2)}, u32[]{:S(2)}) collective-permute-start(f32[3,64,128]{2,1,0:T(8,128)S(1)} %shard_map.78.middle), channel_id=1, source_target_pairs={{0,8},{8,0},{16,24},{24,16},{1,9},{9,1},{17,25},{25,17},{2,10},{10... | collective-permute-start | bytes 294920 | tf_op jit(solution)/shard_map/ppermute | solution.py:294
  13.1 0.9 %shard_map.76 = (f32[128,320]{1,0:T(8,128)S(1)}, bf16[512,320]{1,0:T(8,128)(2,1)S(1)}, bf16[512,320]{1,0:T(8,128)(2,1)S(1)}) custom-call(bf16[128,256]{1,0:T(8,128)(2,1)S(1)} %get-tuple-element.26.high, bf16[128,256]{1,0:T(8,128)(2,1)S(1)} %get-tuple-element.27.low, bf16[128,32]{1,0:T(8,128)(2,1)S(1)} %get-tuple-element.28.picker_in, ...), custom_call_target="tpu_custom_call" | custom-call | flops 10000000000 | bytes 10000000 | tf_op jit(solution)/shard_map/pallas_call | solution.py:277
  14.0 0.5 %collective-permute-done.1.two.refs_2_ = f32[64,384]{1,0:T(8,128)S(1)} collective-permute-done((f32[64,384]{1,0:T(8,128)S(1)}, f32[64,384]{1,0:T(8,128)S(1)}, u32[]{:S(2)}, u32[]{:S(2)}) %collective-permute-start.1) | collective-permute-done | bytes 98336 | tf_op jit(solution)/shard_map/ppermute | solution.py:289
  14.6 0.7 %collective-permute-start.3 = (f32[2,64,384]{2,1,0:T(8,128)S(1)}, f32[2,64,384]{2,1,0:T(8,128)S(1)}, u32[]{:S(2)}, u32[]{:S(2)}) collective-permute-start(f32[2,64,384]{2,1,0:T(8,128)S(1)} %get-tuple-element.34), channel_id=1, source_target_pairs={{0,1},{1,0},{2,3},{3,2},{4,5},{5,4},{6,7},{7,6},{8,9},{9,8},{10,11... | collective-permute-start | bytes 589832 | tf_op jit(solution)/shard_map/ppermute | solution.py:289
  15.3 1.3 %collective-permute-done.7.odd = f32[3,64,128]{2,1,0:T(8,128)S(1)} collective-permute-done((f32[3,64,128]{2,1,0:T(8,128)S(1)}, f32[3,64,128]{2,1,0:T(8,128)S(1)}, u32[]{:S(2)}, u32[]{:S(2)}) %collective-permute-start.7) | collective-permute-done | bytes 98336 | tf_op jit(solution)/shard_map/ppermute | solution.py:295
  16.6 0.5 %shard_map.79 = (f32[2,40,128]{2,1,0:T(8,128)S(1)}, f32[2,40,128]{2,1,0:T(8,128)S(1)}, f32[2,40,128]{2,1,0:T(8,128)S(1)}, f32[2,40,128]{2,1,0:T(8,128)S(1)}) custom-call(f32[3,64,128]{2,1,0:T(8,128)S(1)} %collective-permute-done.7.odd, f32[3,64,128]{2,1,0:T(8,128)S(1)} %shard_map.78.middle, f32[3,64,128]{2,1,0:T(8,128)S(1)} %collective-permute-done.8.even, ...), custom_call_target="tpu_custom_call" | custom-call | flops 10000000000 | bytes 10000000 | tf_op jit(solution)/shard_map/pallas_call | solution.py:277
  17.1 2.4 %collective-permute-start.9 = (f32[2,40,128]{2,1,0:T(8,128)S(1)}, f32[2,40,128]{2,1,0:T(8,128)S(1)}, u32[]{:S(2)}, u32[]{:S(2)}) collective-permute-start(f32[2,40,128]{2,1,0:T(8,128)S(1)} %get-tuple-element.38), channel_id=1, source_target_pairs={{0,6},{1,7},{2,4},{3,5},{4,2},{5,3},{6,0},{7,1},{8,14},{9,15},{10,... | collective-permute-start | bytes 122888 | tf_op jit(solution)/shard_map/ppermute | solution.py:289
  19.5 2.1 %collective-permute-start.12 = (f32[2,40,128]{2,1,0:T(8,128)S(1)}, f32[2,40,128]{2,1,0:T(8,128)S(1)}, u32[]{:S(2)}, u32[]{:S(2)}) collective-permute-start(f32[2,40,128]{2,1,0:T(8,128)S(1)} %get-tuple-element.43), channel_id=1, source_target_pairs={{0,2},{1,3},{2,0},{3,1},{4,6},{5,7},{6,4},{7,5},{8,10},{9,11},{10,... | collective-permute-start | bytes 122888 | tf_op jit(solution)/shard_map/ppermute | solution.py:289
  21.6 1.4 %collective-permute-done.9.refs_0_.refs_3_ = f32[2,40,128]{2,1,0:T(8,128)S(1)} collective-permute-done((f32[2,40,128]{2,1,0:T(8,128)S(1)}, f32[2,40,128]{2,1,0:T(8,128)S(1)}, u32[]{:S(2)}, u32[]{:S(2)}) %collective-permute-start.9) | collective-permute-done | bytes 40992 | tf_op jit(solution)/shard_map/ppermute | solution.py:289
  23.0 0.6 %collective-permute-start.10 = (f32[64,384]{1,0:T(8,128)S(1)}, f32[64,384]{1,0:T(8,128)S(1)}, u32[]{:S(2)}, u32[]{:S(2)}) collective-permute-start(f32[64,384]{1,0:T(8,128)S(1)} %shard_map.80), channel_id=1, source_target_pairs={{0,2},{1,3},{2,0},{3,1},{4,6},{5,7},{6,4},{7,5},{8,10},{9,11},{10,... | collective-permute-start | bytes 294920 | tf_op jit(solution)/shard_map/ppermute | solution.py:289
  23.7 0.8 %collective-permute-done.11.refs_2_.refs_1_ = f32[2,40,128]{2,1,0:T(8,128)S(1)} collective-permute-done((f32[2,40,128]{2,1,0:T(8,128)S(1)}, f32[2,40,128]{2,1,0:T(8,128)S(1)}, u32[]{:S(2)}, u32[]{:S(2)}) %collective-permute-start.11) | collective-permute-done | bytes 40992 | tf_op jit(solution)/shard_map/ppermute | solution.py:289
  24.4 0.1 collective-permute-done.12.refs_1_.refs_2_
  24.5 2.0 %collective-permute-start.13 = (f32[4,40,128]{2,1,0:T(8,128)S(1)}, f32[4,40,128]{2,1,0:T(8,128)S(1)}, u32[]{:S(2)}, u32[]{:S(2)}) collective-permute-start(f32[4,40,128]{2,1,0:T(8,128)S(1)} %shard_map.82), channel_id=1, source_target_pairs={{0,1},{1,0},{2,3},{3,2},{4,5},{5,4},{6,7},{7,6},{8,9},{9,8},{10,11... | collective-permute-start | bytes 245768 | tf_op jit(solution)/shard_map/ppermute | solution.py:289
  26.5 0.8 %collective-permute-done.4.refs_5_ = f32[64,384]{1,0:T(8,128)S(1)} collective-permute-done((f32[64,384]{1,0:T(8,128)S(1)}, f32[64,384]{1,0:T(8,128)S(1)}, u32[]{:S(2)}, u32[]{:S(2)}) %collective-permute-start.4) | collective-permute-done | bytes 98336 | tf_op jit(solution)/shard_map/ppermute | solution.py:289
  27.3 1.3 %collective-permute-done.10.refs_6_ = f32[64,384]{1,0:T(8,128)S(1)} collective-permute-done((f32[64,384]{1,0:T(8,128)S(1)}, f32[64,384]{1,0:T(8,128)S(1)}, u32[]{:S(2)}, u32[]{:S(2)}) %collective-permute-start.10) | collective-permute-done | bytes 98336 | tf_op jit(solution)/shard_map/ppermute | solution.py:289
  28.6 0.1 shard_map.81
  28.7 0.3 collective-permute-done.13.refs_4_
  29.0 1.4 %shard_map.83 = f32[2,16,1024]{2,1,0:T(8,128)} custom-call(bf16[512,512]{1,0:T(8,128)(2,1)S(1)} %get-tuple-element.39.top_high, bf16[512,512]{1,0:T(8,128)(2,1)S(1)} %get-tuple-element.40.top_low, bf16[8,192,256]{2,1,0:T(8,128)(2,1)S(1)} %get-tuple-element.41.local, f32[2,40,128]{2,1,0:T(8,128)S(1)} %collective-permute-done.9.refs_0_.refs_3_, ...), custom_call_target="tpu_custom_call" | custom-call | tf_op jit(solution)/shard_map/pallas_call | solution.py:277
  (15 shorter events, 0.2 us)
Async XLA Ops:
  1.4 9.0 %collective-permute-start.5 = (f32[64,128]{1,0:T(8,128)S(1)}, f32[64,128]{1,0:T(8,128)S(1)}, u32[]{:S(2)}, u32[]{:S(2)}) collective-permute-start(f32[64,128]{1,0:T(8,128)S(1)} %get-tuple-element.35.u), channel_id=1, source_target_pairs={{0,1},{1,0},{2,3},{3,2},{4,5},{5,4},{6,7},{7,6},{8,9},{9,8},{10,11... | collective-permute-start | bytes 98312 | tf_op jit(solution)/shard_map/ppermute | solution.py:294
  4.4 7.0 %collective-permute-start.6 = (f32[64,128]{1,0:T(8,128)S(1)}, f32[64,128]{1,0:T(8,128)S(1)}, u32[]{:S(2)}, u32[]{:S(2)}) collective-permute-start(f32[64,128]{1,0:T(8,128)S(1)} %get-tuple-element.35.u), channel_id=1, source_target_pairs={{0,7},{1,2},{2,1},{3,4},{4,3},{5,6},{6,5},{7,0},{8,15},{9,10},{10,... | collective-permute-start | bytes 98312 | tf_op jit(solution)/shard_map/ppermute | solution.py:295
  8.0 6.0 %collective-permute-start = (f32[64,384]{1,0:T(8,128)S(1)}, f32[64,384]{1,0:T(8,128)S(1)}, u32[]{:S(2)}, u32[]{:S(2)}) collective-permute-start(f32[64,384]{1,0:T(8,128)S(1)} %shard_map.74.static.refs_0_), channel_id=1, source_target_pairs={{0,4},{1,5},{2,6},{3,7},{4,0},{5,1},{6,2},{7,3},{8,12},{9,13},{10,... | collective-permute-start | bytes 294920 | tf_op jit(solution)/shard_map/ppermute | solution.py:289
  8.1 6.5 %collective-permute-start.1 = (f32[64,384]{1,0:T(8,128)S(1)}, f32[64,384]{1,0:T(8,128)S(1)}, u32[]{:S(2)}, u32[]{:S(2)}) collective-permute-start(f32[64,384]{1,0:T(8,128)S(1)} %shard_map.75), channel_id=1, source_target_pairs={{0,2},{1,3},{2,0},{3,1},{4,6},{5,7},{6,4},{7,5},{8,10},{9,11},{10,... | collective-permute-start | bytes 294920 | tf_op jit(solution)/shard_map/ppermute | solution.py:289
  9.1 5.4 %collective-permute-start.2 = (f32[64,384]{1,0:T(8,128)S(1)}, f32[64,384]{1,0:T(8,128)S(1)}, u32[]{:S(2)}, u32[]{:S(2)}) collective-permute-start(f32[64,384]{1,0:T(8,128)S(1)} %shard_map.75), channel_id=1, source_target_pairs={{0,1},{1,0},{2,3},{3,2},{4,5},{5,4},{6,7},{7,6},{8,9},{9,8},{10,11... | collective-permute-start | bytes 294920 | tf_op jit(solution)/shard_map/ppermute | solution.py:289
  11.5 5.1 %collective-permute-start.7 = (f32[3,64,128]{2,1,0:T(8,128)S(1)}, f32[3,64,128]{2,1,0:T(8,128)S(1)}, u32[]{:S(2)}, u32[]{:S(2)}) collective-permute-start(f32[3,64,128]{2,1,0:T(8,128)S(1)} %shard_map.78.middle), channel_id=1, source_target_pairs={{0,24},{8,16},{16,8},{24,0},{1,25},{9,17},{17,9},{25,1},{2,26},{10... | collective-permute-start | bytes 294920 | tf_op jit(solution)/shard_map/ppermute | solution.py:295
  11.5 5.0 %collective-permute-start.8 = (f32[3,64,128]{2,1,0:T(8,128)S(1)}, f32[3,64,128]{2,1,0:T(8,128)S(1)}, u32[]{:S(2)}, u32[]{:S(2)}) collective-permute-start(f32[3,64,128]{2,1,0:T(8,128)S(1)} %shard_map.78.middle), channel_id=1, source_target_pairs={{0,8},{8,0},{16,24},{24,16},{1,9},{9,1},{17,25},{25,17},{2,10},{10... | collective-permute-start | bytes 294920 | tf_op jit(solution)/shard_map/ppermute | solution.py:294
  14.6 8.4 %collective-permute-start.3 = (f32[2,64,384]{2,1,0:T(8,128)S(1)}, f32[2,64,384]{2,1,0:T(8,128)S(1)}, u32[]{:S(2)}, u32[]{:S(2)}) collective-permute-start(f32[2,64,384]{2,1,0:T(8,128)S(1)} %get-tuple-element.34), channel_id=1, source_target_pairs={{0,1},{1,0},{2,3},{3,2},{4,5},{5,4},{6,7},{7,6},{8,9},{9,8},{10,11... | collective-permute-start | bytes 589832 | tf_op jit(solution)/shard_map/ppermute | solution.py:289
  17.1 5.9 %collective-permute-start.9 = (f32[2,40,128]{2,1,0:T(8,128)S(1)}, f32[2,40,128]{2,1,0:T(8,128)S(1)}, u32[]{:S(2)}, u32[]{:S(2)}) collective-permute-start(f32[2,40,128]{2,1,0:T(8,128)S(1)} %get-tuple-element.38), channel_id=1, source_target_pairs={{0,6},{1,7},{2,4},{3,5},{4,2},{5,3},{6,0},{7,1},{8,14},{9,15},{10,... | collective-permute-start | bytes 122888 | tf_op jit(solution)/shard_map/ppermute | solution.py:289
  19.5 4.9 %collective-permute-start.11 = (f32[2,40,128]{2,1,0:T(8,128)S(1)}, f32[2,40,128]{2,1,0:T(8,128)S(1)}, u32[]{:S(2)}, u32[]{:S(2)}) collective-permute-start(f32[2,40,128]{2,1,0:T(8,128)S(1)} %get-tuple-element.42), channel_id=1, source_target_pairs={{0,4},{1,5},{2,6},{3,7},{4,0},{5,1},{6,2},{7,3},{8,12},{9,13},{10,... | collective-permute-start | bytes 122888 | tf_op jit(solution)/shard_map/ppermute | solution.py:289
  19.5 5.1 %collective-permute-start.12 = (f32[2,40,128]{2,1,0:T(8,128)S(1)}, f32[2,40,128]{2,1,0:T(8,128)S(1)}, u32[]{:S(2)}, u32[]{:S(2)}) collective-permute-start(f32[2,40,128]{2,1,0:T(8,128)S(1)} %get-tuple-element.43), channel_id=1, source_target_pairs={{0,2},{1,3},{2,0},{3,1},{4,6},{5,7},{6,4},{7,5},{8,10},{9,11},{10,... | collective-permute-start | bytes 122888 | tf_op jit(solution)/shard_map/ppermute | solution.py:289
  21.6 5.7 %collective-permute-start.4 = (f32[64,384]{1,0:T(8,128)S(1)}, f32[64,384]{1,0:T(8,128)S(1)}, u32[]{:S(2)}, u32[]{:S(2)}) collective-permute-start(f32[64,384]{1,0:T(8,128)S(1)} %get-tuple-element.33.refs_1_), channel_id=1, source_target_pairs={{0,2},{1,3},{2,0},{3,1},{4,6},{5,7},{6,4},{7,5},{8,10},{9,11},{10,... | collective-permute-start | bytes 294920 | tf_op jit(solution)/shard_map/ppermute | solution.py:289
  23.0 5.6 %collective-permute-start.10 = (f32[64,384]{1,0:T(8,128)S(1)}, f32[64,384]{1,0:T(8,128)S(1)}, u32[]{:S(2)}, u32[]{:S(2)}) collective-permute-start(f32[64,384]{1,0:T(8,128)S(1)} %shard_map.80), channel_id=1, source_target_pairs={{0,2},{1,3},{2,0},{3,1},{4,6},{5,7},{6,4},{7,5},{8,10},{9,11},{10,... | collective-permute-start | bytes 294920 | tf_op jit(solution)/shard_map/ppermute | solution.py:289
  24.5 4.5 %collective-permute-start.13 = (f32[4,40,128]{2,1,0:T(8,128)S(1)}, f32[4,40,128]{2,1,0:T(8,128)S(1)}, u32[]{:S(2)}, u32[]{:S(2)}) collective-permute-start(f32[4,40,128]{2,1,0:T(8,128)S(1)} %shard_map.82), channel_id=1, source_target_pairs={{0,1},{1,0},{2,3},{3,2},{4,5},{5,4},{6,7},{7,6},{8,9},{9,8},{10,11... | collective-permute-start | bytes 245768 | tf_op jit(solution)/shard_map/ppermute | solution.py:289

commit v12 on v8

--- a/solution.py
+++ b/solution.py
@@ -339,7 +339,7 @@
             pack_kernel, [(static.shape, F32), ((2,) + static.shape, F32)], four, two, one, base, hbm=(2, 3)
         )
         six, others = swapped(four, "box", 2), swapped(pair, "box", 1)
-        early, late, waited = [static, four, two, one, others, six], [], [others]
+        early, late, waited = [static, four, two, one, others, six], [], [others, six]
         offsets = (0, 4, 2, 1, 3, 5, 6, 7)
     else:
         early, late, waited = [static[None]], [], []

time: 30.3 us -> 30.5 us (level)
  starting transfers between devices: 18.2 us -> 19.3 us
  waiting for transfers between devices: 7.47 us -> 6.58 us
    ppermute x10, starting transfers between devices: 9.98 us -> 11 us  [swapped(): lax.ppermute(value, axis, [(i, i ^ bit) for i in range(lax.axis_size(axis...]
    ppermute x2, waiting for transfers between devices: 1.82 us -> 1.01 us  [beside(): lax.ppermute(value, axis, [(i, (i + 1) % count if i % 2 else (i - 1) % co...]
  transfers between devices with their start and end apart: 14 -> 14, of which waited for: 9 -> 7; matrix products, arithmetic and copies ran while one was open for 0% -> 0% of each run, Pallas kernels for 5% -> 5%
where the time goes in v12:
time: 30.5 us; the launch traced here: 30.3 us
  starting transfers between devices  19.3 us (63%)
  waiting for transfers between devices  6.58 us (22%)
  Pallas kernels  4.38 us (14%)
    ppermute x10, starting transfers between devices, swapped(): lax.ppermute(value, axis, [(i, i ^ bit) for i in range(lax.axis_size(axis...  11 us
    ppermute x10, waiting for transfers between devices, swapped(): lax.ppermute(value, axis, [(i, i ^ bit) for i in range(lax.axis_size(axis...  5.56 us
    ppermute x2, starting transfers between devices, beside(): lax.ppermute(value, axis, [(i, (i + 1) % count if i % 2 else (i - 1) % co...  5.15 us
    pallas_call x11, Pallas kernels, call(): pl.pallas_call(kernel, out_shape=[jax.ShapeDtypeStruct(shape, dtype) for...  4.38 us
    ppermute x2, starting transfers between devices, beside(): even = lax.ppermute(value, axis, [(i, i ^ 1) for i in range(count)])  3.1 us
    ppermute x2, waiting for transfers between devices, beside(): lax.ppermute(value, axis, [(i, (i + 1) % count if i % 2 else (i - 1) % co...  1.01 us
  transfers between devices with their start and end apart: 14, of which 7 were waited for; matrix products, arithmetic and copies ran while one was open for 0% of the time, Pallas kernels for 5%

profile of v12, /device:TPU:0, one launch (start us, length us, event | category | flops | bytes accessed | tf_op | source)
XLA Modules:
  0.0 30.3 jit_solution(2481803623901833699)
XLA Ops:
  0.0 1.4 %shard_map.73 = (f32[64,128]{1,0:T(8,128)S(1)}, f32[64,384]{1,0:T(8,128)S(1)}, bf16[128,256]{1,0:T(8,128)(2,1)S(1)}, bf16[128,256]{1,0:T(8,128)(2,1)S(1)}, bf16[...) custom-call(f32[3,128]{1,0:T(4,128)} %points_in.1, ...), custom_call_target="tpu_custom_call" | custom-call | tf_op jit(solution)/shard_map/pallas_call | solution.py:277
  1.4 3.0 %collective-permute-start.5 = (f32[64,128]{1,0:T(8,128)S(1)}, f32[64,128]{1,0:T(8,128)S(1)}, u32[]{:S(2)}, u32[]{:S(2)}) collective-permute-start(f32[64,128]{1,0:T(8,128)S(1)} %get-tuple-element.35.u), channel_id=1, source_target_pairs={{0,1},{1,0},{2,3},{3,2},{4,5},{5,4},{6,7},{7,6},{8,9},{9,8},{10,11... | collective-permute-start | bytes 98312 | tf_op jit(solution)/shard_map/ppermute | solution.py:294
  4.4 3.5 %collective-permute-start.6 = (f32[64,128]{1,0:T(8,128)S(1)}, f32[64,128]{1,0:T(8,128)S(1)}, u32[]{:S(2)}, u32[]{:S(2)}) collective-permute-start(f32[64,128]{1,0:T(8,128)S(1)} %get-tuple-element.35.u), channel_id=1, source_target_pairs={{0,7},{1,2},{2,1},{3,4},{4,3},{5,6},{6,5},{7,0},{8,15},{9,10},{10,... | collective-permute-start | bytes 98312 | tf_op jit(solution)/shard_map/ppermute | solution.py:295
  8.1 1.1 %collective-permute-start.1 = (f32[64,384]{1,0:T(8,128)S(1)}, f32[64,384]{1,0:T(8,128)S(1)}, u32[]{:S(2)}, u32[]{:S(2)}) collective-permute-start(f32[64,384]{1,0:T(8,128)S(1)} %shard_map.75), channel_id=1, source_target_pairs={{0,2},{1,3},{2,0},{3,1},{4,6},{5,7},{6,4},{7,5},{8,10},{9,11},{10,... | collective-permute-start | bytes 294920 | tf_op jit(solution)/shard_map/ppermute | solution.py:289
  9.1 1.3 %collective-permute-start.2 = (f32[64,384]{1,0:T(8,128)S(1)}, f32[64,384]{1,0:T(8,128)S(1)}, u32[]{:S(2)}, u32[]{:S(2)}) collective-permute-start(f32[64,384]{1,0:T(8,128)S(1)} %shard_map.75), channel_id=1, source_target_pairs={{0,1},{1,0},{2,3},{3,2},{4,5},{5,4},{6,7},{7,6},{8,9},{9,8},{10,11... | collective-permute-start | bytes 294920 | tf_op jit(solution)/shard_map/ppermute | solution.py:289
  10.4 1.0 %collective-permute-done.6.odd = f32[64,128]{1,0:T(8,128)S(1)} collective-permute-done((f32[64,128]{1,0:T(8,128)S(1)}, f32[64,128]{1,0:T(8,128)S(1)}, u32[]{:S(2)}, u32[]{:S(2)}) %collective-permute-start.6) | collective-permute-done | bytes 32800 | tf_op jit(solution)/shard_map/ppermute | solution.py:295
  11.5 1.6 %collective-permute-start.8 = (f32[3,64,128]{2,1,0:T(8,128)S(1)}, f32[3,64,128]{2,1,0:T(8,128)S(1)}, u32[]{:S(2)}, u32[]{:S(2)}) collective-permute-start(f32[3,64,128]{2,1,0:T(8,128)S(1)} %shard_map.78.middle), channel_id=1, source_target_pairs={{0,24},{8,16},{16,8},{24,0},{1,25},{9,17},{17,9},{25,1},{2,26},{10... | collective-permute-start | bytes 294920 | tf_op jit(solution)/shard_map/ppermute | solution.py:295
  13.1 0.8 %shard_map.76 = (f32[128,320]{1,0:T(8,128)S(1)}, bf16[512,320]{1,0:T(8,128)(2,1)S(1)}, bf16[512,320]{1,0:T(8,128)(2,1)S(1)}) custom-call(bf16[128,256]{1,0:T(8,128)(2,1)S(1)} %get-tuple-element.26.high, bf16[128,256]{1,0:T(8,128)(2,1)S(1)} %get-tuple-element.27.low, bf16[128,32]{1,0:T(8,128)(2,1)S(1)} %get-tuple-element.28.picker_in, ...), custom_call_target="tpu_custom_call" | custom-call | flops 10000000000 | bytes 10000000 | tf_op jit(solution)/shard_map/pallas_call | solution.py:277
  14.0 0.5 %collective-permute-done.1.two.refs_2_ = f32[64,384]{1,0:T(8,128)S(1)} collective-permute-done((f32[64,384]{1,0:T(8,128)S(1)}, f32[64,384]{1,0:T(8,128)S(1)}, u32[]{:S(2)}, u32[]{:S(2)}) %collective-permute-start.1) | collective-permute-done | bytes 98336 | tf_op jit(solution)/shard_map/ppermute | solution.py:289
  14.6 0.7 %collective-permute-start.3 = (f32[2,64,384]{2,1,0:T(8,128)S(1)}, f32[2,64,384]{2,1,0:T(8,128)S(1)}, u32[]{:S(2)}, u32[]{:S(2)}) collective-permute-start(f32[2,64,384]{2,1,0:T(8,128)S(1)} %get-tuple-element.34), channel_id=1, source_target_pairs={{0,1},{1,0},{2,3},{3,2},{4,5},{5,4},{6,7},{7,6},{8,9},{9,8},{10,11... | collective-permute-start | bytes 589832 | tf_op jit(solution)/shard_map/ppermute | solution.py:289
  15.3 1.6 %collective-permute-start.4 = (f32[64,384]{1,0:T(8,128)S(1)}, f32[64,384]{1,0:T(8,128)S(1)}, u32[]{:S(2)}, u32[]{:S(2)}) collective-permute-start(f32[64,384]{1,0:T(8,128)S(1)} %get-tuple-element.33.refs_1_), channel_id=1, source_target_pairs={{0,2},{1,3},{2,0},{3,1},{4,6},{5,7},{6,4},{7,5},{8,10},{9,11},{10,... | collective-permute-start | bytes 294920 | tf_op jit(solution)/shard_map/ppermute | solution.py:289
  16.9 0.5 %shard_map.79 = (f32[2,40,128]{2,1,0:T(8,128)S(1)}, f32[2,40,128]{2,1,0:T(8,128)S(1)}, f32[2,40,128]{2,1,0:T(8,128)S(1)}, f32[2,40,128]{2,1,0:T(8,128)S(1)}) custom-call(f32[3,64,128]{2,1,0:T(8,128)S(1)} %collective-permute-done.7.even, f32[3,64,128]{2,1,0:T(8,128)S(1)} %shard_map.78.middle, f32[3,64,128]{2,1,0:T(8,128)S(1)} %collective-permute-done.8.odd, ...), custom_call_target="tpu_custom_call" | custom-call | flops 10000000000 | bytes 10000000 | tf_op jit(solution)/shard_map/pallas_call | solution.py:277
  17.5 1.6 %collective-permute-start.9 = (f32[2,40,128]{2,1,0:T(8,128)S(1)}, f32[2,40,128]{2,1,0:T(8,128)S(1)}, u32[]{:S(2)}, u32[]{:S(2)}) collective-permute-start(f32[2,40,128]{2,1,0:T(8,128)S(1)} %get-tuple-element.38), channel_id=1, source_target_pairs={{0,6},{1,7},{2,4},{3,5},{4,2},{5,3},{6,0},{7,1},{8,14},{9,15},{10,... | collective-permute-start | bytes 122888 | tf_op jit(solution)/shard_map/ppermute | solution.py:289
  19.1 0.4 %collective-permute-start.11 = (f32[2,40,128]{2,1,0:T(8,128)S(1)}, f32[2,40,128]{2,1,0:T(8,128)S(1)}, u32[]{:S(2)}, u32[]{:S(2)}) collective-permute-start(f32[2,40,128]{2,1,0:T(8,128)S(1)} %get-tuple-element.42), channel_id=1, source_target_pairs={{0,4},{1,5},{2,6},{3,7},{4,0},{5,1},{6,2},{7,3},{8,12},{9,13},{10,... | collective-permute-start | bytes 122888 | tf_op jit(solution)/shard_map/ppermute | solution.py:289
  19.5 2.4 %collective-permute-start.12 = (f32[2,40,128]{2,1,0:T(8,128)S(1)}, f32[2,40,128]{2,1,0:T(8,128)S(1)}, u32[]{:S(2)}, u32[]{:S(2)}) collective-permute-start(f32[2,40,128]{2,1,0:T(8,128)S(1)} %get-tuple-element.43), channel_id=1, source_target_pairs={{0,2},{1,3},{2,0},{3,1},{4,6},{5,7},{6,4},{7,5},{8,10},{9,11},{10,... | collective-permute-start | bytes 122888 | tf_op jit(solution)/shard_map/ppermute | solution.py:289
  21.9 1.5 %collective-permute-done.9.refs_0_.refs_3_ = f32[2,40,128]{2,1,0:T(8,128)S(1)} collective-permute-done((f32[2,40,128]{2,1,0:T(8,128)S(1)}, f32[2,40,128]{2,1,0:T(8,128)S(1)}, u32[]{:S(2)}, u32[]{:S(2)}) %collective-permute-start.9) | collective-permute-done | bytes 40992 | tf_op jit(solution)/shard_map/ppermute | solution.py:289
  23.5 0.1 collective-permute-start.10
  23.5 0.5 %collective-permute-done.11.refs_2_.refs_1_ = f32[2,40,128]{2,1,0:T(8,128)S(1)} collective-permute-done((f32[2,40,128]{2,1,0:T(8,128)S(1)}, f32[2,40,128]{2,1,0:T(8,128)S(1)}, u32[]{:S(2)}, u32[]{:S(2)}) %collective-permute-start.11) | collective-permute-done | bytes 40992 | tf_op jit(solution)/shard_map/ppermute | solution.py:289
  24.1 0.3 %collective-permute-done.12.refs_1_.refs_2_ = f32[2,40,128]{2,1,0:T(8,128)S(1)} collective-permute-done((f32[2,40,128]{2,1,0:T(8,128)S(1)}, f32[2,40,128]{2,1,0:T(8,128)S(1)}, u32[]{:S(2)}, u32[]{:S(2)}) %collective-permute-start.12) | collective-permute-done | bytes 40992 | tf_op jit(solution)/shard_map/ppermute | solution.py:289
  24.4 1.7 %collective-permute-start.13 = (f32[4,40,128]{2,1,0:T(8,128)S(1)}, f32[4,40,128]{2,1,0:T(8,128)S(1)}, u32[]{:S(2)}, u32[]{:S(2)}) collective-permute-start(f32[4,40,128]{2,1,0:T(8,128)S(1)} %shard_map.82), channel_id=1, source_target_pairs={{0,1},{1,0},{2,3},{3,2},{4,5},{5,4},{6,7},{7,6},{8,9},{9,8},{10,11... | collective-permute-start | bytes 245768 | tf_op jit(solution)/shard_map/ppermute | solution.py:289
  26.1 2.0 %collective-permute-done.10.refs_6_ = f32[64,384]{1,0:T(8,128)S(1)} collective-permute-done((f32[64,384]{1,0:T(8,128)S(1)}, f32[64,384]{1,0:T(8,128)S(1)}, u32[]{:S(2)}, u32[]{:S(2)}) %collective-permute-start.10) | collective-permute-done | bytes 98336 | tf_op jit(solution)/shard_map/ppermute | solution.py:289
  28.1 0.1 shard_map.81
  28.3 0.6 %collective-permute-done.13.refs_4_ = f32[4,40,128]{2,1,0:T(8,128)S(1)} collective-permute-done((f32[4,40,128]{2,1,0:T(8,128)S(1)}, f32[4,40,128]{2,1,0:T(8,128)S(1)}, u32[]{:S(2)}, u32[]{:S(2)}) %collective-permute-start.13) | collective-permute-done | bytes 81952 | tf_op jit(solution)/shard_map/ppermute | solution.py:289
  28.9 1.4 %shard_map.83 = f32[2,16,1024]{2,1,0:T(8,128)} custom-call(bf16[512,512]{1,0:T(8,128)(2,1)S(1)} %get-tuple-element.39.top_high, bf16[512,512]{1,0:T(8,128)(2,1)S(1)} %get-tuple-element.40.top_low, bf16[8,192,256]{2,1,0:T(8,128)(2,1)S(1)} %get-tuple-element.41.local, f32[2,40,128]{2,1,0:T(8,128)S(1)} %collective-permute-done.9.refs_0_.refs_3_, ...), custom_call_target="tpu_custom_call" | custom-call | tf_op jit(solution)/shard_map/pallas_call | solution.py:277
  (15 shorter events, 0.2 us)
Async XLA Ops:
  1.4 9.0 %collective-permute-start.5 = (f32[64,128]{1,0:T(8,128)S(1)}, f32[64,128]{1,0:T(8,128)S(1)}, u32[]{:S(2)}, u32[]{:S(2)}) collective-permute-start(f32[64,128]{1,0:T(8,128)S(1)} %get-tuple-element.35.u), channel_id=1, source_target_pairs={{0,1},{1,0},{2,3},{3,2},{4,5},{5,4},{6,7},{7,6},{8,9},{9,8},{10,11... | collective-permute-start | bytes 98312 | tf_op jit(solution)/shard_map/ppermute | solution.py:294
  4.4 7.0 %collective-permute-start.6 = (f32[64,128]{1,0:T(8,128)S(1)}, f32[64,128]{1,0:T(8,128)S(1)}, u32[]{:S(2)}, u32[]{:S(2)}) collective-permute-start(f32[64,128]{1,0:T(8,128)S(1)} %get-tuple-element.35.u), channel_id=1, source_target_pairs={{0,7},{1,2},{2,1},{3,4},{4,3},{5,6},{6,5},{7,0},{8,15},{9,10},{10,... | collective-permute-start | bytes 98312 | tf_op jit(solution)/shard_map/ppermute | solution.py:295
  8.0 6.0 %collective-permute-start = (f32[64,384]{1,0:T(8,128)S(1)}, f32[64,384]{1,0:T(8,128)S(1)}, u32[]{:S(2)}, u32[]{:S(2)}) collective-permute-start(f32[64,384]{1,0:T(8,128)S(1)} %shard_map.74.static.refs_0_), channel_id=1, source_target_pairs={{0,4},{1,5},{2,6},{3,7},{4,0},{5,1},{6,2},{7,3},{8,12},{9,13},{10,... | collective-permute-start | bytes 294920 | tf_op jit(solution)/shard_map/ppermute | solution.py:289
  8.1 6.5 %collective-permute-start.1 = (f32[64,384]{1,0:T(8,128)S(1)}, f32[64,384]{1,0:T(8,128)S(1)}, u32[]{:S(2)}, u32[]{:S(2)}) collective-permute-start(f32[64,384]{1,0:T(8,128)S(1)} %shard_map.75), channel_id=1, source_target_pairs={{0,2},{1,3},{2,0},{3,1},{4,6},{5,7},{6,4},{7,5},{8,10},{9,11},{10,... | collective-permute-start | bytes 294920 | tf_op jit(solution)/shard_map/ppermute | solution.py:289
  9.1 5.4 %collective-permute-start.2 = (f32[64,384]{1,0:T(8,128)S(1)}, f32[64,384]{1,0:T(8,128)S(1)}, u32[]{:S(2)}, u32[]{:S(2)}) collective-permute-start(f32[64,384]{1,0:T(8,128)S(1)} %shard_map.75), channel_id=1, source_target_pairs={{0,1},{1,0},{2,3},{3,2},{4,5},{5,4},{6,7},{7,6},{8,9},{9,8},{10,11... | collective-permute-start | bytes 294920 | tf_op jit(solution)/shard_map/ppermute | solution.py:289
  11.5 5.5 %collective-permute-start.7 = (f32[3,64,128]{2,1,0:T(8,128)S(1)}, f32[3,64,128]{2,1,0:T(8,128)S(1)}, u32[]{:S(2)}, u32[]{:S(2)}) collective-permute-start(f32[3,64,128]{2,1,0:T(8,128)S(1)} %shard_map.78.middle), channel_id=1, source_target_pairs={{0,8},{8,0},{16,24},{24,16},{1,9},{9,1},{17,25},{25,17},{2,10},{10... | collective-permute-start | bytes 294920 | tf_op jit(solution)/shard_map/ppermute | solution.py:294
  11.5 5.4 %collective-permute-start.8 = (f32[3,64,128]{2,1,0:T(8,128)S(1)}, f32[3,64,128]{2,1,0:T(8,128)S(1)}, u32[]{:S(2)}, u32[]{:S(2)}) collective-permute-start(f32[3,64,128]{2,1,0:T(8,128)S(1)} %shard_map.78.middle), channel_id=1, source_target_pairs={{0,24},{8,16},{16,8},{24,0},{1,25},{9,17},{17,9},{25,1},{2,26},{10... | collective-permute-start | bytes 294920 | tf_op jit(solution)/shard_map/ppermute | solution.py:295
  14.6 8.9 %collective-permute-start.3 = (f32[2,64,384]{2,1,0:T(8,128)S(1)}, f32[2,64,384]{2,1,0:T(8,128)S(1)}, u32[]{:S(2)}, u32[]{:S(2)}) collective-permute-start(f32[2,64,384]{2,1,0:T(8,128)S(1)} %get-tuple-element.34), channel_id=1, source_target_pairs={{0,1},{1,0},{2,3},{3,2},{4,5},{5,4},{6,7},{7,6},{8,9},{9,8},{10,11... | collective-permute-start | bytes 589832 | tf_op jit(solution)/shard_map/ppermute | solution.py:289
  15.3 9.1 %collective-permute-start.4 = (f32[64,384]{1,0:T(8,128)S(1)}, f32[64,384]{1,0:T(8,128)S(1)}, u32[]{:S(2)}, u32[]{:S(2)}) collective-permute-start(f32[64,384]{1,0:T(8,128)S(1)} %get-tuple-element.33.refs_1_), channel_id=1, source_target_pairs={{0,2},{1,3},{2,0},{3,1},{4,6},{5,7},{6,4},{7,5},{8,10},{9,11},{10,... | collective-permute-start | bytes 294920 | tf_op jit(solution)/shard_map/ppermute | solution.py:289
  17.5 6.0 %collective-permute-start.9 = (f32[2,40,128]{2,1,0:T(8,128)S(1)}, f32[2,40,128]{2,1,0:T(8,128)S(1)}, u32[]{:S(2)}, u32[]{:S(2)}) collective-permute-start(f32[2,40,128]{2,1,0:T(8,128)S(1)} %get-tuple-element.38), channel_id=1, source_target_pairs={{0,6},{1,7},{2,4},{3,5},{4,2},{5,3},{6,0},{7,1},{8,14},{9,15},{10,... | collective-permute-start | bytes 122888 | tf_op jit(solution)/shard_map/ppermute | solution.py:289
  19.1 5.0 %collective-permute-start.11 = (f32[2,40,128]{2,1,0:T(8,128)S(1)}, f32[2,40,128]{2,1,0:T(8,128)S(1)}, u32[]{:S(2)}, u32[]{:S(2)}) collective-permute-start(f32[2,40,128]{2,1,0:T(8,128)S(1)} %get-tuple-element.42), channel_id=1, source_target_pairs={{0,4},{1,5},{2,6},{3,7},{4,0},{5,1},{6,2},{7,3},{8,12},{9,13},{10,... | collective-permute-start | bytes 122888 | tf_op jit(solution)/shard_map/ppermute | solution.py:289
  19.5 4.9 %collective-permute-start.12 = (f32[2,40,128]{2,1,0:T(8,128)S(1)}, f32[2,40,128]{2,1,0:T(8,128)S(1)}, u32[]{:S(2)}, u32[]{:S(2)}) collective-permute-start(f32[2,40,128]{2,1,0:T(8,128)S(1)} %get-tuple-element.43), channel_id=1, source_target_pairs={{0,2},{1,3},{2,0},{3,1},{4,6},{5,7},{6,4},{7,5},{8,10},{9,11},{10,... | collective-permute-start | bytes 122888 | tf_op jit(solution)/shard_map/ppermute | solution.py:289
  23.5 4.7 %collective-permute-start.10 = (f32[64,384]{1,0:T(8,128)S(1)}, f32[64,384]{1,0:T(8,128)S(1)}, u32[]{:S(2)}, u32[]{:S(2)}) collective-permute-start(f32[64,384]{1,0:T(8,128)S(1)} %shard_map.80), channel_id=1, source_target_pairs={{0,2},{1,3},{2,0},{3,1},{4,6},{5,7},{6,4},{7,5},{8,10},{9,11},{10,... | collective-permute-start | bytes 294920 | tf_op jit(solution)/shard_map/ppermute | solution.py:289
  24.4 4.5 %collective-permute-start.13 = (f32[4,40,128]{2,1,0:T(8,128)S(1)}, f32[4,40,128]{2,1,0:T(8,128)S(1)}, u32[]{:S(2)}, u32[]{:S(2)}) collective-permute-start(f32[4,40,128]{2,1,0:T(8,128)S(1)} %shard_map.82), channel_id=1, source_target_pairs={{0,1},{1,0},{2,3},{3,2},{4,5},{5,4},{6,7},{7,6},{8,9},{9,8},{10,11... | collective-permute-start | bytes 245768 | tf_op jit(solution)/shard_map/ppermute | solution.py:289

commit v13 on v8

--- a/solution.py
+++ b/solution.py
@@ -236,17 +236,21 @@
 
 
 def top_kernel(offsets, top_high, top_low, local, *refs):
-    pieces = refs[:-3][::-1]
-    came, out, packed = refs[-3:]
+    pieces = refs[:-4][::-1]
+    first_half, second_half, out, packed = refs[-4:]
     boxes = 2 * len(pieces)
-    width = came.shape[2]
+    width = first_half.shape[2]
+    ways = [0, *reversed(range(1, boxes // 2))]
+    came = {k: (first_half, i) for i, k in enumerate(ways[:1])}
+    came.update({k: (second_half, i) for i, k in enumerate(ways[1:])})
     share = out.shape[1]
     half = share // 2
     rank = local.shape[1] // 6
     rows = 2 * rank
     me = lax.axis_index("box")
-    for k in range(boxes):
-        packed[me ^ k] = came[k // 2, 2 * share : 2 * share + half] if k % 2 else pieces[k // 2][0, 2 * share : 2 * share + half]
+    blocks = [came[k // 2] if k % 2 else (pieces[k // 2], 0) for k in range(boxes)]
+    for k, (piece, side) in enumerate(blocks):
+        packed[me ^ k] = piece[side, 2 * share : 2 * share + half]
     t_re = []
     t_im = []
     for box in range(boxes):
@@ -260,7 +264,7 @@
         at = slice(k * rows, (k + 1) * rows)
         x = dot(cat([y[0][:, at], y[1][:, at], y[0][:, at]], 1), local[k])
         offset = offsets[k]
-        piece, side = (came, offset // 2) if offset % 2 else (pieces[offset // 2], 0)
+        piece, side = blocks[offset]
         at = pl.ds(pl.multiple_of((me ^ offset) * width, width), width)
         out[0, :, at] = piece[side, :share] + x[:, :width]
         out[1, :, at] = piece[side, share : 2 * share] + x[:, width:]
@@ -357,11 +361,15 @@
         cost=COST, extra=[pltpu.VMEM((boxes, length, width), F32)],
     )
     pieces = [swapped(pieces[k], "box", 2 * k) for k in reversed(range(1, boxes // 2))] + [pieces[0]]
-    (send,) = call(
-        functools.partial(forward_kernel, boxes // 2), [((boxes // 2, length, width), F32)],
-        *pieces[::-1], *waited, hbm=range(boxes // 2, boxes // 2 + len(waited)),
-    )
-    came = swapped(send, "box", 1)
+    ways = [0, *reversed(range(1, boxes // 2))]
+    came = []
+    for half in (ways[:1], ways[1:]):
+        held = [*waited, *came] if came else []
+        (send,) = call(
+            functools.partial(forward_kernel, len(half)), [((len(half), length, width), F32)],
+            *[pieces[-1 - k] for k in half], *held, hbm=range(len(half), len(half) + len(held)),
+        )
+        came.append(swapped(send, "box", 1))
     if boxes == 8:
         (five,) = call(copy_kernel, [(six.shape, F32)], others, pieces[0], hbm=(1,))
         late.append(swapped(five, "box", 2))
@@ -369,7 +377,7 @@
     local = ((boxes, 6 * rank, 2 * width), BF16)
     prepared = call(prepare_kernel, [top, top, local], *early, *late)
     (out,) = call(
-        functools.partial(top_kernel, offsets), [((2, share, boxes * width), F32)], *prepared, *pieces, came,
+        functools.partial(top_kernel, offsets), [((2, share, boxes * width), F32)], *prepared, *pieces, *came,
         extra=[pltpu.VMEM((boxes, share // 2, width), F32)],
     )
     return out

time: 30.3 us -> 32.9 us (1.086)
  waiting for transfers between devices: 7.47 us -> 10.9 us
  starting transfers between devices: 18.2 us -> 17.4 us
    ppermute x10 -> x11, waiting for transfers between devices: 5.64 us -> 9.06 us  [swapped(): lax.ppermute(value, axis, [(i, i ^ bit) for i in range(lax.axis_size(axis...]
    ppermute x10 -> x11, starting transfers between devices: 9.98 us -> 9.14 us  [swapped(): lax.ppermute(value, axis, [(i, i ^ bit) for i in range(lax.axis_size(axis...]
    pallas_call x11 -> x12, Pallas kernels: 4.37 us -> 4.38 us  [call(): pl.pallas_call(kernel, out_shape=[jax.ShapeDtypeStruct(shape, dtype) for...]
  transfers between devices with their start and end apart: 14 -> 15, of which waited for: 9 -> 7; matrix products, arithmetic and copies ran while one was open for 0% -> 0% of each run, Pallas kernels for 5% -> 5%
where the time goes in v13:
time: 32.9 us; the launch traced here: 32.8 us
  starting transfers between devices  17.4 us (53%)
  waiting for transfers between devices  10.9 us (33%)
  Pallas kernels  4.38 us (13%)
    ppermute x11, starting transfers between devices, swapped(): lax.ppermute(value, axis, [(i, i ^ bit) for i in range(lax.axis_size(axis...  9.14 us
    ppermute x11, waiting for transfers between devices, swapped(): lax.ppermute(value, axis, [(i, i ^ bit) for i in range(lax.axis_size(axis...  9.06 us
    ppermute x2, starting transfers between devices, beside(): lax.ppermute(value, axis, [(i, (i + 1) % count if i % 2 else (i - 1) % co...  5.15 us
    pallas_call x12, Pallas kernels, call(): pl.pallas_call(kernel, out_shape=[jax.ShapeDtypeStruct(shape, dtype) for...  4.38 us
    ppermute x2, starting transfers between devices, beside(): even = lax.ppermute(value, axis, [(i, i ^ 1) for i in range(count)])  3.1 us
    ppermute x2, waiting for transfers between devices, beside(): lax.ppermute(value, axis, [(i, (i + 1) % count if i % 2 else (i - 1) % co...  1.82 us
  transfers between devices with their start and end apart: 15, of which 7 were waited for; matrix products, arithmetic and copies ran while one was open for 0% of the time, Pallas kernels for 5%

profile of v13, /device:TPU:0, one launch (start us, length us, event | category | flops | bytes accessed | tf_op | source)
XLA Modules:
  0.0 32.8 jit_solution(14197147933858918546)
XLA Ops:
  0.0 1.4 %shard_map.73 = (f32[64,128]{1,0:T(8,128)S(1)}, f32[64,384]{1,0:T(8,128)S(1)}, bf16[128,256]{1,0:T(8,128)(2,1)S(1)}, bf16[128,256]{1,0:T(8,128)(2,1)S(1)}, bf16[...) custom-call(f32[3,128]{1,0:T(4,128)} %points_in.1, ...), custom_call_target="tpu_custom_call" | custom-call | tf_op jit(solution)/shard_map/pallas_call | solution.py:281
  1.4 3.0 %collective-permute-start.5 = (f32[64,128]{1,0:T(8,128)S(1)}, f32[64,128]{1,0:T(8,128)S(1)}, u32[]{:S(2)}, u32[]{:S(2)}) collective-permute-start(f32[64,128]{1,0:T(8,128)S(1)} %get-tuple-element.35.u), channel_id=1, source_target_pairs={{0,1},{1,0},{2,3},{3,2},{4,5},{5,4},{6,7},{7,6},{8,9},{9,8},{10,11... | collective-permute-start | bytes 98312 | tf_op jit(solution)/shard_map/ppermute | solution.py:298
  4.4 3.5 %collective-permute-start.6 = (f32[64,128]{1,0:T(8,128)S(1)}, f32[64,128]{1,0:T(8,128)S(1)}, u32[]{:S(2)}, u32[]{:S(2)}) collective-permute-start(f32[64,128]{1,0:T(8,128)S(1)} %get-tuple-element.35.u), channel_id=1, source_target_pairs={{0,7},{1,2},{2,1},{3,4},{4,3},{5,6},{6,5},{7,0},{8,15},{9,10},{10,... | collective-permute-start | bytes 98312 | tf_op jit(solution)/shard_map/ppermute | solution.py:299
  8.1 1.1 %collective-permute-start.1 = (f32[64,384]{1,0:T(8,128)S(1)}, f32[64,384]{1,0:T(8,128)S(1)}, u32[]{:S(2)}, u32[]{:S(2)}) collective-permute-start(f32[64,384]{1,0:T(8,128)S(1)} %shard_map.75), channel_id=1, source_target_pairs={{0,2},{1,3},{2,0},{3,1},{4,6},{5,7},{6,4},{7,5},{8,10},{9,11},{10,... | collective-permute-start | bytes 294920 | tf_op jit(solution)/shard_map/ppermute | solution.py:293
  9.1 1.3 %collective-permute-start.2 = (f32[64,384]{1,0:T(8,128)S(1)}, f32[64,384]{1,0:T(8,128)S(1)}, u32[]{:S(2)}, u32[]{:S(2)}) collective-permute-start(f32[64,384]{1,0:T(8,128)S(1)} %shard_map.75), channel_id=1, source_target_pairs={{0,1},{1,0},{2,3},{3,2},{4,5},{5,4},{6,7},{7,6},{8,9},{9,8},{10,11... | collective-permute-start | bytes 294920 | tf_op jit(solution)/shard_map/ppermute | solution.py:293
  10.4 1.0 %collective-permute-done.6.odd = f32[64,128]{1,0:T(8,128)S(1)} collective-permute-done((f32[64,128]{1,0:T(8,128)S(1)}, f32[64,128]{1,0:T(8,128)S(1)}, u32[]{:S(2)}, u32[]{:S(2)}) %collective-permute-start.6) | collective-permute-done | bytes 32800 | tf_op jit(solution)/shard_map/ppermute | solution.py:299
  11.5 0.1 collective-permute-start.7
  11.5 1.6 %collective-permute-start.8 = (f32[3,64,128]{2,1,0:T(8,128)S(1)}, f32[3,64,128]{2,1,0:T(8,128)S(1)}, u32[]{:S(2)}, u32[]{:S(2)}) collective-permute-start(f32[3,64,128]{2,1,0:T(8,128)S(1)} %shard_map.78.middle), channel_id=1, source_target_pairs={{0,24},{8,16},{16,8},{24,0},{1,25},{9,17},{17,9},{25,1},{2,26},{10... | collective-permute-start | bytes 294920 | tf_op jit(solution)/shard_map/ppermute | solution.py:299
  13.1 0.8 %shard_map.76 = (f32[128,320]{1,0:T(8,128)S(1)}, bf16[512,320]{1,0:T(8,128)(2,1)S(1)}, bf16[512,320]{1,0:T(8,128)(2,1)S(1)}) custom-call(bf16[128,256]{1,0:T(8,128)(2,1)S(1)} %get-tuple-element.26.high, bf16[128,256]{1,0:T(8,128)(2,1)S(1)} %get-tuple-element.27.low, bf16[128,32]{1,0:T(8,128)(2,1)S(1)} %get-tuple-element.28.picker_in, ...), custom_call_target="tpu_custom_call" | custom-call | flops 10000000000 | bytes 10000000 | tf_op jit(solution)/shard_map/pallas_call | solution.py:281
  14.0 0.5 %collective-permute-done.1.two.refs_2_ = f32[64,384]{1,0:T(8,128)S(1)} collective-permute-done((f32[64,384]{1,0:T(8,128)S(1)}, f32[64,384]{1,0:T(8,128)S(1)}, u32[]{:S(2)}, u32[]{:S(2)}) %collective-permute-start.1) | collective-permute-done | bytes 98336 | tf_op jit(solution)/shard_map/ppermute | solution.py:293
  14.6 0.7 %collective-permute-start.3 = (f32[2,64,384]{2,1,0:T(8,128)S(1)}, f32[2,64,384]{2,1,0:T(8,128)S(1)}, u32[]{:S(2)}, u32[]{:S(2)}) collective-permute-start(f32[2,64,384]{2,1,0:T(8,128)S(1)} %get-tuple-element.34), channel_id=1, source_target_pairs={{0,1},{1,0},{2,3},{3,2},{4,5},{5,4},{6,7},{7,6},{8,9},{9,8},{10,11... | collective-permute-start | bytes 589832 | tf_op jit(solution)/shard_map/ppermute | solution.py:293
  15.3 0.8 %collective-permute-done.8.odd = f32[3,64,128]{2,1,0:T(8,128)S(1)} collective-permute-done((f32[3,64,128]{2,1,0:T(8,128)S(1)}, f32[3,64,128]{2,1,0:T(8,128)S(1)}, u32[]{:S(2)}, u32[]{:S(2)}) %collective-permute-start.8) | collective-permute-done | bytes 98336 | tf_op jit(solution)/shard_map/ppermute | solution.py:299
  16.1 0.5 %shard_map.79 = (f32[2,40,128]{2,1,0:T(8,128)S(1)}, f32[2,40,128]{2,1,0:T(8,128)S(1)}, f32[2,40,128]{2,1,0:T(8,128)S(1)}, f32[2,40,128]{2,1,0:T(8,128)S(1)}) custom-call(f32[3,64,128]{2,1,0:T(8,128)S(1)} %collective-permute-done.7.even, f32[3,64,128]{2,1,0:T(8,128)S(1)} %shard_map.78.middle, f32[3,64,128]{2,1,0:T(8,128)S(1)} %collective-permute-done.8.odd, ...), custom_call_target="tpu_custom_call" | custom-call | flops 10000000000 | bytes 10000000 | tf_op jit(solution)/shard_map/pallas_call | solution.py:281
  16.7 2.4 %collective-permute-start.9 = (f32[2,40,128]{2,1,0:T(8,128)S(1)}, f32[2,40,128]{2,1,0:T(8,128)S(1)}, u32[]{:S(2)}, u32[]{:S(2)}) collective-permute-start(f32[2,40,128]{2,1,0:T(8,128)S(1)} %get-tuple-element.38), channel_id=1, source_target_pairs={{0,6},{1,7},{2,4},{3,5},{4,2},{5,3},{6,0},{7,1},{8,14},{9,15},{10,... | collective-permute-start | bytes 122888 | tf_op jit(solution)/shard_map/ppermute | solution.py:293
  19.1 2.1 %collective-permute-start.12 = (f32[2,40,128]{2,1,0:T(8,128)S(1)}, f32[2,40,128]{2,1,0:T(8,128)S(1)}, u32[]{:S(2)}, u32[]{:S(2)}) collective-permute-start(f32[2,40,128]{2,1,0:T(8,128)S(1)} %get-tuple-element.43), channel_id=1, source_target_pairs={{0,2},{1,3},{2,0},{3,1},{4,6},{5,7},{6,4},{7,5},{8,10},{9,11},{10,... | collective-permute-start | bytes 122888 | tf_op jit(solution)/shard_map/ppermute | solution.py:293
  21.2 1.7 %collective-permute-done.9.refs_0_ = f32[2,40,128]{2,1,0:T(8,128)S(1)} collective-permute-done((f32[2,40,128]{2,1,0:T(8,128)S(1)}, f32[2,40,128]{2,1,0:T(8,128)S(1)}, u32[]{:S(2)}, u32[]{:S(2)}) %collective-permute-start.9) | collective-permute-done | bytes 40992 | tf_op jit(solution)/shard_map/ppermute | solution.py:293
  22.9 0.4 %collective-permute-start.10 = (f32[64,384]{1,0:T(8,128)S(1)}, f32[64,384]{1,0:T(8,128)S(1)}, u32[]{:S(2)}, u32[]{:S(2)}) collective-permute-start(f32[64,384]{1,0:T(8,128)S(1)} %shard_map.80), channel_id=1, source_target_pairs={{0,2},{1,3},{2,0},{3,1},{4,6},{5,7},{6,4},{7,5},{8,10},{9,11},{10,... | collective-permute-start | bytes 294920 | tf_op jit(solution)/shard_map/ppermute | solution.py:293
  23.3 0.5 %collective-permute-start.13 = (f32[1,40,128]{2,1,0:T(8,128)S(1)}, f32[1,40,128]{2,1,0:T(8,128)S(1)}, u32[]{:S(2)}, u32[]{:S(2)}) collective-permute-start(f32[1,40,128]{2,1,0:T(8,128)S(1)} %shard_map.82), channel_id=1, source_target_pairs={{0,1},{1,0},{2,3},{3,2},{4,5},{5,4},{6,7},{7,6},{8,9},{9,8},{10,11... | collective-permute-start | bytes 61448 | tf_op jit(solution)/shard_map/ppermute | solution.py:293
  23.8 3.3 %collective-permute-done.13.refs_4_ = f32[1,40,128]{2,1,0:T(8,128)S(1)} collective-permute-done((f32[1,40,128]{2,1,0:T(8,128)S(1)}, f32[1,40,128]{2,1,0:T(8,128)S(1)}, u32[]{:S(2)}, u32[]{:S(2)}) %collective-permute-start.13) | collective-permute-done | bytes 20512 | tf_op jit(solution)/shard_map/ppermute | solution.py:293
  27.1 0.6 %collective-permute-start.14 = (f32[3,40,128]{2,1,0:T(8,128)S(1)}, f32[3,40,128]{2,1,0:T(8,128)S(1)}, u32[]{:S(2)}, u32[]{:S(2)}) collective-permute-start(f32[3,40,128]{2,1,0:T(8,128)S(1)} %shard_map.83), channel_id=1, source_target_pairs={{0,1},{1,0},{2,3},{3,2},{4,5},{5,4},{6,7},{7,6},{8,9},{9,8},{10,11... | collective-permute-start | bytes 184328 | tf_op jit(solution)/shard_map/ppermute | solution.py:293
  27.6 0.7 %collective-permute-done.10.refs_6_ = f32[64,384]{1,0:T(8,128)S(1)} collective-permute-done((f32[64,384]{1,0:T(8,128)S(1)}, f32[64,384]{1,0:T(8,128)S(1)}, u32[]{:S(2)}, u32[]{:S(2)}) %collective-permute-start.10) | collective-permute-done | bytes 98336 | tf_op jit(solution)/shard_map/ppermute | solution.py:293
  28.3 0.1 shard_map.81
  28.5 2.8 %collective-permute-done.14.refs_5_ = f32[3,40,128]{2,1,0:T(8,128)S(1)} collective-permute-done((f32[3,40,128]{2,1,0:T(8,128)S(1)}, f32[3,40,128]{2,1,0:T(8,128)S(1)}, u32[]{:S(2)}, u32[]{:S(2)}) %collective-permute-start.14) | collective-permute-done | bytes 61472 | tf_op jit(solution)/shard_map/ppermute | solution.py:293
  31.3 1.4 %shard_map.84 = f32[2,16,1024]{2,1,0:T(8,128)} custom-call(bf16[512,512]{1,0:T(8,128)(2,1)S(1)} %get-tuple-element.39.top_high, bf16[512,512]{1,0:T(8,128)(2,1)S(1)} %get-tuple-element.40.top_low, bf16[8,192,256]{2,1,0:T(8,128)(2,1)S(1)} %get-tuple-element.41.local, f32[2,40,128]{2,1,0:T(8,128)S(1)} %collective-permute-done.9.refs_0_, ...), custom_call_target="tpu_custom_call" | custom-call | tf_op jit(solution)/shard_map/pallas_call | solution.py:281
  (18 shorter events, 0.2 us)
Async XLA Ops:
  1.4 9.0 %collective-permute-start.5 = (f32[64,128]{1,0:T(8,128)S(1)}, f32[64,128]{1,0:T(8,128)S(1)}, u32[]{:S(2)}, u32[]{:S(2)}) collective-permute-start(f32[64,128]{1,0:T(8,128)S(1)} %get-tuple-element.35.u), channel_id=1, source_target_pairs={{0,1},{1,0},{2,3},{3,2},{4,5},{5,4},{6,7},{7,6},{8,9},{9,8},{10,11... | collective-permute-start | bytes 98312 | tf_op jit(solution)/shard_map/ppermute | solution.py:298
  4.4 7.0 %collective-permute-start.6 = (f32[64,128]{1,0:T(8,128)S(1)}, f32[64,128]{1,0:T(8,128)S(1)}, u32[]{:S(2)}, u32[]{:S(2)}) collective-permute-start(f32[64,128]{1,0:T(8,128)S(1)} %get-tuple-element.35.u), channel_id=1, source_target_pairs={{0,7},{1,2},{2,1},{3,4},{4,3},{5,6},{6,5},{7,0},{8,15},{9,10},{10,... | collective-permute-start | bytes 98312 | tf_op jit(solution)/shard_map/ppermute | solution.py:299
  8.0 6.0 %collective-permute-start = (f32[64,384]{1,0:T(8,128)S(1)}, f32[64,384]{1,0:T(8,128)S(1)}, u32[]{:S(2)}, u32[]{:S(2)}) collective-permute-start(f32[64,384]{1,0:T(8,128)S(1)} %shard_map.74.static.refs_0_), channel_id=1, source_target_pairs={{0,4},{1,5},{2,6},{3,7},{4,0},{5,1},{6,2},{7,3},{8,12},{9,13},{10,... | collective-permute-start | bytes 294920 | tf_op jit(solution)/shard_map/ppermute | solution.py:293
  8.1 6.5 %collective-permute-start.1 = (f32[64,384]{1,0:T(8,128)S(1)}, f32[64,384]{1,0:T(8,128)S(1)}, u32[]{:S(2)}, u32[]{:S(2)}) collective-permute-start(f32[64,384]{1,0:T(8,128)S(1)} %shard_map.75), channel_id=1, source_target_pairs={{0,2},{1,3},{2,0},{3,1},{4,6},{5,7},{6,4},{7,5},{8,10},{9,11},{10,... | collective-permute-start | bytes 294920 | tf_op jit(solution)/shard_map/ppermute | solution.py:293
  9.1 5.4 %collective-permute-start.2 = (f32[64,384]{1,0:T(8,128)S(1)}, f32[64,384]{1,0:T(8,128)S(1)}, u32[]{:S(2)}, u32[]{:S(2)}) collective-permute-start(f32[64,384]{1,0:T(8,128)S(1)} %shard_map.75), channel_id=1, source_target_pairs={{0,1},{1,0},{2,3},{3,2},{4,5},{5,4},{6,7},{7,6},{8,9},{9,8},{10,11... | collective-permute-start | bytes 294920 | tf_op jit(solution)/shard_map/ppermute | solution.py:293
  11.5 3.9 %collective-permute-start.7 = (f32[3,64,128]{2,1,0:T(8,128)S(1)}, f32[3,64,128]{2,1,0:T(8,128)S(1)}, u32[]{:S(2)}, u32[]{:S(2)}) collective-permute-start(f32[3,64,128]{2,1,0:T(8,128)S(1)} %shard_map.78.middle), channel_id=1, source_target_pairs={{0,8},{8,0},{16,24},{24,16},{1,9},{9,1},{17,25},{25,17},{2,10},{10... | collective-permute-start | bytes 294920 | tf_op jit(solution)/shard_map/ppermute | solution.py:298
  11.5 4.6 %collective-permute-start.8 = (f32[3,64,128]{2,1,0:T(8,128)S(1)}, f32[3,64,128]{2,1,0:T(8,128)S(1)}, u32[]{:S(2)}, u32[]{:S(2)}) collective-permute-start(f32[3,64,128]{2,1,0:T(8,128)S(1)} %shard_map.78.middle), channel_id=1, source_target_pairs={{0,24},{8,16},{16,8},{24,0},{1,25},{9,17},{17,9},{25,1},{2,26},{10... | collective-permute-start | bytes 294920 | tf_op jit(solution)/shard_map/ppermute | solution.py:299
  14.6 8.3 %collective-permute-start.3 = (f32[2,64,384]{2,1,0:T(8,128)S(1)}, f32[2,64,384]{2,1,0:T(8,128)S(1)}, u32[]{:S(2)}, u32[]{:S(2)}) collective-permute-start(f32[2,64,384]{2,1,0:T(8,128)S(1)} %get-tuple-element.34), channel_id=1, source_target_pairs={{0,1},{1,0},{2,3},{3,2},{4,5},{5,4},{6,7},{7,6},{8,9},{9,8},{10,11... | collective-permute-start | bytes 589832 | tf_op jit(solution)/shard_map/ppermute | solution.py:293
  16.7 6.2 %collective-permute-start.9 = (f32[2,40,128]{2,1,0:T(8,128)S(1)}, f32[2,40,128]{2,1,0:T(8,128)S(1)}, u32[]{:S(2)}, u32[]{:S(2)}) collective-permute-start(f32[2,40,128]{2,1,0:T(8,128)S(1)} %get-tuple-element.38), channel_id=1, source_target_pairs={{0,6},{1,7},{2,4},{3,5},{4,2},{5,3},{6,0},{7,1},{8,14},{9,15},{10,... | collective-permute-start | bytes 122888 | tf_op jit(solution)/shard_map/ppermute | solution.py:293
  19.1 8.0 %collective-permute-start.11 = (f32[2,40,128]{2,1,0:T(8,128)S(1)}, f32[2,40,128]{2,1,0:T(8,128)S(1)}, u32[]{:S(2)}, u32[]{:S(2)}) collective-permute-start(f32[2,40,128]{2,1,0:T(8,128)S(1)} %get-tuple-element.42), channel_id=1, source_target_pairs={{0,4},{1,5},{2,6},{3,7},{4,0},{5,1},{6,2},{7,3},{8,12},{9,13},{10,... | collective-permute-start | bytes 122888 | tf_op jit(solution)/shard_map/ppermute | solution.py:293
  19.1 8.0 %collective-permute-start.12 = (f32[2,40,128]{2,1,0:T(8,128)S(1)}, f32[2,40,128]{2,1,0:T(8,128)S(1)}, u32[]{:S(2)}, u32[]{:S(2)}) collective-permute-start(f32[2,40,128]{2,1,0:T(8,128)S(1)} %get-tuple-element.43), channel_id=1, source_target_pairs={{0,2},{1,3},{2,0},{3,1},{4,6},{5,7},{6,4},{7,5},{8,10},{9,11},{10,... | collective-permute-start | bytes 122888 | tf_op jit(solution)/shard_map/ppermute | solution.py:293
  21.1 6.5 %collective-permute-start.4 = (f32[64,384]{1,0:T(8,128)S(1)}, f32[64,384]{1,0:T(8,128)S(1)}, u32[]{:S(2)}, u32[]{:S(2)}) collective-permute-start(f32[64,384]{1,0:T(8,128)S(1)} %get-tuple-element.33.refs_1_), channel_id=1, source_target_pairs={{0,2},{1,3},{2,0},{3,1},{4,6},{5,7},{6,4},{7,5},{8,10},{9,11},{10,... | collective-permute-start | bytes 294920 | tf_op jit(solution)/shard_map/ppermute | solution.py:293
  22.9 5.5 %collective-permute-start.10 = (f32[64,384]{1,0:T(8,128)S(1)}, f32[64,384]{1,0:T(8,128)S(1)}, u32[]{:S(2)}, u32[]{:S(2)}) collective-permute-start(f32[64,384]{1,0:T(8,128)S(1)} %shard_map.80), channel_id=1, source_target_pairs={{0,2},{1,3},{2,0},{3,1},{4,6},{5,7},{6,4},{7,5},{8,10},{9,11},{10,... | collective-permute-start | bytes 294920 | tf_op jit(solution)/shard_map/ppermute | solution.py:293
  23.3 3.8 %collective-permute-start.13 = (f32[1,40,128]{2,1,0:T(8,128)S(1)}, f32[1,40,128]{2,1,0:T(8,128)S(1)}, u32[]{:S(2)}, u32[]{:S(2)}) collective-permute-start(f32[1,40,128]{2,1,0:T(8,128)S(1)} %shard_map.82), channel_id=1, source_target_pairs={{0,1},{1,0},{2,3},{3,2},{4,5},{5,4},{6,7},{7,6},{8,9},{9,8},{10,11... | collective-permute-start | bytes 61448 | tf_op jit(solution)/shard_map/ppermute | solution.py:293
  27.1 4.3 %collective-permute-start.14 = (f32[3,40,128]{2,1,0:T(8,128)S(1)}, f32[3,40,128]{2,1,0:T(8,128)S(1)}, u32[]{:S(2)}, u32[]{:S(2)}) collective-permute-start(f32[3,40,128]{2,1,0:T(8,128)S(1)} %shard_map.83), channel_id=1, source_target_pairs={{0,1},{1,0},{2,3},{3,2},{4,5},{5,4},{6,7},{7,6},{8,9},{9,8},{10,11... | collective-permute-start | bytes 184328 | tf_op jit(solution)/shard_map/ppermute | solution.py:293
